TPU v7x, 256 devices: a whole 4x4x8 slice. The times are simulated.
256 devices in a mesh: dp: 8 (over y, core), mem: 32 (over z, x).
Axes of the slice: x: 4, y: 4, z: 8, core: 2. Of those that a mesh axis runs over, the one named last changes fastest.
Arguments:
- slot_weight: bfloat16 [32768, 32], P(('dp', 'mem')), may hold values from -1.1953125 to 1.1953125
- slot_pos: int32 [32768, 32], P(('dp', 'mem')), may hold values from 0 to 1023, as said below
- touched: int32 [256, 32, 32], P(('dp', 'mem')), may hold values from 0 to 255, as said below
- values: bfloat16 [8192, 4096], P('mem'), may hold values from -6 to 6
- cotangent: bfloat16 [32768, 4096], P(('dp', 'mem')), may hold values from -6 to 6
Outputs:
- memory_out: bfloat16 [32768, 4096], P(('dp', 'mem'))
- weight_grad: float32 [32768, 32], P(('dp', 'mem'))
- value_grad: float32 [8192, 4096], P('mem', 'dp')
Inputs may be any that keep to these rules, and one draw needn't show every extreme that they name: `slot_pos`: each token's 32 positions are distinct. For each device and owner o, the positions used are o * 32 + j with j below a count c of 1 to 32; in each group of devices along mem, one owner has c = 32 from every device. `touched`: for each device and owner, the entries at the used positions are distinct; entries at unused positions are arbitrary rows.
All inputs are finite; a program needn't handle non-finite values.
Results may differ from a plain program's by a relative error of at most 0.001.
Values may be sent and summed in bfloat16 or wider, within the bound.
No kernel may reach another device: no remote copies, remote signals or barrier semaphores. Data moves between devices by JAX's collectives and lax.ppermute only.
A program may use at most 256 MiB of HBM per device.

v0:
```python
import jax
import jax.numpy as jnp
from jax import lax
from jax.sharding import PartitionSpec as P


def on_device(slot_weight, slot_pos, touched, values, cotangent):
    tok_rows = slot_pos.shape[0]
    lists = touched[0]
    groups = lists.shape[0]
    cap_rows = lists.shape[1]
    spread = groups * cap_rows
    feature = cotangent.shape[1]
    owned = values.shape[0]
    dense_w = jnp.zeros((tok_rows, spread), jnp.bfloat16)
    dense_w = dense_w.at[jnp.arange(tok_rows)[:, None], slot_pos].set(slot_weight)
    partial_grad = lax.dot_general(
        dense_w, cotangent, (((0,), (0,)), ((), ())), preferred_element_type=jnp.float32
    )
    partial_grad = partial_grad.reshape(groups, cap_rows, feature)
    got_lists = lax.all_to_all(lists, "mem", split_axis=0, concat_axis=0, tiled=True)
    fetched = values[got_lists.reshape(-1)].reshape(groups, cap_rows, feature)
    arrived = lax.all_to_all(fetched, "mem", split_axis=0, concat_axis=0, tiled=True).reshape(
        spread, feature
    )
    memory_out = jnp.dot(dense_w, arrived, preferred_element_type=jnp.float32).astype(jnp.bfloat16)
    scores = lax.dot_general(
        cotangent, arrived, (((1,), (1,)), ((), ())), preferred_element_type=jnp.float32
    )
    weight_grad = jnp.take_along_axis(scores, slot_pos, axis=1)
    got_grads = lax.all_to_all(partial_grad, "mem", split_axis=0, concat_axis=0, tiled=True)
    owner_table = jax.ops.segment_sum(
        got_grads.reshape(-1, feature), got_lists.reshape(-1), num_segments=owned
    )
    value_grad = lax.psum_scatter(owner_table, "dp", scatter_dimension=1, tiled=True)
    return (memory_out, weight_grad, value_grad)


def solution(mesh):
    return jax.shard_map(
        on_device,
        mesh=mesh,
        in_specs=(
            P(("dp", "mem"), None),
            P(("dp", "mem"), None),
            P(("dp", "mem"), None, None),
            P("mem", None),
            P(("dp", "mem"), None),
        ),
        out_specs=(P(("dp", "mem"), None), P(("dp", "mem"), None), P("mem", "dp")),
        check_vma=False,
    )
```

profile of v0, /device:TPU:8, one launch (start us, length us, event | category | flops | bytes accessed | tf_op | source)
XLA Modules:
  0.0 712.9 jit_solution(16857974039322270438)
XLA Ops:
  7.2 0.0 copy-start
  7.2 11.5 %all-to-all-start = ((s32[32,1,32]{2,1,0:T(1,128)}), s32[32,1,32]{2,1,0:T(1,128)S(1)}, u32[]{:S(2)}, u32[]{:S(2)}) async-start(s32[32,1,32]{2,1,0:T(1,128)} %bitcast.25), calls=%async_computation | async-start | bytes 32768 | tf_op jit(solution)/shard_map/all_to_all | solution.py:21
  18.6 0.8 copy.26
  19.5 0.1 reshape.96
  19.6 0.8 copy.20
  20.4 0.1 copy.24
  20.4 0.8 and_reduce_fusion
  21.2 0.7 multiply_reduce_fusion
  21.9 0.1 copy.25
  22.0 0.1 reshape.94
  22.1 28.7 %scatter_custom_fusion.1 = bf16[131072]{0:T(1024)(128)(2,1)S(1)} fusion(s32[4096]{0:T(1024)S(1)} %reshape.94, bf16[4096]{0:T(1024)(128)(2,1)S(1)} %reshape.96, bf16[]{:T(256)} %constant.7.clone.1), kind=kCustom, calls=%fused_computation.9 | custom fusion | bytes 262146
  50.8 0.1 reshape.71
  50.9 9.3 %fusion.5 = f32[1024,4096]{1,0:T(8,128)} fusion(bf16[128,1024]{1,0:T(8,128)(2,1)S(1)} %reshape.71, bf16[128,4096]{1,0:T(8,128)(2,1)} %param.9), kind=kOutput, calls=%fused_computation.20 | convolution fusion | flops 1073741824 | bytes 18087936 | tf_op jit(solution)/shard_map/dot_general | solution.py:17
  60.2 0.0 all-to-all-done
  60.2 9.9 %all-to-all-start.2 = ((f32[32,32,4096]{2,1,0:T(8,128)}), f32[32,32,4096]{2,1,0:T(8,128)}, u32[]{:S(2)}, u32[]{:S(2)}) async-start(f32[32,32,4096]{2,1,0:T(8,128)} %bitcast.22), calls=%async_computation.2 | async-start | bytes 33554432 | tf_op jit(solution)/shard_map/all_to_all | solution.py:31
  70.2 0.5 broadcast.58
  70.7 0.7 reduce.9
  71.4 0.1 reshape.63
  71.5 0.0 copy-done
  71.5 7.7 %gather_fusion = bf16[1024,4096]{1,0:T(8,128)(2,1)} fusion(bf16[256,4096]{1,0:T(8,128)(2,1)S(1)} %copy-done, s32[1024]{0:T(1024)S(1)} %broadcast_clamp_fusion), kind=kCustom, calls=%fused_computation | custom fusion | bytes 16781312 | tf_op jit(solution)/shard_map/gather | solution.py:22
  79.2 356.7 %all-to-all-done.2 = f32[32,32,4096]{2,1,0:T(8,128)} async-done(((f32[32,32,4096]{2,1,0:T(8,128)}), f32[32,32,4096]{2,1,0:T(8,128)}, u32[]{:S(2)}, u32[]{:S(2)}) %all-to-all-start.2) | async-done | bytes 16777248 | tf_op jit(solution)/shard_map/all_to_all | solution.py:31
  435.8 41.2 %all-to-all-start.1 = ((bf16[32,32,4096]{2,1,0:T(8,128)(2,1)}), bf16[32,32,4096]{2,1,0:T(8,128)(2,1)}, u32[]{:S(2)}, u32[]{:S(2)}) async-start(bf16[32,32,4096]{2,1,0:T(8,128)(2,1)} %bitcast.23), calls=%async_computation.1 | async-start | bytes 16777216 | tf_op jit(solution)/shard_map/all_to_all | solution.py:23
  477.1 0.0 reduce-scatter.2.cloned.1.call-start
  477.1 0.1 reshape.88
  477.2 28.5 %scatter_custom_fusion = f32[256,4096]{1,0:T(8,128)} fusion(s32[1024]{0:T(1024)S(1)} %reshape.88, f32[1024,4096]{1,0:T(8,128)} %bitcast.7, f32[]{:T(128)} %constant.13.clone.1), kind=kCustom, calls=%fused_computation.5 | custom fusion | flops 4194304 | bytes 4194816 | tf_op jit(solution)/shard_map/scatter-add | solution.py:32
  505.7 0.0 reduce-scatter.2.cloned.1.call-update
  505.8 0.1 reshape.80
  505.8 161.3 %all-to-all-done.1 = bf16[32,32,4096]{2,1,0:T(8,128)(2,1)} async-done(((bf16[32,32,4096]{2,1,0:T(8,128)(2,1)}), bf16[32,32,4096]{2,1,0:T(8,128)(2,1)}, u32[]{:S(2)}, u32[]{:S(2)}) %all-to-all-start.1) | async-done | bytes 8388640 | tf_op jit(solution)/shard_map/all_to_all | solution.py:23
  667.2 5.9 convolution_bitcast_fusion
  673.1 26.5 %gather_fusion.1 = f32[4096]{0:T(1024)S(1)} fusion(f32[128,1024]{0,1:T(8,128)S(1)} %convolution_bitcast_fusion, s32[4096]{0:T(1024)S(1)} %reshape.80), kind=kCustom, calls=%fused_computation.1 | custom fusion | bytes 65536 | tf_op jit(solution)/shard_map/jit(take_along_axis)/gather | solution.py:30
  699.7 0.1 reshape.83
  699.8 0.7 copy.27
  700.5 5.6 convolution_convert_fusion
  706.1 0.0 reduce-scatter.2.cloned.1.call-done
  (7 shorter events, 0.1 us)
Async XLA Ops:
  7.2 64.3 %copy-start = (bf16[256,4096]{1,0:T(8,128)(2,1)S(1)}, bf16[256,4096]{1,0:T(8,128)(2,1)}, u32[]{:S(2)}) copy-start(bf16[256,4096]{1,0:T(8,128)(2,1)} %param.8) | copy-start | bytes 6291460
  7.2 53.1 %all-to-all-start = ((s32[32,1,32]{2,1,0:T(1,128)}), s32[32,1,32]{2,1,0:T(1,128)S(1)}, u32[]{:S(2)}, u32[]{:S(2)}) async-start(s32[32,1,32]{2,1,0:T(1,128)} %bitcast.25), calls=%async_computation | async-start | bytes 32768 | tf_op jit(solution)/shard_map/all_to_all | solution.py:21
  60.2 375.6 %all-to-all-start.2 = ((f32[32,32,4096]{2,1,0:T(8,128)}), f32[32,32,4096]{2,1,0:T(8,128)}, u32[]{:S(2)}, u32[]{:S(2)}) async-start(f32[32,32,4096]{2,1,0:T(8,128)} %bitcast.22), calls=%async_computation.2 | async-start | bytes 33554432 | tf_op jit(solution)/shard_map/all_to_all | solution.py:31
  435.8 231.3 %all-to-all-start.1 = ((bf16[32,32,4096]{2,1,0:T(8,128)(2,1)}), bf16[32,32,4096]{2,1,0:T(8,128)(2,1)}, u32[]{:S(2)}, u32[]{:S(2)}) async-start(bf16[32,32,4096]{2,1,0:T(8,128)(2,1)} %bitcast.23), calls=%async_computation.1 | async-start | bytes 16777216 | tf_op jit(solution)/shard_map/all_to_all | solution.py:23
  477.1 229.0 %reduce-scatter.2.cloned.1.call-start = ((), (), s32[]{:S(2)}) async-start(), calls=%async_computation.4 | async-start | bytes 4718592 | tf_op jit(solution)/shard_map/reduce_scatter | solution.py:35
Sparse Core Ops, SparseCore 0:
  505.8 38.7 reduce-scatter.1
where the time goes:
time: 713 us
  waiting for transfers between devices  518 us (73%)
  local copies, waits for them, and re-layouts  66.5 us (9%)
  starting transfers between devices  62.6 us (9%)
  other arithmetic  30.7 us (4%)
  matrix products  20.9 us (3%)
  between operations  14.1 us (2%)
    all_to_all x1, waiting for transfers between devices, on_device(): lax.all_to_all(partial_grad, 'mem', split_axis=0, concat_axis=0, tiled=True)  357 us
    all_to_all x1, waiting for transfers between devices, on_device(): lax.all_to_all(fetched, 'mem', split_axis=0, concat_axis=0, tiled=True)  161 us
    all_to_all x1, starting transfers between devices, on_device(): lax.all_to_all(fetched, 'mem', split_axis=0, concat_axis=0, tiled=True)  41.2 us
    unnamed x9, local copies, waits for them, and re-layouts  31.3 us
    scatter-add x1, other arithmetic, on_device(): jax.ops.segment_sum(got_grads.reshape(-1, feature), got_lists.reshape(-1)...  28.5 us
    gather x2, local copies, waits for them, and re-layouts, on_device(): weight_grad = jnp.take_along_axis(scores, slot_pos, axis=1)  26.6 us
  transfers between devices with their start and end apart: 4, of which 2 were waited for; matrix products, arithmetic and copies ran while one was open for 17% of the time, Pallas kernels for 0%

commit v1 on v0

v1 whole, which is shorter than its diff:
```python
import jax
import jax.numpy as jnp
from jax import lax
from jax.experimental import pallas as pl
from jax.experimental.pallas import tpu as pltpu
from jax.sharding import Mesh
from jax.sharding import PartitionSpec as P

BF = jnp.bfloat16
F32 = jnp.float32
NZ, NX, ND = 8, 4, 8
NS = ND * NX
TOK = 128
CB = 128
CAP = 32
TOPK = 32
OWN = 256
GRP = NX * CAP
POS = NZ * GRP
R_W = TOK
R_C = R_W + TOPK
R_T = R_C + TOPK
R_ALL = R_T + 16
B_ALL = TOK + 2 * TOPK
VMEM = 56 * 1024 * 1024


def split(v):
    hi = v.astype(BF)
    return hi, (v - hi.astype(F32)).astype(BF)


def pack_kernel(z_ref, cot_ref, w_ref, pos_ref, list_ref, out_ref):
    z = z_ref[0]
    pos = pos_ref[...]
    plane = ((pos >> 7) - z) & (NZ - 1)
    code = ((pos & (GRP - 1)) + GRP) << plane
    code_t = code.astype(F32).T.astype(BF)
    w_t = w_ref[...].astype(F32).T.astype(BF)
    rows = [list_ref[pl.ds((z + h) & (NZ - 1), 1), :] for h in range(NZ)]
    lists = jnp.concatenate(rows + rows, axis=0).astype(F32).astype(BF)
    for i in range(out_ref.shape[0]):
        out_ref[i, 0:TOK, :] = cot_ref[:, i * CB:(i + 1) * CB]
        out_ref[i, R_W:R_C, :] = w_t
        out_ref[i, R_C:R_T, :] = code_t
        out_ref[i, R_T:R_ALL, :] = lists


def pack(z, cot, w, pos, lists):
    per = 8
    return pl.pallas_call(
        pack_kernel,
        grid=(NS // per,),
        in_specs=[
            pl.BlockSpec(memory_space=pltpu.SMEM),
            pl.BlockSpec((TOK, per * CB), lambda g: (0, g)),
            pl.BlockSpec((TOK, TOPK), lambda g: (0, 0)),
            pl.BlockSpec((TOK, TOPK), lambda g: (0, 0)),
            pl.BlockSpec((NZ, GRP), lambda g: (0, 0)),
        ],
        out_specs=pl.BlockSpec((per, R_ALL, CB), lambda g: (g, 0, 0)),
        out_shape=jax.ShapeDtypeStruct((NS, R_ALL, CB), BF),
        name="pack",
    )(z, cot, w, pos, lists)


def grads_kernel(z_ref, r_ref, wt_ref, out_ref, parts, lists):
    h = pl.program_id(0)

    @pl.when(h == 0)
    def _():
        for e in range(NS):
            lists[e * 16:(e + 1) * 16, :] = r_ref[e, R_T:R_ALL, :].astype(F32)

    sub = lax.broadcasted_iota(jnp.int32, (GRP, TOK), 0)
    codes = ((sub + GRP) << h).astype(F32).astype(BF)

    def one(e, carry):
        acc = jnp.zeros((GRP, TOK), BF)
        ce = r_ref[e, R_C:R_T, :]
        we = r_ref[e, R_W:R_C, :]
        for k in range(TOPK):
            acc = jnp.where(codes == ce[k:k + 1, :], we[k:k + 1, :], acc)
        wt_ref[e] = acc
        hi, lo = split(jnp.dot(acc, r_ref[e, 0:TOK, :], preferred_element_type=F32))
        for x in range(NX):
            parts[x, pl.ds(pl.multiple_of(e * CAP, CAP), CAP), 0:CB] = hi[x * CAP:(x + 1) * CAP]
            parts[x, pl.ds(pl.multiple_of(e * CAP, CAP), CAP), CB:2 * CB] = lo[x * CAP:(x + 1) * CAP]
        return carry

    lax.fori_loop(0, NS, one, 0)
    lane = lax.broadcasted_iota(jnp.int32, (8, GRP), 1) // CAP
    row = lax.broadcasted_iota(jnp.int32, (OWN, GRP), 0).astype(F32)
    raw = [lists[pl.ds(q * 16 + h, 8, stride=64), :] for q in range(4)]
    for x in range(NX):
        rows = jnp.zeros((8, GRP), F32)
        for q in range(4):
            rows = jnp.where(lane == q, pltpu.roll(raw[q], ((q - x) % 4) * CAP, 1), rows)
        total = jnp.zeros((OWN, 2 * CB), F32)
        for g in range(8):
            hot = jnp.where(row == rows[g:g + 1, :], 1.0, 0.0).astype(BF)
            total += jnp.dot(hot, parts[x, g * GRP:(g + 1) * GRP, :], preferred_element_type=F32)
        out_ref[0, x] = total[:, :CB] + total[:, CB:]


def grads(z, r):
    spec = pltpu.PrefetchScalarGridSpec(
        num_scalar_prefetch=1,
        grid=(NZ,),
        in_specs=[pl.BlockSpec((NS, R_ALL, CB), lambda h, z: (0, 0, 0))],
        out_specs=[
            pl.BlockSpec((NS, GRP, TOK), lambda h, z: (0, h, 0)),
            pl.BlockSpec((1, NX, OWN, CB), lambda h, z: ((z[0] + h) & (NZ - 1), 0, 0, 0)),
        ],
        scratch_shapes=[
            pltpu.VMEM((NX, NS * CAP, 2 * CB), BF),
            pltpu.VMEM((NS * 16, GRP), F32),
        ],
    )
    return pl.pallas_call(
        grads_kernel,
        grid_spec=spec,
        out_shape=[
            jax.ShapeDtypeStruct((NS, POS, TOK), BF),
            jax.ShapeDtypeStruct((NZ, NX, OWN, CB), F32),
        ],
        compiler_params=pltpu.CompilerParams(vmem_limit_bytes=VMEM),
        cost_estimate=pl.CostEstimate(flops=6 * 10**9, bytes_accessed=20 * 2**20, transcendentals=0),
        name="grads",
    )(z, r)


def bags_kernel(z_ref, r_ref, wt_ref, v_ref, out_ref, arrived, hots, lists):
    z = z_ref[0]
    for e in range(NS):
        lists[e * 16:(e + 1) * 16, :] = r_ref[e, R_T:R_ALL, :].astype(F32)
    col = lax.broadcasted_iota(jnp.int32, (GRP, OWN), 1).astype(F32)

    def fetch(h, carry):
        cols = lists[pl.ds(h, NS, stride=16), :].T
        for e in range(NS):
            hot = jnp.where(col == cols[:, e:e + 1], 1.0, 0.0).astype(BF)
            for x in range(NX):
                hots[x, e * CAP:(e + 1) * CAP, :] = hot[x * CAP:(x + 1) * CAP]
        for x in range(NX):
            got = jnp.dot(
                hots[x], v_ref[(z + h) & (NZ - 1), x], preferred_element_type=F32
            ).astype(BF)
            at = pl.multiple_of(h * GRP + x * CAP, CAP)
            for e in range(NS):
                arrived[e, pl.ds(at, CAP), :] = got[e * CAP:(e + 1) * CAP]
        return carry

    lax.fori_loop(0, NZ, fetch, 0)

    def one(e, carry):
        bag = lax.dot_general(
            wt_ref[e], arrived[e], (((0,), (0,)), ((), ())), preferred_element_type=F32
        )
        out_ref[e, 0:TOK, :] = bag.astype(BF)
        scores = lax.dot_general(
            r_ref[e, 0:TOK, :], arrived[e], (((1,), (1,)), ((), ())), preferred_element_type=F32
        )
        code = r_ref[e, R_C:R_T, :].astype(F32)
        code = jnp.concatenate([code] * (TOK // TOPK), axis=0).T.astype(jnp.int32)
        plane = jnp.zeros_like(code)
        for i in range(1, NZ):
            plane += (code >= (GRP << i)).astype(jnp.int32)
        within = (code >> plane) - GRP
        acc = jnp.zeros((TOK, GRP), F32)
        for h in range(NZ):
            tile = jnp.take_along_axis(
                scores[:, h * GRP:(h + 1) * GRP], within, axis=1, mode="promise_in_bounds"
            )
            acc = jnp.where(plane == h, tile, acc)
        hi, lo = split(acc.T[0:TOPK, :])
        out_ref[e, TOK:TOK + TOPK, :] = hi
        out_ref[e, TOK + TOPK:B_ALL, :] = lo
        return carry

    lax.fori_loop(0, NS, one, 0)


def bags(z, r, wt, v):
    vm = pl.BlockSpec(memory_space=pltpu.VMEM)
    return pl.pallas_call(
        bags_kernel,
        in_specs=[pl.BlockSpec(memory_space=pltpu.SMEM), vm, vm, vm],
        out_specs=vm,
        out_shape=jax.ShapeDtypeStruct((NS, B_ALL, CB), BF),
        scratch_shapes=[
            pltpu.VMEM((NS, POS, CB), BF),
            pltpu.VMEM((NX, NS * CAP, OWN), BF),
            pltpu.VMEM((NS * 16, GRP), F32),
        ],
        compiler_params=pltpu.CompilerParams(vmem_limit_bytes=VMEM),
        cost_estimate=pl.CostEstimate(flops=6 * 10**9, bytes_accessed=16 * 2**20, transcendentals=0),
        name="bags",
    )(z, r, wt, v)


def unpack_kernel(b_ref, out_ref, wg_ref, total):
    g = pl.program_id(0)
    part = jnp.zeros((TOPK, TOK), F32)
    for i in range(b_ref.shape[0]):
        out_ref[:, i * CB:(i + 1) * CB] = b_ref[i, 0:TOK, :]
        part += b_ref[i, TOK:TOK + TOPK, :].astype(F32) + b_ref[i, TOK + TOPK:B_ALL, :].astype(F32)
    part += jnp.where(g == 0, 0.0, total[...])
    total[...] = part
    wg_ref[...] = part.T


def unpack(b):
    per = 8
    return pl.pallas_call(
        unpack_kernel,
        grid=(NS // per,),
        in_specs=[pl.BlockSpec((per, B_ALL, CB), lambda g: (g, 0, 0))],
        out_specs=[
            pl.BlockSpec((TOK, per * CB), lambda g: (0, g)),
            pl.BlockSpec((TOK, TOPK), lambda g: (0, 0)),
        ],
        out_shape=[
            jax.ShapeDtypeStruct((TOK, NS * CB), BF),
            jax.ShapeDtypeStruct((TOK, TOPK), F32),
        ],
        scratch_shapes=[pltpu.VMEM((TOPK, TOK), F32)],
        name="unpack",
    )(b)


def on_device(slot_weight, slot_pos, touched, values, cotangent):
    z = lax.axis_index("z").astype(jnp.int32).reshape(1)
    d = lax.axis_index("dp")
    mine = lax.dynamic_slice(values, (0, d * (NX * CB)), (OWN, NX * CB))
    mine = mine.reshape(OWN, NX, CB).transpose(1, 0, 2)
    mine = lax.all_to_all(mine, "x", 0, 0, tiled=True)
    v = lax.all_gather(mine, "z")
    r = pack(z, cotangent, slot_weight, slot_pos, touched.reshape(NZ, GRP))
    r = lax.all_to_all(r, ("dp", "x"), 0, 0, tiled=True)
    wt, table = grads(z, r)
    table = lax.psum_scatter(table, "z", scatter_dimension=0, tiled=True)
    b = bags(z, r, wt, v)
    b = lax.all_to_all(b, ("dp", "x"), 0, 0, tiled=True)
    memory_out, weight_grad = unpack(b)
    table = lax.all_to_all(table.reshape(NX, OWN, CB), "x", 0, 0, tiled=True)
    value_grad = table.transpose(1, 0, 2).reshape(OWN, NX * CB)
    return memory_out, weight_grad, value_grad


def solution(mesh):
    cube = Mesh(mesh.devices.reshape(ND, NZ, NX), ("dp", "z", "x"))
    tokens = ("dp", "z", "x")
    return jax.shard_map(
        on_device,
        mesh=cube,
        in_specs=(
            P(tokens, None),
            P(tokens, None),
            P(tokens, None, None),
            P(("z", "x"), None),
            P(tokens, None),
        ),
        out_specs=(P(tokens, None), P(tokens, None), P(("z", "x"), "dp")),
        check_vma=False,
    )
```

time: 713 us -> 208 us (0.29)
  waiting for transfers between devices: 518 us -> 4.72 us
  Pallas kernels: 0 us -> 109 us
  blocking collectives: 0 us -> 67.4 us
  local copies, waits for them, and re-layouts: 66.5 us -> 7.32 us
  starting transfers between devices: 62.6 us -> 3.55 us
  other arithmetic: 30.7 us -> 0 us
  matrix products: 20.9 us -> 0 us
    all_to_all x3 -> x1, waiting for transfers between devices: 518 us -> 4.66 us  [on_device(): table = lax.all_to_all(table.reshape(NX, OWN, CB), 'x', 0, 0, tiled=True)]
    pallas_call x0 -> x4, Pallas kernels: none -> 109 us  [the longest x1 67.1 us: grads(): pl.pallas_call(grads_kernel, grid_spec=spec, out_shape=[jax.ShapeDtypeStr...]
    all_to_all x0 -> x3, blocking collectives: none -> 67.4 us  [the longest x1 29.2 us: on_device(): r = lax.all_to_all(r, ('dp', 'x'), 0, 0, tiled=True)]
    all_to_all x3 -> x1, starting transfers between devices: 62.6 us -> 3.47 us  [on_device(): table = lax.all_to_all(table.reshape(NX, OWN, CB), 'x', 0, 0, tiled=True)]
    gather x3 -> x0, local copies, waits for them, and re-layouts: 34.3 us -> none  [the longest x2 26.6 us: on_device(): weight_grad = jnp.take_along_axis(scores, slot_pos, axis=1)]
    scatter-add x1 -> x0, other arithmetic: 28.5 us -> none  [on_device(): jax.ops.segment_sum(got_grads.reshape(-1, feature), got_lists.reshape(-1)...]
    unnamed x9 -> x13, local copies, waits for them, and re-layouts: 31.3 us -> 5.6 us
    dot_general x3 -> x0, matrix products: 20.9 us -> none  [the longest x1 9.3 us: on_device(): lax.dot_general(dense_w, cotangent, (((0,), (0,)), ((), ())), preferred_e...]
  transfers between devices with their start and end apart: 4 -> 3, of which waited for: 2 -> 1; matrix products, arithmetic and copies ran while one was open for 17% -> 2% of each run, Pallas kernels for 0% -> 53%
where the time goes in v1:
time: 208 us; the launch traced here: 206 us
  Pallas kernels  109 us (52%)
  blocking collectives  67.4 us (32%)
  between operations  14.1 us (7%)
  local copies, waits for them, and re-layouts  7.32 us (4%)
  waiting for transfers between devices  4.72 us (2%)
  starting transfers between devices  3.55 us (2%)
    pallas_call x1, Pallas kernels, grads(): pl.pallas_call(grads_kernel, grid_spec=spec, out_shape=[jax.ShapeDtypeStr...  67.1 us
    pallas_call x1, Pallas kernels, bags(): pl.pallas_call(bags_kernel, in_specs=[pl.BlockSpec(memory_space=pltpu.SME...  35.1 us
    all_to_all x1, blocking collectives, on_device(): r = lax.all_to_all(r, ('dp', 'x'), 0, 0, tiled=True)  29.2 us
    all_to_all x1, blocking collectives, on_device(): b = lax.all_to_all(b, ('dp', 'x'), 0, 0, tiled=True)  27.5 us
    all_to_all x1, blocking collectives, on_device(): mine = lax.all_to_all(mine, 'x', 0, 0, tiled=True)  10.8 us
    unnamed x13, local copies, waits for them, and re-layouts  5.6 us
    all_to_all x1, waiting for transfers between devices, on_device(): table = lax.all_to_all(table.reshape(NX, OWN, CB), 'x', 0, 0, tiled=True)  4.66 us
  transfers between devices with their start and end apart: 3, of which 1 were waited for; matrix products, arithmetic and copies ran while one was open for 2% of the time, Pallas kernels for 53%

profile of v1, /device:TPU:8, one launch (start us, length us, event | category | flops | bytes accessed | tf_op | source)
XLA Modules:
  0.0 206.5 jit_solution(2085995020176361134)
XLA Ops:
  7.2 0.0 copy-start
  7.2 0.0 copy-start.2
  7.2 0.0 copy-start.3
  7.2 0.0 copy-start.1
  7.2 0.0 all-gather.3.cloned.1.call-start
  7.3 1.5 copy-done
  8.8 0.1 copy.25
  8.9 10.8 %all_to_all.20 = bf16[4,256,128]{1,2,0:T(8,128)(2,1)S(1)} all-to-all(bf16[4,256,128]{1,2,0:T(8,128)(2,1)S(1)} %bitcast.10), channel_id=1, replica_groups=mesh['dp'=8,'z'=8,'x'=4] {'x'}, dimensions={0} | all-to-all | bytes 524288 | tf_op jit(solution)/shard_map/all_to_all | solution.py:237
  19.7 0.8 copy.21
  20.5 0.0 all-gather.3.cloned.1.call-update
  20.6 0.0 reduce-scatter.2.cloned.1.call-start
  20.6 0.0 copy-done.2
  20.6 0.7 reshape.22.list_ref
  21.3 0.0 copy-done.3
  21.3 0.7 copy.18.w_ref
  22.0 0.0 copy-done.1
  22.0 0.7 copy.19.pos_ref
  22.7 3.6 %pack.1 = bf16[32,208,128]{2,1,0:T(8,128)(2,1)} custom-call(s32[1]{0:T(128)} %bitcast.z_ref, bf16[128,4096]{1,0:T(8,128)(2,1)} %cot_ref.1, bf16[128,32]{1,0:T(8,128)(2,1)} %copy.18.w_ref, s32[128,32]{1,0:T(8,128)} %copy.19.pos_ref, s32[8,128]{1,0:T(8,128)} %reshape.22.list_ref), custom_call_target="tpu_custom_call" | custom-call | tf_op jit(solution)/shard_map/pack/pallas_call | solution.py:51
  26.4 29.2 %all_to_all.21.r_ref = bf16[32,208,128]{2,1,0:T(8,128)(2,1)} all-to-all(bf16[32,208,128]{2,1,0:T(8,128)(2,1)} %pack.1), channel_id=1, replica_groups=mesh['dp'=8,'z'=8,'x'=4] {'dp','x'}, dimensions={0} | all-to-all | bytes 3407872 | tf_op jit(solution)/shard_map/all_to_all | solution.py:240
  55.5 67.1 %grads.1 = (bf16[32,1024,128]{2,1,0:T(8,128)(2,1)}, f32[8,4,256,128]{3,2,1,0:T(8,128)}) custom-call(s32[1]{0:T(128)} %bitcast.z_ref, bf16[32,208,128]{2,1,0:T(8,128)(2,1)} %all_to_all.21.r_ref), custom_call_target="tpu_custom_call" | custom-call | flops 6000000000 | bytes 20971520 | tf_op jit(solution)/shard_map/grads/pallas_call | solution.py:120
  122.6 0.0 reduce-scatter.2.cloned.1.call-update
  122.6 0.0 all-gather.3.cloned.1.call-done
  122.7 35.1 %bags.1 = bf16[32,192,128]{2,1,0:T(8,128)(2,1)} custom-call(s32[1]{0:T(128)} %bitcast.z_ref, bf16[32,208,128]{2,1,0:T(8,128)(2,1)} %all_to_all.21.r_ref, bf16[32,1024,128]{2,1,0:T(8,128)(2,1)} %get-tuple-element.7.wt_ref, bf16[8,4,256,128]{3,2,1,0:T(8,128)(2,1)} %bitcast.12), custom_call_target="tpu_custom_call" | custom-call | flops 6000000000 | bytes 16777216 | tf_op jit(solution)/shard_map/bags/pallas_call | solution.py:186
  157.7 27.5 %all_to_all.22.b_ref = bf16[32,192,128]{2,1,0:T(8,128)(2,1)} all-to-all(bf16[32,192,128]{2,1,0:T(8,128)(2,1)} %bags.1), channel_id=1, replica_groups=mesh['dp'=8,'z'=8,'x'=4] {'dp','x'}, dimensions={0} | all-to-all | bytes 3145728 | tf_op jit(solution)/shard_map/all_to_all | solution.py:244
  185.2 0.0 reduce-scatter.2.cloned.1.call-done
  185.2 3.5 %all-to-all-start.3 = ((f32[4,256,128]{2,1,0:T(8,128)}), f32[4,256,128]{2,1,0:T(8,128)S(1)}, u32[]{:S(2)}, u32[]{:S(2)}) async-start(f32[4,256,128]{2,1,0:T(8,128)} %bitcast.11), calls=%async_computation.4 | async-start | bytes 1048576 | tf_op jit(solution)/shard_map/all_to_all | solution.py:246
  188.7 3.6 %unpack.1 = (bf16[128,4096]{1,0:T(8,128)(2,1)}, f32[128,32]{1,0:T(8,128)}) custom-call(bf16[32,192,128]{2,1,0:T(8,128)(2,1)} %all_to_all.22.b_ref), custom_call_target="tpu_custom_call" | custom-call | tf_op jit(solution)/shard_map/unpack/pallas_call | solution.py:215
  192.3 1.5 copy.23
  193.8 4.7 %all-to-all-done.3 = f32[4,256,128]{2,1,0:T(8,128)S(1)} async-done(((f32[4,256,128]{2,1,0:T(8,128)}), f32[4,256,128]{2,1,0:T(8,128)S(1)}, u32[]{:S(2)}, u32[]{:S(2)}) %all-to-all-start.3) | async-done | bytes 524320 | tf_op jit(solution)/shard_map/all_to_all | solution.py:246
  198.5 0.2 copy.22
  198.7 1.0 copy.24
  (1 shorter events, 0.0 us)
Async XLA Ops:
  7.2 1.6 copy-start
  7.2 13.4 %copy-start.2 = (s32[1,32,32]{2,1,0:T(8,128)S(1)}, s32[1,32,32]{2,1,0:T(8,128)}, u32[]{:S(2)}) copy-start(s32[1,32,32]{2,1,0:T(8,128)} %param.7) | copy-start | bytes 12292
  7.2 14.1 %copy-start.3 = (bf16[128,32]{0,1:T(8,128)(2,1)S(1)}, bf16[128,32]{0,1:T(8,128)(2,1)}, u32[]{:S(2)}) copy-start(bf16[128,32]{0,1:T(8,128)(2,1)} %param.5) | copy-start | bytes 24580
  7.2 14.8 %copy-start.1 = (s32[128,32]{0,1:T(8,128)S(1)}, s32[128,32]{0,1:T(8,128)}, u32[]{:S(2)}) copy-start(s32[128,32]{0,1:T(8,128)} %param.6) | copy-start | bytes 49156
  7.2 115.4 %all-gather.3.cloned.1.call-start = ((), (), s32[]{:S(2)}) async-start(), calls=%async_computation.6 | async-start | bytes 2359296 | tf_op jit(solution)/shard_map/all_gather | solution.py:238
  20.6 164.6 %reduce-scatter.2.cloned.1.call-start = ((), (), s32[]{:S(2)}) async-start(), calls=%async_computation.5 | async-start | bytes 4718592 | tf_op jit(solution)/shard_map/reduce_scatter | solution.py:242
  185.2 13.3 %all-to-all-start.3 = ((f32[4,256,128]{2,1,0:T(8,128)}), f32[4,256,128]{2,1,0:T(8,128)S(1)}, u32[]{:S(2)}, u32[]{:S(2)}) async-start(f32[4,256,128]{2,1,0:T(8,128)} %bitcast.11), calls=%async_computation.4 | async-start | bytes 1048576 | tf_op jit(solution)/shard_map/all_to_all | solution.py:246
Sparse Core Ops, SparseCore 0:
  20.7 42.2 all-gather.2
  122.7 55.5 reduce-scatter.1

commit v2 on v1

v2 whole, which is shorter than its diff:
```python
import jax
import jax.numpy as jnp
from jax import lax
from jax.experimental import pallas as pl
from jax.experimental.pallas import tpu as pltpu
from jax.sharding import Mesh
from jax.sharding import PartitionSpec as P

BF = jnp.bfloat16
F32 = jnp.float32
NZ, NX, ND = 8, 4, 8
NS = ND * NX
TOK = 128
CB = 128
CAP = 32
TOPK = 32
OWN = 256
GRP = NX * CAP
POS = NZ * GRP
M_C = TOPK
M_T = 2 * TOPK
M_ALL = M_T + 16
VMEM = 56 * 1024 * 1024


def split(v):
    hi = v.astype(BF)
    return hi, (v - hi.astype(F32)).astype(BF)


def slots_kernel(z_ref, w_ref, pos_ref, list_ref, out_ref):
    z = z_ref[0]
    pos = pos_ref[...]
    plane = ((pos >> 7) - z) & (NZ - 1)
    code = (((pos & (GRP - 1)) + GRP) << plane).astype(F32).astype(BF)
    rows = [list_ref[pl.ds((z + h) & (NZ - 1), 1), :] for h in range(NZ)]
    lists = jnp.concatenate(rows + rows, axis=0).astype(F32).astype(BF)
    w = w_ref[...]
    for i in range(NS):
        out_ref[i, 0:M_C, :] = w
        out_ref[i, M_C:M_T, :] = code
        out_ref[i, M_T:M_ALL, :] = lists


def cost(us):
    return pl.CostEstimate(flops=int(us * 1e9), bytes_accessed=2**20, transcendentals=0)


def slots(z, w, pos, lists):
    vm = pl.BlockSpec(memory_space=pltpu.VMEM)
    return pl.pallas_call(
        slots_kernel,
        in_specs=[pl.BlockSpec(memory_space=pltpu.SMEM), vm, vm, vm],
        out_specs=vm,
        out_shape=jax.ShapeDtypeStruct((NS, M_ALL, TOK), BF),
        cost_estimate=cost(2),
        name="slots",
    )(z, w, pos, lists)


def blocks_kernel(cot_ref, out_ref):
    for i in range(out_ref.shape[0]):
        out_ref[i] = cot_ref[:, i * CB:(i + 1) * CB]


def blocks(cot):
    per = 8
    return pl.pallas_call(
        blocks_kernel,
        grid=(NS // per,),
        in_specs=[pl.BlockSpec((TOK, per * CB), lambda g: (0, g))],
        out_specs=pl.BlockSpec((per, TOK, CB), lambda g: (g, 0, 0)),
        out_shape=jax.ShapeDtypeStruct((NS, TOK, CB), BF),
        cost_estimate=cost(2),
        name="blocks",
    )(cot)


def dense_kernel(m_ref, wt_ref):
    sub = lax.broadcasted_iota(jnp.int32, (GRP, TOK), 0)
    codes = ((sub + GRP) << pl.program_id(0)).astype(F32).astype(BF)

    def one(e, carry):
        acc = jnp.zeros((GRP, TOK), BF)
        we = m_ref[e, 0:M_C, :]
        ce = m_ref[e, M_C:M_T, :]
        for k in range(TOPK):
            acc = jnp.where(codes == ce[k:k + 1, :], we[k:k + 1, :], acc)
        wt_ref[e] = acc
        return carry

    lax.fori_loop(0, NS, one, 0, unroll=4)


def dense(m):
    return pl.pallas_call(
        dense_kernel,
        grid=(NZ,),
        in_specs=[pl.BlockSpec((NS, M_ALL, TOK), lambda h: (0, 0, 0))],
        out_specs=pl.BlockSpec((NS, GRP, TOK), lambda h: (0, h, 0)),
        out_shape=jax.ShapeDtypeStruct((NS, POS, TOK), BF),
        compiler_params=pltpu.CompilerParams(vmem_limit_bytes=VMEM),
        cost_estimate=cost(25),
        name="dense",
    )(m)


def grads_kernel(z_ref, m_ref, c_ref, wt_ref, out_ref, parts, lists):
    h = pl.program_id(0)

    @pl.when(h == 0)
    def _():
        for e in range(NS):
            lists[e * 16:(e + 1) * 16, :] = m_ref[e, M_T:M_ALL, :].astype(F32)

    for e in range(NS):
        hi, lo = split(jnp.dot(wt_ref[e], c_ref[e], preferred_element_type=F32))
        for x in range(NX):
            at = slice(e * CAP, (e + 1) * CAP)
            parts[x, at, 0:CB] = hi[x * CAP:(x + 1) * CAP]
            parts[x, at, CB:2 * CB] = lo[x * CAP:(x + 1) * CAP]
    lane = lax.broadcasted_iota(jnp.int32, (8, GRP), 1) // CAP
    row = lax.broadcasted_iota(jnp.int32, (OWN, GRP), 0).astype(F32).astype(BF)
    raw = [lists[pl.ds(q * 16 + h, 8, stride=64), :] for q in range(4)]
    for x in range(NX):
        rows = jnp.zeros((8, GRP), F32)
        for q in range(4):
            rows = jnp.where(lane == q, pltpu.roll(raw[q], ((q - x) % 4) * CAP, 1), rows)
        rows = rows.astype(BF)
        one, zero = jnp.ones((), BF), jnp.zeros((), BF)
        hot = jnp.concatenate([jnp.where(row == rows[g:g + 1, :], one, zero) for g in range(8)], axis=1)
        total = jnp.dot(hot, parts[x], preferred_element_type=F32)
        out_ref[0, x] = total[:, :CB] + total[:, CB:]


def grads(z, m, c, wt):
    whole = lambda h, z: (0, 0, 0)
    spec = pltpu.PrefetchScalarGridSpec(
        num_scalar_prefetch=1,
        grid=(NZ,),
        in_specs=[
            pl.BlockSpec((NS, M_ALL, TOK), whole),
            pl.BlockSpec((NS, TOK, CB), whole),
            pl.BlockSpec((NS, GRP, TOK), lambda h, z: (0, h, 0)),
        ],
        out_specs=pl.BlockSpec((1, NX, OWN, CB), lambda h, z: ((z[0] + h) & (NZ - 1), 0, 0, 0)),
        scratch_shapes=[
            pltpu.VMEM((NX, NS * CAP, 2 * CB), BF),
            pltpu.VMEM((NS * 16, GRP), F32),
        ],
    )
    return pl.pallas_call(
        grads_kernel,
        grid_spec=spec,
        out_shape=jax.ShapeDtypeStruct((NZ, NX, OWN, CB), F32),
        compiler_params=pltpu.CompilerParams(vmem_limit_bytes=VMEM),
        cost_estimate=cost(15),
        name="grads",
    )(z, m, c, wt)


EG = 8


def bags_kernel(z_ref, m_ref, wt_ref, v_ref, arrived_ref, out_ref, hots, lists):
    z = z_ref[0]
    for e in range(EG):
        lists[e * 16:(e + 1) * 16, :] = m_ref[e, M_T:M_ALL, :].astype(F32)
    col = lax.broadcasted_iota(jnp.int32, (GRP, OWN), 1).astype(F32)
    for h in range(NZ):
        cols = lists[pl.ds(h, EG, stride=16), :].T
        for e in range(EG):
            hot = jnp.where(col == cols[:, e:e + 1], 1.0, 0.0).astype(BF)
            for x in range(NX):
                hots[x, e * CAP:(e + 1) * CAP, :] = hot[x * CAP:(x + 1) * CAP]
        for x in range(NX):
            got = jnp.dot(
                hots[x], v_ref[(z + h) & (NZ - 1), x], preferred_element_type=F32
            ).astype(BF)
            at = h * GRP + x * CAP
            for e in range(EG):
                arrived_ref[e, at:at + CAP, :] = got[e * CAP:(e + 1) * CAP]
    for e in range(EG):
        bag = lax.dot_general(
            wt_ref[e], arrived_ref[e], (((0,), (0,)), ((), ())), preferred_element_type=F32
        )
        out_ref[e] = bag.astype(BF)


def bags(z, m, wt, v):
    part = lambda g: (g, 0, 0)
    return pl.pallas_call(
        bags_kernel,
        grid=(NS // EG,),
        in_specs=[
            pl.BlockSpec(memory_space=pltpu.SMEM),
            pl.BlockSpec((EG, M_ALL, TOK), part),
            pl.BlockSpec((EG, POS, TOK), part),
            pl.BlockSpec((NZ, NX, OWN, CB), lambda g: (0, 0, 0, 0)),
        ],
        out_specs=[pl.BlockSpec((EG, POS, CB), part), pl.BlockSpec((EG, TOK, CB), part)],
        out_shape=[
            jax.ShapeDtypeStruct((NS, POS, CB), BF),
            jax.ShapeDtypeStruct((NS, TOK, CB), BF),
        ],
        scratch_shapes=[
            pltpu.VMEM((NX, EG * CAP, OWN), BF),
            pltpu.VMEM((EG * 16, GRP), F32),
        ],
        compiler_params=pltpu.CompilerParams(vmem_limit_bytes=VMEM),
        cost_estimate=cost(18),
        name="bags",
    )(z, m, wt, v)


def scores_kernel(m_ref, c_ref, arrived_ref, out_ref):
    def one(e, carry):
        scores = lax.dot_general(
            c_ref[e], arrived_ref[e], (((1,), (1,)), ((), ())), preferred_element_type=F32
        )
        code = m_ref[e, M_C:M_T, :].astype(F32)
        code = jnp.concatenate([code] * (TOK // TOPK), axis=0).T.astype(jnp.int32)
        plane = jnp.zeros_like(code)
        for i in range(1, NZ):
            plane += (code >= (GRP << i)).astype(jnp.int32)
        within = (code >> plane) - GRP
        acc = jnp.zeros((TOK, GRP), F32)
        for h in range(NZ):
            tile = jnp.take_along_axis(
                scores[:, h * GRP:(h + 1) * GRP], within, axis=1, mode="promise_in_bounds"
            )
            acc = jnp.where(plane == h, tile, acc)
        out_ref[e] = acc.T[0:TOPK, :]
        return carry

    lax.fori_loop(0, EG, one, 0, unroll=2)


def scores(m, c, arrived):
    part = lambda g: (g, 0, 0)
    return pl.pallas_call(
        scores_kernel,
        grid=(NS // EG,),
        in_specs=[
            pl.BlockSpec((EG, M_ALL, TOK), part),
            pl.BlockSpec((EG, TOK, CB), part),
            pl.BlockSpec((EG, POS, CB), part),
        ],
        out_specs=pl.BlockSpec((EG, TOPK, TOK), part),
        out_shape=jax.ShapeDtypeStruct((NS, TOPK, TOK), F32),
        compiler_params=pltpu.CompilerParams(vmem_limit_bytes=VMEM),
        cost_estimate=cost(18),
        name="scores",
    )(m, c, arrived)


def gather_kernel(b_ref, out_ref):
    for i in range(b_ref.shape[0]):
        out_ref[:, i * CB:(i + 1) * CB] = b_ref[i]


def gather_blocks(b):
    per = 8
    rows = b.shape[1]
    return pl.pallas_call(
        gather_kernel,
        grid=(b.shape[0] // per,),
        in_specs=[pl.BlockSpec((per, rows, CB), lambda g: (g, 0, 0))],
        out_specs=pl.BlockSpec((rows, per * CB), lambda g: (0, g)),
        out_shape=jax.ShapeDtypeStruct((rows, b.shape[0] * CB), b.dtype),
        cost_estimate=cost(2),
        name="rows",
    )(b)


def on_device(slot_weight, slot_pos, touched, values, cotangent):
    z = lax.axis_index("z").astype(jnp.int32).reshape(1)
    d = lax.axis_index("dp")
    plane = ("dp", "x")
    m = slots(z, slot_weight.T, slot_pos.T, touched.reshape(NZ, GRP))
    m = lax.all_to_all(m, plane, 0, 0, tiled=True)
    mine = lax.dynamic_slice(values, (0, d * (NX * CB)), (OWN, NX * CB))
    mine = jnp.stack([mine[:, i * CB:(i + 1) * CB] for i in range(NX)])
    mine = lax.all_to_all(mine, "x", 0, 0, tiled=True)
    v = lax.all_gather(mine, "z")
    c = lax.all_to_all(blocks(cotangent), plane, 0, 0, tiled=True)
    wt = dense(m)
    table = grads(z, m, c, wt)
    arrived, b = bags(z, m, wt, v)
    b = lax.all_to_all(b, plane, 0, 0, tiled=True)
    b, g = lax.optimization_barrier((b, scores(m, c, arrived)))
    g = lax.all_to_all(g, plane, 0, 0, tiled=True)
    table = lax.psum_scatter(table, "z", scatter_dimension=0, tiled=True)
    table = lax.all_to_all(table.reshape(NX, OWN, CB), "x", 0, 0, tiled=True)
    value_grad = jnp.concatenate([table[i] for i in range(NX)], axis=1)
    return gather_blocks(b), g.sum(axis=0).T, value_grad


def solution(mesh):
    cube = Mesh(mesh.devices.reshape(ND, NZ, NX), ("dp", "z", "x"))
    tokens = ("dp", "z", "x")
    return jax.shard_map(
        on_device,
        mesh=cube,
        in_specs=(
            P(tokens, None),
            P(tokens, None),
            P(tokens, None, None),
            P(("z", "x"), None),
            P(tokens, None),
        ),
        out_specs=(P(tokens, None), P(tokens, None), P(("z", "x"), "dp")),
        check_vma=False,
    )
```

time: 208 us -> 161 us (0.77)
  blocking collectives: 67.4 us -> 18 us
  Pallas kernels: 109 us -> 75.3 us
  starting transfers between devices: 3.55 us -> 26.7 us
  waiting for transfers between devices: 4.72 us -> 20.6 us
  local copies, waits for them, and re-layouts: 7.32 us -> 3.39 us
  other arithmetic: 0 us -> 2.22 us
    all_to_all x3 -> x1, blocking collectives: 67.4 us -> 18 us  [on_device(): g = lax.all_to_all(g, plane, 0, 0, tiled=True)]
    pallas_call x4 -> x7, Pallas kernels: 109 us -> 75.3 us  [the longest x1 24.2 us: dense(): pl.pallas_call(dense_kernel, grid=(NZ,), in_specs=[pl.BlockSpec((NS, M_AL...]
    all_to_all x0 -> x4, starting transfers between devices: none -> 22.3 us  [the longest x1 7.38 us: on_device(): b = lax.all_to_all(b, plane, 0, 0, tiled=True)]
    all_to_all x0 -> x4, waiting for transfers between devices: none -> 12.3 us  [the longest x1 8.64 us: on_device(): m = lax.all_to_all(m, plane, 0, 0, tiled=True)]
    unnamed x13 -> x8, local copies, waits for them, and re-layouts: 5.6 us -> 1.01 us
    reduce_scatter x1, waiting for transfers between devices: 0.01 us -> 2.77 us  [on_device(): table = lax.psum_scatter(table, 'z', scatter_dimension=0, tiled=True)]
  transfers between devices with their start and end apart: 3 -> 7, of which waited for: 1 -> 4; matrix products, arithmetic and copies ran while one was open for 2% -> 1% of each run, Pallas kernels for 53% -> 47%
where the time goes in v2:
time: 161 us; the launch traced here: 160 us
  Pallas kernels  75.3 us (47%)
  starting transfers between devices  26.7 us (17%)
  waiting for transfers between devices  20.6 us (13%)
  blocking collectives  18 us (11%)
  between operations  14.1 us (9%)
  local copies, waits for them, and re-layouts  3.39 us (2%)
  other arithmetic  2.22 us (1%)
    pallas_call x1, Pallas kernels, dense(): pl.pallas_call(dense_kernel, grid=(NZ,), in_specs=[pl.BlockSpec((NS, M_AL...  24.2 us
    all_to_all x1, blocking collectives, on_device(): g = lax.all_to_all(g, plane, 0, 0, tiled=True)  18 us
    pallas_call x1, Pallas kernels, scores(): pl.pallas_call(scores_kernel, grid=(NS // EG,), in_specs=[pl.BlockSpec((E...  16.5 us
    pallas_call x1, Pallas kernels, bags(): pl.pallas_call(bags_kernel, grid=(NS // EG,), in_specs=[pl.BlockSpec(memo...  13.5 us
    pallas_call x1, Pallas kernels, grads(): pl.pallas_call(grads_kernel, grid_spec=spec, out_shape=jax.ShapeDtypeStru...  12.7 us
    all_to_all x1, waiting for transfers between devices, on_device(): m = lax.all_to_all(m, plane, 0, 0, tiled=True)  8.64 us
    all_to_all x1, starting transfers between devices, on_device(): b = lax.all_to_all(b, plane, 0, 0, tiled=True)  7.38 us
    all_to_all x1, starting transfers between devices, on_device(): m = lax.all_to_all(m, plane, 0, 0, tiled=True)  5.68 us
  transfers between devices with their start and end apart: 7, of which 4 were waited for; matrix products, arithmetic and copies ran while one was open for 1% of the time, Pallas kernels for 47%

profile of v2, /device:TPU:8, one launch (start us, length us, event | category | flops | bytes accessed | tf_op | source)
XLA Modules:
  0.0 160.2 jit_solution(10916497653574962107)
XLA Ops:
  7.2 1.0 dynamic-slice_bitcast_fusion.3
  8.1 0.7 pad_maximum_fusion.1
  8.9 4.3 %all-to-all-start.1 = ((bf16[4,256,128]{2,1,0:T(8,128)(2,1)}), bf16[4,256,128]{2,1,0:T(8,128)(2,1)S(1)}, u32[]{:S(2)}, u32[]{:S(2)}) async-start(bf16[4,256,128]{2,1,0:T(8,128)(2,1)} %pad_maximum_fusion.1), calls=%async_computation.1 | async-start | bytes 524288 | tf_op jit(solution)/shard_map/all_to_all | solution.py:284
  13.2 1.4 reshape.16.list_ref
  14.6 1.6 %slots.1 = bf16[32,80,128]{2,1,0:T(8,128)(2,1)} custom-call(s32[1]{0:T(128)} %bitcast.z_ref, bf16[32,128]{1,0:T(8,128)(2,1)} %bitcast.26, s32[32,128]{1,0:T(8,128)} %bitcast.25, s32[8,128]{1,0:T(8,128)} %reshape.16.list_ref), custom_call_target="tpu_custom_call" | custom-call | flops 2000000000 | bytes 1048576 | tf_op jit(solution)/shard_map/slots/pallas_call | solution.py:51
  16.2 3.7 %all-to-all-done.1 = bf16[4,256,128]{2,1,0:T(8,128)(2,1)S(1)} async-done(((bf16[4,256,128]{2,1,0:T(8,128)(2,1)}), bf16[4,256,128]{2,1,0:T(8,128)(2,1)S(1)}, u32[]{:S(2)}, u32[]{:S(2)}) %all-to-all-start.1) | async-done | bytes 262176 | tf_op jit(solution)/shard_map/all_to_all | solution.py:284
  19.9 0.0 copy-start.2
  19.9 5.7 %all-to-all-start = ((bf16[32,80,128]{2,1,0:T(8,128)(2,1)}), bf16[32,80,128]{2,1,0:T(8,128)(2,1)S(1)}, u32[]{:S(2)}, u32[]{:S(2)}) async-start(bf16[32,80,128]{2,1,0:T(8,128)(2,1)} %slots.1), calls=%async_computation | async-start | bytes 1310720 | tf_op jit(solution)/shard_map/all_to_all | solution.py:281
  25.5 0.0 all-gather.3.cloned.1.call-start
  25.6 3.4 %blocks.1 = bf16[32,128,128]{2,1,0:T(8,128)(2,1)} custom-call(bf16[128,4096]{1,0:T(8,128)(2,1)} %cot_ref.1), custom_call_target="tpu_custom_call" | custom-call | flops 2000000000 | bytes 1048576 | tf_op jit(solution)/shard_map/blocks/pallas_call | solution.py:68
  29.0 0.0 copy-done.2
  29.0 0.0 all-gather.3.cloned.1.call-update
  29.1 8.6 %all-to-all-done.m_ref = bf16[32,80,128]{2,1,0:T(8,128)(2,1)S(1)} async-done(((bf16[32,80,128]{2,1,0:T(8,128)(2,1)}), bf16[32,80,128]{2,1,0:T(8,128)(2,1)S(1)}, u32[]{:S(2)}, u32[]{:S(2)}) %all-to-all-start) | async-done | bytes 655392 | tf_op jit(solution)/shard_map/all_to_all | solution.py:281
  37.7 0.0 copy-start.3
  37.7 5.0 %all-to-all-start.3 = ((bf16[32,128,128]{2,1,0:T(8,128)(2,1)}), bf16[32,128,128]{2,1,0:T(8,128)(2,1)S(1)}, u32[]{:S(2)}, u32[]{:S(2)}) async-start(bf16[32,128,128]{2,1,0:T(8,128)(2,1)} %blocks.1), calls=%async_computation.3 | async-start | bytes 2097152 | tf_op jit(solution)/shard_map/all_to_all | solution.py:286
  42.7 0.0 reduce-scatter.2.cloned.1.call-start
  42.7 0.0 copy-done.3
  42.7 24.2 %dense.1.wt_ref = bf16[32,1024,128]{2,1,0:T(8,128)(2,1)} custom-call(bf16[32,80,128]{2,1,0:T(8,128)(2,1)} %copy-done.3), custom_call_target="tpu_custom_call" | custom-call | flops 24999999488 | bytes 1048576 | tf_op jit(solution)/shard_map/dense/pallas_call | solution.py:96
  66.9 0.0 all-to-all-done.3.c_ref
  66.9 0.0 copy-start
  66.9 1.0 copy-done
  67.9 12.7 %grads.1 = f32[8,4,256,128]{3,2,1,0:T(8,128)} custom-call(s32[1]{0:T(128)} %bitcast.z_ref, bf16[32,80,128]{2,1,0:T(8,128)(2,1)} %copy-done.3, bf16[32,128,128]{2,1,0:T(8,128)(2,1)} %copy-done, bf16[32,1024,128]{2,1,0:T(8,128)(2,1)} %dense.1.wt_ref), custom_call_target="tpu_custom_call" | custom-call | flops 15000000512 | bytes 1048576 | tf_op jit(solution)/shard_map/grads/pallas_call | solution.py:152
  80.6 0.0 reduce-scatter.2.cloned.1.call-update
  80.6 0.0 all-gather.3.cloned.1.call-done
  80.6 13.5 %bags.1 = (bf16[32,1024,128]{2,1,0:T(8,128)(2,1)}, bf16[32,128,128]{2,1,0:T(8,128)(2,1)}) custom-call(s32[1]{0:T(128)} %bitcast.z_ref, bf16[32,80,128]{2,1,0:T(8,128)(2,1)} %copy-done.3, bf16[32,1024,128]{2,1,0:T(8,128)(2,1)} %dense.1.wt_ref, bf16[8,4,256,128]{3,2,1,0:T(8,128)(2,1)} %bitcast.24), custom_call_target="tpu_custom_call" | custom-call | flops 17999998976 | bytes 1048576 | tf_op jit(solution)/shard_map/bags/pallas_call | solution.py:192
  94.1 7.4 %all-to-all-start.2 = ((bf16[32,128,128]{2,1,0:T(8,128)(2,1)}), bf16[32,128,128]{2,1,0:T(8,128)(2,1)S(1)}, u32[]{:S(2)}, u32[]{:S(2)}) async-start(bf16[32,128,128]{2,1,0:T(8,128)(2,1)} %get-tuple-element.7), calls=%async_computation.2 | async-start | bytes 2097152 | tf_op jit(solution)/shard_map/all_to_all | solution.py:290
  101.5 16.5 %scores.1 = f32[32,32,128]{2,1,0:T(8,128)} custom-call(bf16[32,80,128]{2,1,0:T(8,128)(2,1)} %copy-done.3, bf16[32,128,128]{2,1,0:T(8,128)(2,1)} %copy-done, bf16[32,1024,128]{2,1,0:T(8,128)(2,1)} %get-tuple-element.8.arrived_ref), custom_call_target="tpu_custom_call" | custom-call | flops 17999998976 | bytes 1048576 | tf_op jit(solution)/shard_map/scores/pallas_call | solution.py:241
  118.0 0.0 all-to-all-done.2.b_ref
  118.0 0.0 copy-start.1
  118.0 18.0 %all_to_all.30 = f32[32,32,128]{2,1,0:T(8,128)S(1)} all-to-all(f32[32,32,128]{2,1,0:T(8,128)} %scores.1), channel_id=1, replica_groups=mesh['dp'=8,'z'=8,'x'=4] {'dp','x'}, dimensions={0} | all-to-all | bytes 1048576 | tf_op jit(solution)/shard_map/all_to_all | solution.py:292
  136.0 2.8 %reduce-scatter.2.cloned.1.call-done = f32[1,4,256,128]{3,2,1,0:T(8,128)} async-done(((f32[8,4,256,128]{3,2,1,0:T(8,128)}), f32[1,4,256,128]{3,2,1,0:T(8,128)}) %reduce-scatter.2.cloned.1.call-update) | async-done | bytes 524304 | tf_op jit(solution)/shard_map/reduce_scatter | solution.py:293
  138.7 4.3 %all-to-all-start.5 = ((f32[4,256,128]{2,1,0:T(8,128)}), f32[4,256,128]{2,1,0:T(8,128)S(1)}, u32[]{:S(2)}, u32[]{:S(2)}) async-start(f32[4,256,128]{2,1,0:T(8,128)} %bitcast.22), calls=%async_computation.6 | async-start | bytes 1048576 | tf_op jit(solution)/shard_map/all_to_all | solution.py:294
  143.0 0.0 copy-done.1
  143.0 3.5 %rows.1 = bf16[128,4096]{1,0:T(8,128)(2,1)} custom-call(bf16[32,128,128]{2,1,0:T(8,128)(2,1)} %copy-done.1), custom_call_target="tpu_custom_call" | custom-call | flops 2000000000 | bytes 1048576 | tf_op jit(solution)/shard_map/rows/pallas_call | solution.py:265
  146.5 0.6 reduce_sum.9
  147.1 5.4 %all-to-all-done.5 = f32[4,256,128]{2,1,0:T(8,128)S(1)} async-done(((f32[4,256,128]{2,1,0:T(8,128)}), f32[4,256,128]{2,1,0:T(8,128)S(1)}, u32[]{:S(2)}, u32[]{:S(2)}) %all-to-all-start.5) | async-done | bytes 524320 | tf_op jit(solution)/shard_map/all_to_all | solution.py:294
  152.6 0.8 pad_maximum_fusion
  (1 shorter events, 0.0 us)
Async XLA Ops:
  8.9 11.0 %all-to-all-start.1 = ((bf16[4,256,128]{2,1,0:T(8,128)(2,1)}), bf16[4,256,128]{2,1,0:T(8,128)(2,1)S(1)}, u32[]{:S(2)}, u32[]{:S(2)}) async-start(bf16[4,256,128]{2,1,0:T(8,128)(2,1)} %pad_maximum_fusion.1), calls=%async_computation.1 | async-start | bytes 524288 | tf_op jit(solution)/shard_map/all_to_all | solution.py:284
  19.9 9.2 %copy-start.2 = (bf16[4,256,128]{2,1,0:T(8,128)(2,1)}, bf16[4,256,128]{2,1,0:T(8,128)(2,1)S(1)}, u32[]{:S(2)}) copy-start(bf16[4,256,128]{2,1,0:T(8,128)(2,1)S(1)} %all-to-all-done.1) | copy-start | bytes 786436
  19.9 17.8 %all-to-all-start = ((bf16[32,80,128]{2,1,0:T(8,128)(2,1)}), bf16[32,80,128]{2,1,0:T(8,128)(2,1)S(1)}, u32[]{:S(2)}, u32[]{:S(2)}) async-start(bf16[32,80,128]{2,1,0:T(8,128)(2,1)} %slots.1), calls=%async_computation | async-start | bytes 1310720 | tf_op jit(solution)/shard_map/all_to_all | solution.py:281
  25.5 55.1 %all-gather.3.cloned.1.call-start = ((), (), s32[]{:S(2)}) async-start(), calls=%async_computation.8 | async-start | bytes 2359296 | tf_op jit(solution)/shard_map/all_gather | solution.py:285
  37.7 5.0 %copy-start.3 = (bf16[32,80,128]{2,1,0:T(8,128)(2,1)}, bf16[32,80,128]{2,1,0:T(8,128)(2,1)S(1)}, u32[]{:S(2)}) copy-start(bf16[32,80,128]{2,1,0:T(8,128)(2,1)S(1)} %all-to-all-done.m_ref) | copy-start | bytes 1966084
  37.7 29.2 %all-to-all-start.3 = ((bf16[32,128,128]{2,1,0:T(8,128)(2,1)}), bf16[32,128,128]{2,1,0:T(8,128)(2,1)S(1)}, u32[]{:S(2)}, u32[]{:S(2)}) async-start(bf16[32,128,128]{2,1,0:T(8,128)(2,1)} %blocks.1), calls=%async_computation.3 | async-start | bytes 2097152 | tf_op jit(solution)/shard_map/all_to_all | solution.py:286
  42.7 96.1 %reduce-scatter.2.cloned.1.call-start = ((), (), s32[]{:S(2)}) async-start(), calls=%async_computation.7 | async-start | bytes 4718592 | tf_op jit(solution)/shard_map/reduce_scatter | solution.py:293
  66.9 1.0 copy-start
  94.1 23.9 %all-to-all-start.2 = ((bf16[32,128,128]{2,1,0:T(8,128)(2,1)}), bf16[32,128,128]{2,1,0:T(8,128)(2,1)S(1)}, u32[]{:S(2)}, u32[]{:S(2)}) async-start(bf16[32,128,128]{2,1,0:T(8,128)(2,1)} %get-tuple-element.7), calls=%async_computation.2 | async-start | bytes 2097152 | tf_op jit(solution)/shard_map/all_to_all | solution.py:290
  118.0 25.0 %copy-start.1 = (bf16[32,128,128]{2,1,0:T(8,128)(2,1)}, bf16[32,128,128]{2,1,0:T(8,128)(2,1)S(1)}, u32[]{:S(2)}) copy-start(bf16[32,128,128]{2,1,0:T(8,128)(2,1)S(1)} %all-to-all-done.2.b_ref) | copy-start | bytes 3145732
  138.7 13.8 %all-to-all-start.5 = ((f32[4,256,128]{2,1,0:T(8,128)}), f32[4,256,128]{2,1,0:T(8,128)S(1)}, u32[]{:S(2)}, u32[]{:S(2)}) async-start(f32[4,256,128]{2,1,0:T(8,128)} %bitcast.22), calls=%async_computation.6 | async-start | bytes 1048576 | tf_op jit(solution)/shard_map/all_to_all | solution.py:294
Sparse Core Ops, SparseCore 0:
  29.2 44.0 all-gather.2
  80.7 57.9 reduce-scatter.1

commit v3 on v2

--- a/solution.py
+++ b/solution.py
@@ -19,7 +19,9 @@
 POS = NZ * GRP
 M_C = TOPK
 M_T = 2 * TOPK
-M_ALL = M_T + 16
+M_V = M_T + 16
+PIECE = OWN // ND
+M_ALL = M_V + PIECE
 VMEM = 56 * 1024 * 1024
 
 
@@ -28,34 +30,53 @@
     return hi, (v - hi.astype(F32)).astype(BF)
 
 
-def slots_kernel(z_ref, w_ref, pos_ref, list_ref, out_ref):
-    z = z_ref[0]
+def slots_kernel(at_ref, w_ref, pos_ref, list_ref, v_ref, out_ref, wide):
+    z = at_ref[0]
     pos = pos_ref[...]
     plane = ((pos >> 7) - z) & (NZ - 1)
     code = (((pos & (GRP - 1)) + GRP) << plane).astype(F32).astype(BF)
-    rows = [list_ref[pl.ds((z + h) & (NZ - 1), 1), :] for h in range(NZ)]
+    lists = list_ref[0]
+    owner = lax.broadcasted_iota(jnp.int32, (NX * NZ, GRP), 0) & (NX - 1)
+    lane = lax.broadcasted_iota(jnp.int32, (NX * NZ, GRP), 1) // CAP
+    wide[...] = jnp.where(owner == lane, jnp.concatenate([lists] * NX, axis=1), 0)
+    rows = []
+    for h in range(NZ):
+        four = [wide[pl.ds(((z + h) & (NZ - 1)) * NX + i, 1), :] for i in range(NX)]
+        rows.append(four[0] + four[1] + four[2] + four[3])
     lists = jnp.concatenate(rows + rows, axis=0).astype(F32).astype(BF)
     w = w_ref[...]
     for i in range(NS):
         out_ref[i, 0:M_C, :] = w
         out_ref[i, M_C:M_T, :] = code
-        out_ref[i, M_T:M_ALL, :] = lists
+        out_ref[i, M_T:M_V, :] = lists
+        out_ref[i, M_V:M_ALL, :] = v_ref[:, i * CB:(i + 1) * CB]
 
 
 def cost(us):
     return pl.CostEstimate(flops=int(us * 1e9), bytes_accessed=2**20, transcendentals=0)
 
 
-def slots(z, w, pos, lists):
-    vm = pl.BlockSpec(memory_space=pltpu.VMEM)
+def slots(at, w, pos, lists, values):
+    spec = pltpu.PrefetchScalarGridSpec(
+        num_scalar_prefetch=1,
+        grid=(1,),
+        in_specs=[
+            pl.BlockSpec((TOPK, TOK), lambda i, at: (0, 0)),
+            pl.BlockSpec((TOPK, TOK), lambda i, at: (0, 0)),
+            pl.BlockSpec((1, NX * NZ, CAP), lambda i, at: (0, 0, 0)),
+            pl.BlockSpec((PIECE, NS * CB), lambda i, at: (at[1], 0)),
+        ],
+        out_specs=pl.BlockSpec((NS, M_ALL, TOK), lambda i, at: (0, 0, 0)),
+        scratch_shapes=[pltpu.VMEM((NX * NZ, GRP), jnp.int32)],
+    )
     return pl.pallas_call(
         slots_kernel,
-        in_specs=[pl.BlockSpec(memory_space=pltpu.SMEM), vm, vm, vm],
-        out_specs=vm,
+        grid_spec=spec,
         out_shape=jax.ShapeDtypeStruct((NS, M_ALL, TOK), BF),
+        compiler_params=pltpu.CompilerParams(vmem_limit_bytes=VMEM),
         cost_estimate=cost(2),
         name="slots",
-    )(z, w, pos, lists)
+    )(at, w, pos, lists, values)
 
 
 def blocks_kernel(cot_ref, out_ref):
@@ -96,7 +117,7 @@
     return pl.pallas_call(
         dense_kernel,
         grid=(NZ,),
-        in_specs=[pl.BlockSpec((NS, M_ALL, TOK), lambda h: (0, 0, 0))],
+        in_specs=[pl.BlockSpec((NS, M_T, TOK), lambda h: (0, 0, 0))],
         out_specs=pl.BlockSpec((NS, GRP, TOK), lambda h: (0, h, 0)),
         out_shape=jax.ShapeDtypeStruct((NS, POS, TOK), BF),
         compiler_params=pltpu.CompilerParams(vmem_limit_bytes=VMEM),
@@ -105,47 +126,51 @@
     )(m)
 
 
-def grads_kernel(z_ref, m_ref, c_ref, wt_ref, out_ref, parts, lists):
-    h = pl.program_id(0)
-
-    @pl.when(h == 0)
+def grads_kernel(at_ref, t_ref, c_ref, wt0_ref, wt1_ref, out_ref, parts, lists):
+    q = pl.program_id(0)
+
+    @pl.when(q == 0)
     def _():
         for e in range(NS):
-            lists[e * 16:(e + 1) * 16, :] = m_ref[e, M_T:M_ALL, :].astype(F32)
-
-    for e in range(NS):
-        hi, lo = split(jnp.dot(wt_ref[e], c_ref[e], preferred_element_type=F32))
-        for x in range(NX):
-            at = slice(e * CAP, (e + 1) * CAP)
-            parts[x, at, 0:CB] = hi[x * CAP:(x + 1) * CAP]
-            parts[x, at, CB:2 * CB] = lo[x * CAP:(x + 1) * CAP]
+            lists[e * 16:(e + 1) * 16, :] = t_ref[e].astype(F32)
+
     lane = lax.broadcasted_iota(jnp.int32, (8, GRP), 1) // CAP
     row = lax.broadcasted_iota(jnp.int32, (OWN, GRP), 0).astype(F32).astype(BF)
-    raw = [lists[pl.ds(q * 16 + h, 8, stride=64), :] for q in range(4)]
-    for x in range(NX):
-        rows = jnp.zeros((8, GRP), F32)
-        for q in range(4):
-            rows = jnp.where(lane == q, pltpu.roll(raw[q], ((q - x) % 4) * CAP, 1), rows)
-        rows = rows.astype(BF)
-        one, zero = jnp.ones((), BF), jnp.zeros((), BF)
-        hot = jnp.concatenate([jnp.where(row == rows[g:g + 1, :], one, zero) for g in range(8)], axis=1)
-        total = jnp.dot(hot, parts[x], preferred_element_type=F32)
-        out_ref[0, x] = total[:, :CB] + total[:, CB:]
-
-
-def grads(z, m, c, wt):
-    whole = lambda h, z: (0, 0, 0)
+    one, zero = jnp.ones((), BF), jnp.zeros((), BF)
+    for i, wt_ref in enumerate((wt0_ref, wt1_ref)):
+        h = (2 * q + i - at_ref[0]) & (NZ - 1)
+        for e in range(NS):
+            hi, lo = split(jnp.dot(wt_ref[e], c_ref[e], preferred_element_type=F32))
+            for x in range(NX):
+                at = slice(e * CAP, (e + 1) * CAP)
+                parts[i, x, at, 0:CB] = hi[x * CAP:(x + 1) * CAP]
+                parts[i, x, at, CB:2 * CB] = lo[x * CAP:(x + 1) * CAP]
+        raw = [lists[pl.ds(j * 16 + h, 8, stride=64), :] for j in range(4)]
+        for x in range(NX):
+            rows = jnp.zeros((8, GRP), F32)
+            for j in range(4):
+                rows = jnp.where(lane == j, pltpu.roll(raw[j], ((j - x) % 4) * CAP, 1), rows)
+            rows = rows.astype(BF)
+            hot = jnp.concatenate(
+                [jnp.where(row == rows[g:g + 1, :], one, zero) for g in range(8)], axis=1
+            )
+            total = jnp.dot(hot, parts[i, x], preferred_element_type=F32)
+            out_ref[i, x] = total[:, :CB] + total[:, CB:]
+
+
+def grads(at, m, c, wt):
     spec = pltpu.PrefetchScalarGridSpec(
         num_scalar_prefetch=1,
-        grid=(NZ,),
+        grid=(NZ // 2,),
         in_specs=[
-            pl.BlockSpec((NS, M_ALL, TOK), whole),
-            pl.BlockSpec((NS, TOK, CB), whole),
-            pl.BlockSpec((NS, GRP, TOK), lambda h, z: (0, h, 0)),
-        ],
-        out_specs=pl.BlockSpec((1, NX, OWN, CB), lambda h, z: ((z[0] + h) & (NZ - 1), 0, 0, 0)),
+            pl.BlockSpec((NS, 16, TOK), lambda q, at: (0, M_T // 16, 0)),
+            pl.BlockSpec((NS, TOK, CB), lambda q, at: (0, 0, 0)),
+            pl.BlockSpec((NS, GRP, TOK), lambda q, at: (0, (2 * q - at[0]) & (NZ - 1), 0)),
+            pl.BlockSpec((NS, GRP, TOK), lambda q, at: (0, (2 * q + 1 - at[0]) & (NZ - 1), 0)),
+        ],
+        out_specs=pl.BlockSpec((2, NX, OWN, CB), lambda q, at: (q, 0, 0, 0)),
         scratch_shapes=[
-            pltpu.VMEM((NX, NS * CAP, 2 * CB), BF),
+            pltpu.VMEM((2, NX, NS * CAP, 2 * CB), BF),
             pltpu.VMEM((NS * 16, GRP), F32),
         ],
     )
@@ -154,18 +179,18 @@
         grid_spec=spec,
         out_shape=jax.ShapeDtypeStruct((NZ, NX, OWN, CB), F32),
         compiler_params=pltpu.CompilerParams(vmem_limit_bytes=VMEM),
-        cost_estimate=cost(15),
+        cost_estimate=cost(12),
         name="grads",
-    )(z, m, c, wt)
+    )(at, m, c, wt, wt)
 
 
 EG = 8
 
 
-def bags_kernel(z_ref, m_ref, wt_ref, v_ref, arrived_ref, out_ref, hots, lists):
-    z = z_ref[0]
+def bags_kernel(at_ref, t_ref, wt_ref, v_ref, arrived_ref, out_ref, hots, lists):
+    z = at_ref[0]
     for e in range(EG):
-        lists[e * 16:(e + 1) * 16, :] = m_ref[e, M_T:M_ALL, :].astype(F32)
+        lists[e * 16:(e + 1) * 16, :] = t_ref[e].astype(F32)
     col = lax.broadcasted_iota(jnp.int32, (GRP, OWN), 1).astype(F32)
     for h in range(NZ):
         cols = lists[pl.ds(h, EG, stride=16), :].T
@@ -174,9 +199,10 @@
             for x in range(NX):
                 hots[x, e * CAP:(e + 1) * CAP, :] = hot[x * CAP:(x + 1) * CAP]
         for x in range(NX):
-            got = jnp.dot(
-                hots[x], v_ref[(z + h) & (NZ - 1), x], preferred_element_type=F32
-            ).astype(BF)
+            rows = jnp.concatenate(
+                [v_ref[(z + h) & (NZ - 1), d * NX + x] for d in range(ND)], axis=0
+            )
+            got = jnp.dot(hots[x], rows, preferred_element_type=F32).astype(BF)
             at = h * GRP + x * CAP
             for e in range(EG):
                 arrived_ref[e, at:at + CAP, :] = got[e * CAP:(e + 1) * CAP]
@@ -187,16 +213,16 @@
         out_ref[e] = bag.astype(BF)
 
 
-def bags(z, m, wt, v):
+def bags(at, m, wt, v):
     part = lambda g: (g, 0, 0)
     return pl.pallas_call(
         bags_kernel,
         grid=(NS // EG,),
         in_specs=[
             pl.BlockSpec(memory_space=pltpu.SMEM),
-            pl.BlockSpec((EG, M_ALL, TOK), part),
+            pl.BlockSpec((EG, 16, TOK), lambda g: (g, M_T // 16, 0)),
             pl.BlockSpec((EG, POS, TOK), part),
-            pl.BlockSpec((NZ, NX, OWN, CB), lambda g: (0, 0, 0, 0)),
+            pl.BlockSpec((NZ, NS, PIECE, CB), lambda g: (0, 0, 0, 0)),
         ],
         out_specs=[pl.BlockSpec((EG, POS, CB), part), pl.BlockSpec((EG, TOK, CB), part)],
         out_shape=[
@@ -210,7 +236,7 @@
         compiler_params=pltpu.CompilerParams(vmem_limit_bytes=VMEM),
         cost_estimate=cost(18),
         name="bags",
-    )(z, m, wt, v)
+    )(at, m, wt, v)
 
 
 def scores_kernel(m_ref, c_ref, arrived_ref, out_ref):
@@ -218,7 +244,7 @@
         scores = lax.dot_general(
             c_ref[e], arrived_ref[e], (((1,), (1,)), ((), ())), preferred_element_type=F32
         )
-        code = m_ref[e, M_C:M_T, :].astype(F32)
+        code = m_ref[e].astype(F32)
         code = jnp.concatenate([code] * (TOK // TOPK), axis=0).T.astype(jnp.int32)
         plane = jnp.zeros_like(code)
         for i in range(1, NZ):
@@ -242,7 +268,7 @@
         scores_kernel,
         grid=(NS // EG,),
         in_specs=[
-            pl.BlockSpec((EG, M_ALL, TOK), part),
+            pl.BlockSpec((EG, TOPK, TOK), lambda g: (g, 1, 0)),
             pl.BlockSpec((EG, TOK, CB), part),
             pl.BlockSpec((EG, POS, CB), part),
         ],
@@ -274,19 +300,16 @@
 
 
 def on_device(slot_weight, slot_pos, touched, values, cotangent):
-    z = lax.axis_index("z").astype(jnp.int32).reshape(1)
-    d = lax.axis_index("dp")
+    at = jnp.stack([lax.axis_index("z"), lax.axis_index("dp")]).astype(jnp.int32)
     plane = ("dp", "x")
-    m = slots(z, slot_weight.T, slot_pos.T, touched.reshape(NZ, GRP))
+    m = slots(at, slot_weight.T, slot_pos.T, touched, values)
     m = lax.all_to_all(m, plane, 0, 0, tiled=True)
-    mine = lax.dynamic_slice(values, (0, d * (NX * CB)), (OWN, NX * CB))
-    mine = jnp.stack([mine[:, i * CB:(i + 1) * CB] for i in range(NX)])
-    mine = lax.all_to_all(mine, "x", 0, 0, tiled=True)
-    v = lax.all_gather(mine, "z")
-    c = lax.all_to_all(blocks(cotangent), plane, 0, 0, tiled=True)
+    m, c = lax.optimization_barrier((m, blocks(cotangent)))
+    v = lax.all_gather(m[:, M_V:, :], "z")
+    c = lax.all_to_all(c, plane, 0, 0, tiled=True)
     wt = dense(m)
-    table = grads(z, m, c, wt)
-    arrived, b = bags(z, m, wt, v)
+    table = grads(at, m, c, wt)
+    arrived, b = bags(at, m, wt, v)
     b = lax.all_to_all(b, plane, 0, 0, tiled=True)
     b, g = lax.optimization_barrier((b, scores(m, c, arrived)))
     g = lax.all_to_all(g, plane, 0, 0, tiled=True)

time: 161 us -> 156 us (0.969)
  starting transfers between devices: 26.7 us -> 24.2 us
    all_to_all x2 -> x1, starting transfers between devices: 9.25 us -> 5 us  [on_device(): c = lax.all_to_all(c, plane, 0, 0, tiled=True)]
    all_to_all x2 -> x1, waiting for transfers between devices: 3.68 us -> 0.01 us  [on_device(): c = lax.all_to_all(c, plane, 0, 0, tiled=True)]
    all_to_all x1, waiting for transfers between devices: 8.64 us -> 11.4 us  [on_device(): m = lax.all_to_all(m, plane, 0, 0, tiled=True)]
    all_to_all x1, starting transfers between devices: 5.68 us -> 7.54 us  [on_device(): m = lax.all_to_all(m, plane, 0, 0, tiled=True)]
  transfers between devices with their start and end apart: 7 -> 6, of which waited for: 4 -> 3; matrix products, arithmetic and copies ran while one was open for 1% -> 0% of each run, Pallas kernels for 47% -> 47%
where the time goes in v3:
time: 156 us
  Pallas kernels  75.7 us (49%)
  starting transfers between devices  24.2 us (16%)
  waiting for transfers between devices  19.8 us (13%)
  blocking collectives  18 us (12%)
  between operations  14.1 us (9%)
  other arithmetic  2.09 us (1%)
  local copies, waits for them, and re-layouts  1.81 us (1%)
    pallas_call x1, Pallas kernels, dense(): pl.pallas_call(dense_kernel, grid=(NZ,), in_specs=[pl.BlockSpec((NS, M_T,...  24.1 us
    all_to_all x1, blocking collectives, on_device(): g = lax.all_to_all(g, plane, 0, 0, tiled=True)  18 us
    pallas_call x1, Pallas kernels, scores(): pl.pallas_call(scores_kernel, grid=(NS // EG,), in_specs=[pl.BlockSpec((E...  16.4 us
    pallas_call x1, Pallas kernels, bags(): pl.pallas_call(bags_kernel, grid=(NS // EG,), in_specs=[pl.BlockSpec(memo...  13.4 us
    pallas_call x1, Pallas kernels, grads(): pl.pallas_call(grads_kernel, grid_spec=spec, out_shape=jax.ShapeDtypeStru...  12.2 us
    all_to_all x1, waiting for transfers between devices, on_device(): m = lax.all_to_all(m, plane, 0, 0, tiled=True)  11.4 us
    all_to_all x1, starting transfers between devices, on_device(): m = lax.all_to_all(m, plane, 0, 0, tiled=True)  7.54 us
    all_to_all x1, starting transfers between devices, on_device(): b = lax.all_to_all(b, plane, 0, 0, tiled=True)  7.36 us
  transfers between devices with their start and end apart: 6, of which 3 were waited for; matrix products, arithmetic and copies ran while one was open for 0% of the time, Pallas kernels for 47%

profile of v3, /device:TPU:8, one launch (start us, length us, event | category | flops | bytes accessed | tf_op | source)
XLA Modules:
  0.0 155.6 jit_solution(11963842395588773868)
XLA Ops:
  7.2 0.6 pad_add_fusion.at_ref
  7.8 2.7 %slots.1 = bf16[32,112,128]{2,1,0:T(8,128)(2,1)} custom-call(s32[2]{0:T(128)} %pad_add_fusion.at_ref, bf16[32,128]{1,0:T(8,128)(2,1)} %bitcast.19, s32[32,128]{1,0:T(8,128)} %bitcast.18, s32[1,32,32]{2,1,0:T(8,128)} %list_ref.1, bf16[256,4096]{1,0:T(8,128)(2,1)} %v_ref.1), custom_call_target="tpu_custom_call" | custom-call | flops 2000000000 | bytes 1048576 | tf_op jit(solution)/shard_map/slots/pallas_call | solution.py:72
  10.5 7.5 %all-to-all-start = ((bf16[32,112,128]{2,1,0:T(8,128)(2,1)}), bf16[32,112,128]{2,1,0:T(8,128)(2,1)S(1)}, u32[]{:S(2)}, u32[]{:S(2)}) async-start(bf16[32,112,128]{2,1,0:T(8,128)(2,1)} %slots.1), calls=%async_computation | async-start | bytes 1835008 | tf_op jit(solution)/shard_map/all_to_all | solution.py:306
  18.0 0.0 all-gather.3.cloned.1.call-start
  18.1 3.4 %blocks.1 = bf16[32,128,128]{2,1,0:T(8,128)(2,1)} custom-call(bf16[128,4096]{1,0:T(8,128)(2,1)} %cot_ref.1), custom_call_target="tpu_custom_call" | custom-call | flops 2000000000 | bytes 1048576 | tf_op jit(solution)/shard_map/blocks/pallas_call | solution.py:89
  21.5 11.4 %all-to-all-done.m_ref.t_ref = bf16[32,112,128]{2,1,0:T(8,128)(2,1)S(1)} async-done(((bf16[32,112,128]{2,1,0:T(8,128)(2,1)}), bf16[32,112,128]{2,1,0:T(8,128)(2,1)S(1)}, u32[]{:S(2)}, u32[]{:S(2)}) %all-to-all-start) | async-done | bytes 917536 | tf_op jit(solution)/shard_map/all_to_all | solution.py:306
  32.9 0.0 copy-start
  32.9 0.8 slice.15
  33.6 0.0 all-gather.3.cloned.1.call-update
  33.7 5.0 %all-to-all-start.2 = ((bf16[32,128,128]{2,1,0:T(8,128)(2,1)}), bf16[32,128,128]{2,1,0:T(8,128)(2,1)S(1)}, u32[]{:S(2)}, u32[]{:S(2)}) async-start(bf16[32,128,128]{2,1,0:T(8,128)(2,1)} %blocks.1), calls=%async_computation.2 | async-start | bytes 2097152 | tf_op jit(solution)/shard_map/all_to_all | solution.py:309
  38.7 0.0 reduce-scatter.2.cloned.1.call-start
  38.7 0.0 copy-done
  38.7 24.1 %dense.1.wt_ref.wt0_ref.wt1_ref = bf16[32,1024,128]{2,1,0:T(8,128)(2,1)} custom-call(bf16[32,112,128]{2,1,0:T(8,128)(2,1)} %copy-done), custom_call_target="tpu_custom_call" | custom-call | flops 24999999488 | bytes 1048576 | tf_op jit(solution)/shard_map/dense/pallas_call | solution.py:117
  62.8 0.0 all-to-all-done.2.c_ref
  62.8 0.0 copy-start.1
  62.8 1.0 copy-done.1
  63.8 12.2 %grads.1 = f32[8,4,256,128]{3,2,1,0:T(8,128)} custom-call(s32[2]{0:T(128)} %pad_add_fusion.at_ref, bf16[32,112,128]{2,1,0:T(8,128)(2,1)} %copy-done, bf16[32,128,128]{2,1,0:T(8,128)(2,1)} %copy-done.1, bf16[32,1024,128]{2,1,0:T(8,128)(2,1)} %dense.1.wt_ref.wt0_ref.wt1_ref, bf16[32,1024,128]{2,1,0:T(8,128)(2,1)} %dense.1.wt_ref.wt0_ref.wt1_ref), custom_call_target="tpu_custom_call" | custom-call | flops 12000000000 | bytes 1048576 | tf_op jit(solution)/shard_map/grads/pallas_call | solution.py:177
  76.0 0.0 reduce-scatter.2.cloned.1.call-update
  76.0 0.0 all-gather.3.cloned.1.call-done
  76.0 13.4 %bags.1 = (bf16[32,1024,128]{2,1,0:T(8,128)(2,1)}, bf16[32,128,128]{2,1,0:T(8,128)(2,1)}) custom-call(s32[2]{0:T(128)} %pad_add_fusion.at_ref, bf16[32,112,128]{2,1,0:T(8,128)(2,1)} %copy-done, bf16[32,1024,128]{2,1,0:T(8,128)(2,1)} %dense.1.wt_ref.wt0_ref.wt1_ref, bf16[8,32,32,128]{3,2,1,0:T(8,128)(2,1)} %bitcast.17), custom_call_target="tpu_custom_call" | custom-call | flops 17999998976 | bytes 1048576 | tf_op jit(solution)/shard_map/bags/pallas_call | solution.py:218
  89.5 7.4 %all-to-all-start.1 = ((bf16[32,128,128]{2,1,0:T(8,128)(2,1)}), bf16[32,128,128]{2,1,0:T(8,128)(2,1)S(1)}, u32[]{:S(2)}, u32[]{:S(2)}) async-start(bf16[32,128,128]{2,1,0:T(8,128)(2,1)} %get-tuple-element.10), calls=%async_computation.1 | async-start | bytes 2097152 | tf_op jit(solution)/shard_map/all_to_all | solution.py:313
  96.8 16.4 %scores.1 = f32[32,32,128]{2,1,0:T(8,128)} custom-call(bf16[32,112,128]{2,1,0:T(8,128)(2,1)} %copy-done, bf16[32,128,128]{2,1,0:T(8,128)(2,1)} %copy-done.1, bf16[32,1024,128]{2,1,0:T(8,128)(2,1)} %get-tuple-element.12.arrived_ref), custom_call_target="tpu_custom_call" | custom-call | flops 17999998976 | bytes 1048576 | tf_op jit(solution)/shard_map/scores/pallas_call | solution.py:267
  113.2 0.0 all-to-all-done.1.b_ref
  113.2 0.0 copy-start.2
  113.2 18.0 %all_to_all.25 = f32[32,32,128]{2,1,0:T(8,128)S(1)} all-to-all(f32[32,32,128]{2,1,0:T(8,128)} %scores.1), channel_id=1, replica_groups=mesh['dp'=8,'z'=8,'x'=4] {'dp','x'}, dimensions={0} | all-to-all | bytes 1048576 | tf_op jit(solution)/shard_map/all_to_all | solution.py:315
  131.2 2.9 %reduce-scatter.2.cloned.1.call-done = f32[1,4,256,128]{3,2,1,0:T(8,128)} async-done(((f32[8,4,256,128]{3,2,1,0:T(8,128)}), f32[1,4,256,128]{3,2,1,0:T(8,128)}) %reduce-scatter.2.cloned.1.call-update) | async-done | bytes 524304 | tf_op jit(solution)/shard_map/reduce_scatter | solution.py:316
  134.2 4.3 %all-to-all-start.4 = ((f32[4,256,128]{2,1,0:T(8,128)}), f32[4,256,128]{2,1,0:T(8,128)S(1)}, u32[]{:S(2)}, u32[]{:S(2)}) async-start(f32[4,256,128]{2,1,0:T(8,128)} %bitcast.15), calls=%async_computation.5 | async-start | bytes 1048576 | tf_op jit(solution)/shard_map/all_to_all | solution.py:317
  138.4 0.0 copy-done.2
  138.4 3.5 %rows.1 = bf16[128,4096]{1,0:T(8,128)(2,1)} custom-call(bf16[32,128,128]{2,1,0:T(8,128)(2,1)} %copy-done.2), custom_call_target="tpu_custom_call" | custom-call | flops 2000000000 | bytes 1048576 | tf_op jit(solution)/shard_map/rows/pallas_call | solution.py:291
  141.9 0.6 reduce_sum.9
  142.5 5.4 %all-to-all-done.4 = f32[4,256,128]{2,1,0:T(8,128)S(1)} async-done(((f32[4,256,128]{2,1,0:T(8,128)}), f32[4,256,128]{2,1,0:T(8,128)S(1)}, u32[]{:S(2)}, u32[]{:S(2)}) %all-to-all-start.4) | async-done | bytes 524320 | tf_op jit(solution)/shard_map/all_to_all | solution.py:317
  148.0 0.8 pad_maximum_fusion
  (1 shorter events, 0.0 us)
Async XLA Ops:
  10.5 22.4 %all-to-all-start = ((bf16[32,112,128]{2,1,0:T(8,128)(2,1)}), bf16[32,112,128]{2,1,0:T(8,128)(2,1)S(1)}, u32[]{:S(2)}, u32[]{:S(2)}) async-start(bf16[32,112,128]{2,1,0:T(8,128)(2,1)} %slots.1), calls=%async_computation | async-start | bytes 1835008 | tf_op jit(solution)/shard_map/all_to_all | solution.py:306
  18.0 58.0 %all-gather.3.cloned.1.call-start = ((), (), s32[]{:S(2)}) async-start(), calls=%async_computation.7 | async-start | bytes 2359296 | tf_op jit(solution)/shard_map/all_gather | solution.py:308
  32.9 5.9 %copy-start = (bf16[32,112,128]{2,1,0:T(8,128)(2,1)}, bf16[32,112,128]{2,1,0:T(8,128)(2,1)S(1)}, u32[]{:S(2)}) copy-start(bf16[32,112,128]{2,1,0:T(8,128)(2,1)S(1)} %all-to-all-done.m_ref.t_ref) | copy-start | bytes 2752516
  33.7 29.2 %all-to-all-start.2 = ((bf16[32,128,128]{2,1,0:T(8,128)(2,1)}), bf16[32,128,128]{2,1,0:T(8,128)(2,1)S(1)}, u32[]{:S(2)}, u32[]{:S(2)}) async-start(bf16[32,128,128]{2,1,0:T(8,128)(2,1)} %blocks.1), calls=%async_computation.2 | async-start | bytes 2097152 | tf_op jit(solution)/shard_map/all_to_all | solution.py:309
  38.7 95.5 %reduce-scatter.2.cloned.1.call-start = ((), (), s32[]{:S(2)}) async-start(), calls=%async_computation.6 | async-start | bytes 4718592 | tf_op jit(solution)/shard_map/reduce_scatter | solution.py:316
  62.8 1.0 copy-start.1
  89.5 23.8 %all-to-all-start.1 = ((bf16[32,128,128]{2,1,0:T(8,128)(2,1)}), bf16[32,128,128]{2,1,0:T(8,128)(2,1)S(1)}, u32[]{:S(2)}, u32[]{:S(2)}) async-start(bf16[32,128,128]{2,1,0:T(8,128)(2,1)} %get-tuple-element.10), calls=%async_computation.1 | async-start | bytes 2097152 | tf_op jit(solution)/shard_map/all_to_all | solution.py:313
  113.2 25.2 %copy-start.2 = (bf16[32,128,128]{2,1,0:T(8,128)(2,1)}, bf16[32,128,128]{2,1,0:T(8,128)(2,1)S(1)}, u32[]{:S(2)}) copy-start(bf16[32,128,128]{2,1,0:T(8,128)(2,1)S(1)} %all-to-all-done.1.b_ref) | copy-start | bytes 3145732
  134.2 13.8 %all-to-all-start.4 = ((f32[4,256,128]{2,1,0:T(8,128)}), f32[4,256,128]{2,1,0:T(8,128)S(1)}, u32[]{:S(2)}, u32[]{:S(2)}) async-start(f32[4,256,128]{2,1,0:T(8,128)} %bitcast.15), calls=%async_computation.5 | async-start | bytes 1048576 | tf_op jit(solution)/shard_map/all_to_all | solution.py:317
Sparse Core Ops, SparseCore 0:
  33.8 41.6 all-gather.2
  78.0 56.0 reduce-scatter.1

commit v4 on v3

--- a/solution.py
+++ b/solution.py
@@ -19,10 +19,8 @@
 POS = NZ * GRP
 M_C = TOPK
 M_T = 2 * TOPK
-M_V = M_T + 16
-PIECE = OWN // ND
-M_ALL = M_V + PIECE
-VMEM = 56 * 1024 * 1024
+M_ALL = M_T + 16
+MIB = 1024 * 1024
 
 
 def split(v):
@@ -30,7 +28,7 @@
     return hi, (v - hi.astype(F32)).astype(BF)
 
 
-def slots_kernel(at_ref, w_ref, pos_ref, list_ref, v_ref, out_ref, wide):
+def slots_kernel(at_ref, w_ref, pos_ref, list_ref, out_ref, wide):
     z = at_ref[0]
     pos = pos_ref[...]
     plane = ((pos >> 7) - z) & (NZ - 1)
@@ -48,15 +46,14 @@
     for i in range(NS):
         out_ref[i, 0:M_C, :] = w
         out_ref[i, M_C:M_T, :] = code
-        out_ref[i, M_T:M_V, :] = lists
-        out_ref[i, M_V:M_ALL, :] = v_ref[:, i * CB:(i + 1) * CB]
+        out_ref[i, M_T:M_ALL, :] = lists
 
 
 def cost(us):
     return pl.CostEstimate(flops=int(us * 1e9), bytes_accessed=2**20, transcendentals=0)
 
 
-def slots(at, w, pos, lists, values):
+def slots(at, w, pos, lists):
     spec = pltpu.PrefetchScalarGridSpec(
         num_scalar_prefetch=1,
         grid=(1,),
@@ -64,7 +61,6 @@
             pl.BlockSpec((TOPK, TOK), lambda i, at: (0, 0)),
             pl.BlockSpec((TOPK, TOK), lambda i, at: (0, 0)),
             pl.BlockSpec((1, NX * NZ, CAP), lambda i, at: (0, 0, 0)),
-            pl.BlockSpec((PIECE, NS * CB), lambda i, at: (at[1], 0)),
         ],
         out_specs=pl.BlockSpec((NS, M_ALL, TOK), lambda i, at: (0, 0, 0)),
         scratch_shapes=[pltpu.VMEM((NX * NZ, GRP), jnp.int32)],
@@ -73,10 +69,10 @@
         slots_kernel,
         grid_spec=spec,
         out_shape=jax.ShapeDtypeStruct((NS, M_ALL, TOK), BF),
-        compiler_params=pltpu.CompilerParams(vmem_limit_bytes=VMEM),
+        compiler_params=pltpu.CompilerParams(vmem_limit_bytes=56 * MIB),
         cost_estimate=cost(2),
         name="slots",
-    )(at, w, pos, lists, values)
+    )(at, w, pos, lists)
 
 
 def blocks_kernel(cot_ref, out_ref):
@@ -99,15 +95,24 @@
 
 def dense_kernel(m_ref, wt_ref):
     sub = lax.broadcasted_iota(jnp.int32, (GRP, TOK), 0)
-    codes = ((sub + GRP) << pl.program_id(0)).astype(F32).astype(BF)
+    codes = ((sub + GRP) << (2 * pl.program_id(0))).astype(F32).astype(BF)
+    tile = 16
+    tiles = [codes[i:i + tile] for i in range(0, GRP, tile)]
 
     def one(e, carry):
-        acc = jnp.zeros((GRP, TOK), BF)
+        accs = [[jnp.zeros((tile, TOK), BF) for _ in tiles] for _ in range(2)]
         we = m_ref[e, 0:M_C, :]
         ce = m_ref[e, M_C:M_T, :]
         for k in range(TOPK):
-            acc = jnp.where(codes == ce[k:k + 1, :], we[k:k + 1, :], acc)
-        wt_ref[e] = acc
+            w = jnp.broadcast_to(we[k:k + 1, :], (tile, TOK))
+            at = jnp.broadcast_to(ce[k:k + 1, :], (tile, TOK))
+            for acc in accs:
+                for i, t in enumerate(tiles):
+                    acc[i] = jnp.where(t == at, w, acc[i])
+                at = at * jnp.asarray(0.5, BF)
+        for j, acc in enumerate(accs):
+            for i, t in enumerate(acc):
+                wt_ref[e, j * GRP + i * tile:j * GRP + (i + 1) * tile, :] = t
         return carry
 
     lax.fori_loop(0, NS, one, 0, unroll=4)
@@ -116,11 +121,11 @@
 def dense(m):
     return pl.pallas_call(
         dense_kernel,
-        grid=(NZ,),
+        grid=(NZ // 2,),
         in_specs=[pl.BlockSpec((NS, M_T, TOK), lambda h: (0, 0, 0))],
-        out_specs=pl.BlockSpec((NS, GRP, TOK), lambda h: (0, h, 0)),
+        out_specs=pl.BlockSpec((NS, 2 * GRP, TOK), lambda h: (0, h, 0)),
         out_shape=jax.ShapeDtypeStruct((NS, POS, TOK), BF),
-        compiler_params=pltpu.CompilerParams(vmem_limit_bytes=VMEM),
+        compiler_params=pltpu.CompilerParams(vmem_limit_bytes=56 * MIB),
         cost_estimate=cost(25),
         name="dense",
     )(m)
@@ -178,7 +183,7 @@
         grads_kernel,
         grid_spec=spec,
         out_shape=jax.ShapeDtypeStruct((NZ, NX, OWN, CB), F32),
-        compiler_params=pltpu.CompilerParams(vmem_limit_bytes=VMEM),
+        compiler_params=pltpu.CompilerParams(vmem_limit_bytes=56 * MIB),
         cost_estimate=cost(12),
         name="grads",
     )(at, m, c, wt, wt)
@@ -199,9 +204,7 @@
             for x in range(NX):
                 hots[x, e * CAP:(e + 1) * CAP, :] = hot[x * CAP:(x + 1) * CAP]
         for x in range(NX):
-            rows = jnp.concatenate(
-                [v_ref[(z + h) & (NZ - 1), d * NX + x] for d in range(ND)], axis=0
-            )
+            rows = v_ref[(z + h) & (NZ - 1), (x - at_ref[1]) & (NX - 1)]
             got = jnp.dot(hots[x], rows, preferred_element_type=F32).astype(BF)
             at = h * GRP + x * CAP
             for e in range(EG):
@@ -222,7 +225,7 @@
             pl.BlockSpec(memory_space=pltpu.SMEM),
             pl.BlockSpec((EG, 16, TOK), lambda g: (g, M_T // 16, 0)),
             pl.BlockSpec((EG, POS, TOK), part),
-            pl.BlockSpec((NZ, NS, PIECE, CB), lambda g: (0, 0, 0, 0)),
+            pl.BlockSpec((NZ, NX, OWN, CB), lambda g: (0, 0, 0, 0)),
         ],
         out_specs=[pl.BlockSpec((EG, POS, CB), part), pl.BlockSpec((EG, TOK, CB), part)],
         out_shape=[
@@ -233,7 +236,7 @@
             pltpu.VMEM((NX, EG * CAP, OWN), BF),
             pltpu.VMEM((EG * 16, GRP), F32),
         ],
-        compiler_params=pltpu.CompilerParams(vmem_limit_bytes=VMEM),
+        compiler_params=pltpu.CompilerParams(vmem_limit_bytes=56 * MIB),
         cost_estimate=cost(18),
         name="bags",
     )(at, m, wt, v)
@@ -259,7 +262,7 @@
         out_ref[e] = acc.T[0:TOPK, :]
         return carry
 
-    lax.fori_loop(0, EG, one, 0, unroll=2)
+    lax.fori_loop(0, EG, one, 0, unroll=8)
 
 
 def scores(m, c, arrived):
@@ -274,7 +277,7 @@
         ],
         out_specs=pl.BlockSpec((EG, TOPK, TOK), part),
         out_shape=jax.ShapeDtypeStruct((NS, TOPK, TOK), F32),
-        compiler_params=pltpu.CompilerParams(vmem_limit_bytes=VMEM),
+        compiler_params=pltpu.CompilerParams(vmem_limit_bytes=56 * MIB),
         cost_estimate=cost(18),
         name="scores",
     )(m, c, arrived)
@@ -300,12 +303,21 @@
 
 
 def on_device(slot_weight, slot_pos, touched, values, cotangent):
-    at = jnp.stack([lax.axis_index("z"), lax.axis_index("dp")]).astype(jnp.int32)
+    x = lax.axis_index("x").astype(jnp.int32)
+    d = lax.axis_index("dp").astype(jnp.int32)
+    at = jnp.stack([lax.axis_index("z").astype(jnp.int32), x])
     plane = ("dp", "x")
-    m = slots(at, slot_weight.T, slot_pos.T, touched, values)
+    m = slots(at, slot_weight.T, slot_pos.T, touched)
+    m, values, cotangent = lax.optimization_barrier((m, values, cotangent))
     m = lax.all_to_all(m, plane, 0, 0, tiled=True)
-    m, c = lax.optimization_barrier((m, blocks(cotangent)))
-    v = lax.all_gather(m[:, M_V:, :], "z")
+    mine = []
+    for i in range(NX):
+        to = (x - i) & (NX - 1)
+        part = lax.dynamic_slice(values, (0, (d * NX + to) * CB), (OWN, CB))
+        mine.append(lax.ppermute(part, "x", [(j, (j - i) % NX) for j in range(NX)]) if i else part)
+    mine = jnp.stack(mine)
+    m, c, _ = lax.optimization_barrier((m, blocks(cotangent), mine))
+    v = lax.all_gather(mine, "z")
     c = lax.all_to_all(c, plane, 0, 0, tiled=True)
     wt = dense(m)
     table = grads(at, m, c, wt)

time: 156 us -> 158 us (1.013)
  starting transfers between devices: 24.2 us -> 30.5 us
  waiting for transfers between devices: 19.8 us -> 16.9 us
  Pallas kernels: 75.7 us -> 73.3 us
    all_to_all x1, waiting for transfers between devices: 11.4 us -> 0.01 us  [on_device(): m = lax.all_to_all(m, plane, 0, 0, tiled=True)]
    ppermute x0 -> x3, waiting for transfers between devices: none -> 7.18 us  [on_device(): lax.ppermute(part, 'x', [(j, (j - i) % NX) for j in range(NX)])]
    ppermute x0 -> x3, starting transfers between devices: none -> 5.68 us  [on_device(): lax.ppermute(part, 'x', [(j, (j - i) % NX) for j in range(NX)])]
  transfers between devices with their start and end apart: 6 -> 9, of which waited for: 3 -> 5; matrix products, arithmetic and copies ran while one was open for 0% -> 2% of each run, Pallas kernels for 47% -> 45%
where the time goes in v4:
time: 158 us; the launch traced here: 157 us
  Pallas kernels  73.3 us (46%)
  starting transfers between devices  30.5 us (19%)
  blocking collectives  17.4 us (11%)
  waiting for transfers between devices  16.9 us (11%)
  between operations  14.1 us (9%)
  other arithmetic  2.88 us (2%)
  local copies, waits for them, and re-layouts  2.01 us (1%)
    pallas_call x1, Pallas kernels, dense(): pl.pallas_call(dense_kernel, grid=(NZ // 2,), in_specs=[pl.BlockSpec((NS,...  22.8 us
    all_to_all x1, blocking collectives, on_device(): g = lax.all_to_all(g, plane, 0, 0, tiled=True)  17.4 us
    pallas_call x1, Pallas kernels, scores(): pl.pallas_call(scores_kernel, grid=(NS // EG,), in_specs=[pl.BlockSpec((E...  15.6 us
    pallas_call x1, Pallas kernels, bags(): pl.pallas_call(bags_kernel, grid=(NS // EG,), in_specs=[pl.BlockSpec(memo...  13.4 us
    pallas_call x1, Pallas kernels, grads(): pl.pallas_call(grads_kernel, grid_spec=spec, out_shape=jax.ShapeDtypeStru...  12.2 us
    all_to_all x1, starting transfers between devices, on_device(): m = lax.all_to_all(m, plane, 0, 0, tiled=True)  7.54 us
    all_to_all x1, starting transfers between devices, on_device(): b = lax.all_to_all(b, plane, 0, 0, tiled=True)  7.38 us
    ppermute x3, waiting for transfers between devices, on_device(): lax.ppermute(part, 'x', [(j, (j - i) % NX) for j in range(NX)])  7.18 us
  transfers between devices with their start and end apart: 9, of which 5 were waited for; matrix products, arithmetic and copies ran while one was open for 2% of the time, Pallas kernels for 45%

profile of v4, /device:TPU:8, one launch (start us, length us, event | category | flops | bytes accessed | tf_op | source)
XLA Modules:
  0.0 157.1 jit_solution(1223930655587951008)
XLA Ops:
  7.2 0.7 pad_add_fusion.at_ref
  7.8 2.4 %slots.1 = bf16[32,80,128]{2,1,0:T(8,128)(2,1)} custom-call(s32[2]{0:T(128)} %pad_add_fusion.at_ref, bf16[32,128]{1,0:T(8,128)(2,1)} %bitcast.27, s32[32,128]{1,0:T(8,128)} %bitcast.26, s32[1,32,32]{2,1,0:T(8,128)} %list_ref.1), custom_call_target="tpu_custom_call" | custom-call | flops 2000000000 | bytes 1048576 | tf_op jit(solution)/shard_map/slots/pallas_call | solution.py:68
  10.2 7.5 %all-to-all-start = ((bf16[32,80,128]{2,1,0:T(8,128)(2,1)}), bf16[32,80,128]{2,1,0:T(8,128)(2,1)S(1)}, u32[]{:S(2)}, u32[]{:S(2)}) async-start(bf16[32,80,128]{2,1,0:T(8,128)(2,1)} %slots.1), calls=%async_computation | async-start | bytes 1310720 | tf_op jit(solution)/shard_map/all_to_all | solution.py:312
  17.7 0.0 all-gather.3.cloned.1.call-start
  17.8 1.0 dynamic-slice_bitcast_fusion
  18.8 1.5 collective-permute-start.2
  20.3 2.7 %collective-permute-start.1 = (bf16[256,128]{1,0:T(8,128)(2,1)S(1)}, bf16[256,128]{1,0:T(8,128)(2,1)S(1)}, u32[]{:S(2)}, u32[]{:S(2)}) collective-permute-start(bf16[256,128]{1,0:T(8,128)(2,1)S(1)} %get-tuple-element.23), channel_id=1, source_target_pairs={{0,2},{1,3},{2,0},{3,1},{4,6},{5,7},{6,4},{7,5},{8,10},{9,11},{10,... | collective-permute-start | bytes 196616 | tf_op jit(solution)/shard_map/ppermute | solution.py:317
  23.0 1.5 collective-permute-start
  24.4 5.7 %collective-permute-done.2 = bf16[256,128]{1,0:T(8,128)(2,1)S(1)} collective-permute-done((bf16[256,128]{1,0:T(8,128)(2,1)S(1)}, bf16[256,128]{1,0:T(8,128)(2,1)S(1)}, u32[]{:S(2)}, u32[]{:S(2)}) %collective-permute-start.2) | collective-permute-done | bytes 65568 | tf_op jit(solution)/shard_map/ppermute | solution.py:317
  30.1 1.5 collective-permute-done.1
  31.6 0.0 collective-permute-done
  31.6 0.7 pad_maximum_fusion.1
  32.4 0.0 all-gather.3.cloned.1.call-update
  32.4 3.4 %blocks.1 = bf16[32,128,128]{2,1,0:T(8,128)(2,1)} custom-call(bf16[128,4096]{1,0:T(8,128)(2,1)} %cot_ref), custom_call_target="tpu_custom_call" | custom-call | flops 2000000000 | bytes 1048576 | tf_op jit(solution)/shard_map/blocks/pallas_call | solution.py:85
  35.8 0.0 all-to-all-done.m_ref.t_ref
  35.8 0.0 copy-start.2
  35.8 5.6 %all-to-all-start.2 = ((bf16[32,128,128]{2,1,0:T(8,128)(2,1)}), bf16[32,128,128]{2,1,0:T(8,128)(2,1)S(1)}, u32[]{:S(2)}, u32[]{:S(2)}) async-start(bf16[32,128,128]{2,1,0:T(8,128)(2,1)} %blocks.1), calls=%async_computation.2 | async-start | bytes 2097152 | tf_op jit(solution)/shard_map/all_to_all | solution.py:321
  41.4 0.0 reduce-scatter.2.cloned.1.call-start
  41.5 0.0 copy-done.2
  41.5 22.8 %dense.1.wt_ref.wt0_ref.wt1_ref = bf16[32,1024,128]{2,1,0:T(8,128)(2,1)} custom-call(bf16[32,80,128]{2,1,0:T(8,128)(2,1)} %copy-done.2), custom_call_target="tpu_custom_call" | custom-call | flops 24999999488 | bytes 1048576 | tf_op jit(solution)/shard_map/dense/pallas_call | solution.py:122
  64.3 0.0 all-to-all-done.2.c_ref
  64.3 0.0 copy-start
  64.3 1.0 copy-done
  65.3 12.2 %grads.1 = f32[8,4,256,128]{3,2,1,0:T(8,128)} custom-call(s32[2]{0:T(128)} %pad_add_fusion.at_ref, bf16[32,80,128]{2,1,0:T(8,128)(2,1)} %copy-done.2, bf16[32,128,128]{2,1,0:T(8,128)(2,1)} %copy-done, bf16[32,1024,128]{2,1,0:T(8,128)(2,1)} %dense.1.wt_ref.wt0_ref.wt1_ref, bf16[32,1024,128]{2,1,0:T(8,128)(2,1)} %dense.1.wt_ref.wt0_ref.wt1_ref), custom_call_target="tpu_custom_call" | custom-call | flops 12000000000 | bytes 1048576 | tf_op jit(solution)/shard_map/grads/pallas_call | solution.py:182
  77.5 0.0 reduce-scatter.2.cloned.1.call-update
  77.5 0.0 all-gather.3.cloned.1.call-done
  77.5 13.4 %bags.1 = (bf16[32,1024,128]{2,1,0:T(8,128)(2,1)}, bf16[32,128,128]{2,1,0:T(8,128)(2,1)}) custom-call(s32[2]{0:T(128)} %pad_add_fusion.at_ref, bf16[32,80,128]{2,1,0:T(8,128)(2,1)} %copy-done.2, bf16[32,1024,128]{2,1,0:T(8,128)(2,1)} %dense.1.wt_ref.wt0_ref.wt1_ref, bf16[8,4,256,128]{3,2,1,0:T(8,128)(2,1)} %bitcast.25), custom_call_target="tpu_custom_call" | custom-call | flops 17999998976 | bytes 1048576 | tf_op jit(solution)/shard_map/bags/pallas_call | solution.py:221
  90.9 7.4 %all-to-all-start.1 = ((bf16[32,128,128]{2,1,0:T(8,128)(2,1)}), bf16[32,128,128]{2,1,0:T(8,128)(2,1)S(1)}, u32[]{:S(2)}, u32[]{:S(2)}) async-start(bf16[32,128,128]{2,1,0:T(8,128)(2,1)} %get-tuple-element.16), calls=%async_computation.1 | async-start | bytes 2097152 | tf_op jit(solution)/shard_map/all_to_all | solution.py:325
  98.3 15.6 %scores.1 = f32[32,32,128]{2,1,0:T(8,128)} custom-call(bf16[32,80,128]{2,1,0:T(8,128)(2,1)} %copy-done.2, bf16[32,128,128]{2,1,0:T(8,128)(2,1)} %copy-done, bf16[32,1024,128]{2,1,0:T(8,128)(2,1)} %get-tuple-element.18.arrived_ref), custom_call_target="tpu_custom_call" | custom-call | flops 17999998976 | bytes 1048576 | tf_op jit(solution)/shard_map/scores/pallas_call | solution.py:270
  113.9 0.6 all-to-all-done.1.b_ref
  114.5 0.0 copy-start.1
  114.5 17.4 %all_to_all.25 = f32[32,32,128]{2,1,0:T(8,128)S(1)} all-to-all(f32[32,32,128]{2,1,0:T(8,128)} %scores.1), channel_id=1, replica_groups=mesh['dp'=8,'z'=8,'x'=4] {'dp','x'}, dimensions={0} | all-to-all | bytes 1048576 | tf_op jit(solution)/shard_map/all_to_all | solution.py:327
  132.0 3.7 %reduce-scatter.2.cloned.1.call-done = f32[1,4,256,128]{3,2,1,0:T(8,128)} async-done(((f32[8,4,256,128]{3,2,1,0:T(8,128)}), f32[1,4,256,128]{3,2,1,0:T(8,128)}) %reduce-scatter.2.cloned.1.call-update) | async-done | bytes 524304 | tf_op jit(solution)/shard_map/reduce_scatter | solution.py:328
  135.7 4.3 %all-to-all-start.4 = ((f32[4,256,128]{2,1,0:T(8,128)}), f32[4,256,128]{2,1,0:T(8,128)S(1)}, u32[]{:S(2)}, u32[]{:S(2)}) async-start(f32[4,256,128]{2,1,0:T(8,128)} %bitcast.20), calls=%async_computation.5 | async-start | bytes 1048576 | tf_op jit(solution)/shard_map/all_to_all | solution.py:329
  139.9 0.0 copy-done.1
  139.9 3.5 %rows.1 = bf16[128,4096]{1,0:T(8,128)(2,1)} custom-call(bf16[32,128,128]{2,1,0:T(8,128)(2,1)} %copy-done.1), custom_call_target="tpu_custom_call" | custom-call | flops 2000000000 | bytes 1048576 | tf_op jit(solution)/shard_map/rows/pallas_call | solution.py:294
  143.4 0.6 reduce_sum.9
  144.0 5.4 %all-to-all-done.4 = f32[4,256,128]{2,1,0:T(8,128)S(1)} async-done(((f32[4,256,128]{2,1,0:T(8,128)}), f32[4,256,128]{2,1,0:T(8,128)S(1)}, u32[]{:S(2)}, u32[]{:S(2)}) %all-to-all-start.4) | async-done | bytes 524320 | tf_op jit(solution)/shard_map/all_to_all | solution.py:329
  149.5 0.8 pad_maximum_fusion
  (1 shorter events, 0.0 us)
Async XLA Ops:
  10.2 25.6 %all-to-all-start = ((bf16[32,80,128]{2,1,0:T(8,128)(2,1)}), bf16[32,80,128]{2,1,0:T(8,128)(2,1)S(1)}, u32[]{:S(2)}, u32[]{:S(2)}) async-start(bf16[32,80,128]{2,1,0:T(8,128)(2,1)} %slots.1), calls=%async_computation | async-start | bytes 1310720 | tf_op jit(solution)/shard_map/all_to_all | solution.py:312
  17.7 59.8 %all-gather.3.cloned.1.call-start = ((), (), s32[]{:S(2)}) async-start(), calls=%async_computation.7 | async-start | bytes 2359296 | tf_op jit(solution)/shard_map/all_gather | solution.py:320
  18.8 11.3 %collective-permute-start.2 = (bf16[256,128]{1,0:T(8,128)(2,1)S(1)}, bf16[256,128]{1,0:T(8,128)(2,1)S(1)}, u32[]{:S(2)}, u32[]{:S(2)}) collective-permute-start(bf16[256,128]{1,0:T(8,128)(2,1)S(1)} %get-tuple-element.22), channel_id=1, source_target_pairs={{0,1},{1,2},{2,3},{3,0},{4,5},{5,6},{6,7},{7,4},{8,9},{9,10},{10,1... | collective-permute-start | bytes 196616 | tf_op jit(solution)/shard_map/ppermute | solution.py:317
  20.3 11.3 %collective-permute-start.1 = (bf16[256,128]{1,0:T(8,128)(2,1)S(1)}, bf16[256,128]{1,0:T(8,128)(2,1)S(1)}, u32[]{:S(2)}, u32[]{:S(2)}) collective-permute-start(bf16[256,128]{1,0:T(8,128)(2,1)S(1)} %get-tuple-element.23), channel_id=1, source_target_pairs={{0,2},{1,3},{2,0},{3,1},{4,6},{5,7},{6,4},{7,5},{8,10},{9,11},{10,... | collective-permute-start | bytes 196616 | tf_op jit(solution)/shard_map/ppermute | solution.py:317
  23.0 8.6 %collective-permute-start = (bf16[256,128]{1,0:T(8,128)(2,1)S(1)}, bf16[256,128]{1,0:T(8,128)(2,1)S(1)}, u32[]{:S(2)}, u32[]{:S(2)}) collective-permute-start(bf16[256,128]{1,0:T(8,128)(2,1)S(1)} %get-tuple-element.24), channel_id=1, source_target_pairs={{0,3},{1,0},{2,1},{3,2},{4,7},{5,4},{6,5},{7,6},{8,11},{9,8},{10,9... | collective-permute-start | bytes 196616 | tf_op jit(solution)/shard_map/ppermute | solution.py:317
  35.8 5.6 %copy-start.2 = (bf16[32,80,128]{2,1,0:T(8,128)(2,1)}, bf16[32,80,128]{2,1,0:T(8,128)(2,1)S(1)}, u32[]{:S(2)}) copy-start(bf16[32,80,128]{2,1,0:T(8,128)(2,1)S(1)} %all-to-all-done.m_ref.t_ref) | copy-start | bytes 1966084
  35.8 28.5 %all-to-all-start.2 = ((bf16[32,128,128]{2,1,0:T(8,128)(2,1)}), bf16[32,128,128]{2,1,0:T(8,128)(2,1)S(1)}, u32[]{:S(2)}, u32[]{:S(2)}) async-start(bf16[32,128,128]{2,1,0:T(8,128)(2,1)} %blocks.1), calls=%async_computation.2 | async-start | bytes 2097152 | tf_op jit(solution)/shard_map/all_to_all | solution.py:321
  41.4 94.3 %reduce-scatter.2.cloned.1.call-start = ((), (), s32[]{:S(2)}) async-start(), calls=%async_computation.6 | async-start | bytes 4718592 | tf_op jit(solution)/shard_map/reduce_scatter | solution.py:328
  64.3 1.0 copy-start
  90.9 23.6 %all-to-all-start.1 = ((bf16[32,128,128]{2,1,0:T(8,128)(2,1)}), bf16[32,128,128]{2,1,0:T(8,128)(2,1)S(1)}, u32[]{:S(2)}, u32[]{:S(2)}) async-start(bf16[32,128,128]{2,1,0:T(8,128)(2,1)} %get-tuple-element.16), calls=%async_computation.1 | async-start | bytes 2097152 | tf_op jit(solution)/shard_map/all_to_all | solution.py:325
  114.5 25.4 %copy-start.1 = (bf16[32,128,128]{2,1,0:T(8,128)(2,1)}, bf16[32,128,128]{2,1,0:T(8,128)(2,1)S(1)}, u32[]{:S(2)}) copy-start(bf16[32,128,128]{2,1,0:T(8,128)(2,1)S(1)} %all-to-all-done.1.b_ref) | copy-start | bytes 3145732
  135.7 13.8 %all-to-all-start.4 = ((f32[4,256,128]{2,1,0:T(8,128)}), f32[4,256,128]{2,1,0:T(8,128)S(1)}, u32[]{:S(2)}, u32[]{:S(2)}) async-start(f32[4,256,128]{2,1,0:T(8,128)} %bitcast.20), calls=%async_computation.5 | async-start | bytes 1048576 | tf_op jit(solution)/shard_map/all_to_all | solution.py:329
Sparse Core Ops, SparseCore 0:
  32.5 42.2 all-gather.2
  77.6 57.9 reduce-scatter.1

commit v5 on v4

--- a/solution.py
+++ b/solution.py
@@ -19,7 +19,9 @@
 POS = NZ * GRP
 M_C = TOPK
 M_T = 2 * TOPK
-M_ALL = M_T + 16
+M_V = M_T + 16
+PIECE = OWN // ND
+M_ALL = M_V + PIECE
 MIB = 1024 * 1024
 
 
@@ -28,7 +30,7 @@
     return hi, (v - hi.astype(F32)).astype(BF)
 
 
-def slots_kernel(at_ref, w_ref, pos_ref, list_ref, out_ref, wide):
+def slots_kernel(at_ref, own_ref, w_ref, pos_ref, list_ref, v_ref, out_ref, wide):
     z = at_ref[0]
     pos = pos_ref[...]
     plane = ((pos >> 7) - z) & (NZ - 1)
@@ -46,23 +48,25 @@
     for i in range(NS):
         out_ref[i, 0:M_C, :] = w
         out_ref[i, M_C:M_T, :] = code
-        out_ref[i, M_T:M_ALL, :] = lists
+        out_ref[i, M_T:M_V, :] = lists
+        out_ref[i, M_V:M_ALL, :] = v_ref[:, i * CB:(i + 1) * CB]
 
 
 def cost(us):
     return pl.CostEstimate(flops=int(us * 1e9), bytes_accessed=2**20, transcendentals=0)
 
 
-def slots(at, w, pos, lists):
+def slots(at, own, w, pos, lists, values):
     spec = pltpu.PrefetchScalarGridSpec(
-        num_scalar_prefetch=1,
+        num_scalar_prefetch=2,
         grid=(1,),
         in_specs=[
-            pl.BlockSpec((TOPK, TOK), lambda i, at: (0, 0)),
-            pl.BlockSpec((TOPK, TOK), lambda i, at: (0, 0)),
-            pl.BlockSpec((1, NX * NZ, CAP), lambda i, at: (0, 0, 0)),
-        ],
-        out_specs=pl.BlockSpec((NS, M_ALL, TOK), lambda i, at: (0, 0, 0)),
+            pl.BlockSpec((TOPK, TOK), lambda i, at, own: (0, 0)),
+            pl.BlockSpec((TOPK, TOK), lambda i, at, own: (0, 0)),
+            pl.BlockSpec((1, NX * NZ, CAP), lambda i, at, own: (0, 0, 0)),
+            pl.BlockSpec((PIECE, NS * CB), lambda i, at, own: (own[0], 0)),
+        ],
+        out_specs=pl.BlockSpec((NS, M_ALL, TOK), lambda i, at, own: (0, 0, 0)),
         scratch_shapes=[pltpu.VMEM((NX * NZ, GRP), jnp.int32)],
     )
     return pl.pallas_call(
@@ -72,7 +76,7 @@
         compiler_params=pltpu.CompilerParams(vmem_limit_bytes=56 * MIB),
         cost_estimate=cost(2),
         name="slots",
-    )(at, w, pos, lists)
+    )(at, own, w, pos, lists, values)
 
 
 def blocks_kernel(cot_ref, out_ref):
@@ -125,7 +129,7 @@
         in_specs=[pl.BlockSpec((NS, M_T, TOK), lambda h: (0, 0, 0))],
         out_specs=pl.BlockSpec((NS, 2 * GRP, TOK), lambda h: (0, h, 0)),
         out_shape=jax.ShapeDtypeStruct((NS, POS, TOK), BF),
-        compiler_params=pltpu.CompilerParams(vmem_limit_bytes=56 * MIB),
+        compiler_params=pltpu.CompilerParams(vmem_limit_bytes=63 * MIB),
         cost_estimate=cost(25),
         name="dense",
     )(m)
@@ -204,7 +208,9 @@
             for x in range(NX):
                 hots[x, e * CAP:(e + 1) * CAP, :] = hot[x * CAP:(x + 1) * CAP]
         for x in range(NX):
-            rows = v_ref[(z + h) & (NZ - 1), (x - at_ref[1]) & (NX - 1)]
+            rows = jnp.concatenate(
+                [v_ref[(z + h) & (NZ - 1), d * NX + x] for d in range(ND)], axis=0
+            )
             got = jnp.dot(hots[x], rows, preferred_element_type=F32).astype(BF)
             at = h * GRP + x * CAP
             for e in range(EG):
@@ -225,7 +231,7 @@
             pl.BlockSpec(memory_space=pltpu.SMEM),
             pl.BlockSpec((EG, 16, TOK), lambda g: (g, M_T // 16, 0)),
             pl.BlockSpec((EG, POS, TOK), part),
-            pl.BlockSpec((NZ, NX, OWN, CB), lambda g: (0, 0, 0, 0)),
+            pl.BlockSpec((NZ, NS, PIECE, CB), lambda g: (0, 0, 0, 0)),
         ],
         out_specs=[pl.BlockSpec((EG, POS, CB), part), pl.BlockSpec((EG, TOK, CB), part)],
         out_shape=[
@@ -277,7 +283,7 @@
         ],
         out_specs=pl.BlockSpec((EG, TOPK, TOK), part),
         out_shape=jax.ShapeDtypeStruct((NS, TOPK, TOK), F32),
-        compiler_params=pltpu.CompilerParams(vmem_limit_bytes=56 * MIB),
+        compiler_params=pltpu.CompilerParams(vmem_limit_bytes=63 * MIB),
         cost_estimate=cost(18),
         name="scores",
     )(m, c, arrived)
@@ -303,21 +309,13 @@
 
 
 def on_device(slot_weight, slot_pos, touched, values, cotangent):
-    x = lax.axis_index("x").astype(jnp.int32)
-    d = lax.axis_index("dp").astype(jnp.int32)
-    at = jnp.stack([lax.axis_index("z").astype(jnp.int32), x])
+    at = lax.axis_index("z").astype(jnp.int32).reshape(1)
+    own = lax.axis_index("dp").astype(jnp.int32).reshape(1)
     plane = ("dp", "x")
-    m = slots(at, slot_weight.T, slot_pos.T, touched)
-    m, values, cotangent = lax.optimization_barrier((m, values, cotangent))
+    m = slots(at, own, slot_weight.T, slot_pos.T, touched, values)
     m = lax.all_to_all(m, plane, 0, 0, tiled=True)
-    mine = []
-    for i in range(NX):
-        to = (x - i) & (NX - 1)
-        part = lax.dynamic_slice(values, (0, (d * NX + to) * CB), (OWN, CB))
-        mine.append(lax.ppermute(part, "x", [(j, (j - i) % NX) for j in range(NX)]) if i else part)
-    mine = jnp.stack(mine)
-    m, c, _ = lax.optimization_barrier((m, blocks(cotangent), mine))
-    v = lax.all_gather(mine, "z")
+    m, c = lax.optimization_barrier((m, blocks(cotangent)))
+    v = lax.all_gather(m[:, M_V:, :], "z")
     c = lax.all_to_all(c, plane, 0, 0, tiled=True)
     wt = dense(m)
     table = grads(at, m, c, wt)

time: 158 us -> 153 us (0.968)
  starting transfers between devices: 30.5 us -> 24.7 us
  waiting for transfers between devices: 16.9 us -> 21.2 us
    all_to_all x1, waiting for transfers between devices: 0.01 us -> 11.4 us  [on_device(): m = lax.all_to_all(m, plane, 0, 0, tiled=True)]
    ppermute x3 -> x0, waiting for transfers between devices: 7.18 us -> none  [on_device(): lax.ppermute(part, 'x', [(j, (j - i) % NX) for j in range(NX)])]
    ppermute x3 -> x0, starting transfers between devices: 5.68 us -> none  [on_device(): lax.ppermute(part, 'x', [(j, (j - i) % NX) for j in range(NX)])]
    all_gather x1, waiting for transfers between devices: 0.02 us -> 1.97 us  [on_device(): v = lax.all_gather(m[:, M_V:, :], 'z')]
    reduce_scatter x1, waiting for transfers between devices: 3.71 us -> 1.8 us  [on_device(): table = lax.psum_scatter(table, 'z', scatter_dimension=0, tiled=True)]
  transfers between devices with their start and end apart: 9 -> 6, of which waited for: 5 -> 5; matrix products, arithmetic and copies ran while one was open for 2% -> 0% of each run, Pallas kernels for 45% -> 46%
where the time goes in v5:
time: 153 us; the launch traced here: 152 us
  Pallas kernels  72.3 us (47%)
  starting transfers between devices  24.7 us (16%)
  waiting for transfers between devices  21.2 us (14%)
  blocking collectives  17.4 us (11%)
  between operations  14.1 us (9%)
    pallas_call x1, Pallas kernels, dense(): pl.pallas_call(dense_kernel, grid=(NZ // 2,), in_specs=[pl.BlockSpec((NS,...  22.8 us
    all_to_all x1, blocking collectives, on_device(): g = lax.all_to_all(g, plane, 0, 0, tiled=True)  17.4 us
    pallas_call x1, Pallas kernels, scores(): pl.pallas_call(scores_kernel, grid=(NS // EG,), in_specs=[pl.BlockSpec((E...  15.6 us
    pallas_call x1, Pallas kernels, bags(): pl.pallas_call(bags_kernel, grid=(NS // EG,), in_specs=[pl.BlockSpec(memo...  13.4 us
    pallas_call x1, Pallas kernels, grads(): pl.pallas_call(grads_kernel, grid_spec=spec, out_shape=jax.ShapeDtypeStru...  11.5 us
    all_to_all x1, waiting for transfers between devices, on_device(): m = lax.all_to_all(m, plane, 0, 0, tiled=True)  11.4 us
    all_to_all x1, starting transfers between devices, on_device(): m = lax.all_to_all(m, plane, 0, 0, tiled=True)  7.54 us
    all_to_all x1, starting transfers between devices, on_device(): b = lax.all_to_all(b, plane, 0, 0, tiled=True)  7.45 us
  transfers between devices with their start and end apart: 6, of which 5 were waited for; matrix products, arithmetic and copies ran while one was open for 0% of the time, Pallas kernels for 46%

profile of v5, /device:TPU:8, one launch (start us, length us, event | category | flops | bytes accessed | tf_op | source)
XLA Modules:
  0.0 152.0 jit_solution(18291179089815989786)
XLA Ops:
  7.2 2.0 %slots.1 = bf16[32,112,128]{2,1,0:T(8,128)(2,1)} custom-call(s32[1]{0:T(128)} %bitcast.at_ref, s32[1]{0:T(128)} %bitcast.1.own_ref, bf16[32,128]{1,0:T(8,128)(2,1)} %bitcast.19, s32[32,128]{1,0:T(8,128)} %bitcast.18, s32[1,32,32]{2,1,0:T(8,128)} %list_ref.1, bf16[256,4096]{1,0:T(8,128)(2,1)} %v_ref.1), custom_call_target="tpu_custom_call" | custom-call | flops 2000000000 | bytes 1048576 | tf_op jit(solution)/shard_map/slots/pallas_call | solution.py:72
  9.2 7.5 %all-to-all-start = ((bf16[32,112,128]{2,1,0:T(8,128)(2,1)}), bf16[32,112,128]{2,1,0:T(8,128)(2,1)S(1)}, u32[]{:S(2)}, u32[]{:S(2)}) async-start(bf16[32,112,128]{2,1,0:T(8,128)(2,1)} %slots.1), calls=%async_computation | async-start | bytes 1835008 | tf_op jit(solution)/shard_map/all_to_all | solution.py:316
  16.8 0.0 all-gather.3.cloned.1.call-start
  16.8 3.4 %blocks.1 = bf16[32,128,128]{2,1,0:T(8,128)(2,1)} custom-call(bf16[128,4096]{1,0:T(8,128)(2,1)} %cot_ref.1), custom_call_target="tpu_custom_call" | custom-call | flops 2000000000 | bytes 1048576 | tf_op jit(solution)/shard_map/blocks/pallas_call | solution.py:89
  20.2 11.4 %all-to-all-done.m_ref.t_ref = bf16[32,112,128]{2,1,0:T(8,128)(2,1)S(1)} async-done(((bf16[32,112,128]{2,1,0:T(8,128)(2,1)}), bf16[32,112,128]{2,1,0:T(8,128)(2,1)S(1)}, u32[]{:S(2)}, u32[]{:S(2)}) %all-to-all-start) | async-done | bytes 917536 | tf_op jit(solution)/shard_map/all_to_all | solution.py:316
  31.6 0.0 copy-start
  31.6 0.8 slice.15
  32.4 0.0 all-gather.3.cloned.1.call-update
  32.4 5.4 %all-to-all-start.2 = ((bf16[32,128,128]{2,1,0:T(8,128)(2,1)}), bf16[32,128,128]{2,1,0:T(8,128)(2,1)}, u32[]{:S(2)}, u32[]{:S(2)}) async-start(bf16[32,128,128]{2,1,0:T(8,128)(2,1)} %blocks.1), calls=%async_computation.2 | async-start | bytes 2097152 | tf_op jit(solution)/shard_map/all_to_all | solution.py:319
  37.8 0.0 reduce-scatter.2.cloned.1.call-start
  37.9 0.0 copy-done
  37.9 22.8 %dense.1.wt_ref.wt0_ref.wt1_ref = bf16[32,1024,128]{2,1,0:T(8,128)(2,1)} custom-call(bf16[32,112,128]{2,1,0:T(8,128)(2,1)} %copy-done), custom_call_target="tpu_custom_call" | custom-call | flops 24999999488 | bytes 1048576 | tf_op jit(solution)/shard_map/dense/pallas_call | solution.py:126
  60.7 0.0 all-to-all-done.2.c_ref
  60.7 11.5 %grads.1 = f32[8,4,256,128]{3,2,1,0:T(8,128)} custom-call(s32[1]{0:T(128)} %bitcast.at_ref, bf16[32,112,128]{2,1,0:T(8,128)(2,1)} %copy-done, bf16[32,128,128]{2,1,0:T(8,128)(2,1)} %all-to-all-done.2.c_ref, bf16[32,1024,128]{2,1,0:T(8,128)(2,1)} %dense.1.wt_ref.wt0_ref.wt1_ref, bf16[32,1024,128]{2,1,0:T(8,128)(2,1)} %dense.1.wt_ref.wt0_ref.wt1_ref), custom_call_target="tpu_custom_call" | custom-call | flops 12000000000 | bytes 1048576 | tf_op jit(solution)/shard_map/grads/pallas_call | solution.py:186
  72.2 0.0 reduce-scatter.2.cloned.1.call-update
  72.3 2.0 %all-gather.3.cloned.1.call-done = bf16[256,32,128]{2,1,0:T(8,128)(2,1)} async-done(((bf16[32,32,128]{2,1,0:T(8,128)(2,1)}), bf16[256,32,128]{2,1,0:T(8,128)(2,1)}) %all-gather.3.cloned.1.call-update) | async-done | bytes 2097168 | tf_op jit(solution)/shard_map/all_gather | solution.py:318
  74.2 13.4 %bags.1 = (bf16[32,1024,128]{2,1,0:T(8,128)(2,1)}, bf16[32,128,128]{2,1,0:T(8,128)(2,1)}) custom-call(s32[1]{0:T(128)} %bitcast.at_ref, bf16[32,112,128]{2,1,0:T(8,128)(2,1)} %copy-done, bf16[32,1024,128]{2,1,0:T(8,128)(2,1)} %dense.1.wt_ref.wt0_ref.wt1_ref, bf16[8,32,32,128]{3,2,1,0:T(8,128)(2,1)} %bitcast.17), custom_call_target="tpu_custom_call" | custom-call | flops 17999998976 | bytes 1048576 | tf_op jit(solution)/shard_map/bags/pallas_call | solution.py:227
  87.6 7.5 %all-to-all-start.1 = ((bf16[32,128,128]{2,1,0:T(8,128)(2,1)}), bf16[32,128,128]{2,1,0:T(8,128)(2,1)}, u32[]{:S(2)}, u32[]{:S(2)}) async-start(bf16[32,128,128]{2,1,0:T(8,128)(2,1)} %get-tuple-element.10), calls=%async_computation.1 | async-start | bytes 2097152 | tf_op jit(solution)/shard_map/all_to_all | solution.py:323
  95.1 15.6 %scores.1 = f32[32,32,128]{2,1,0:T(8,128)} custom-call(bf16[32,112,128]{2,1,0:T(8,128)(2,1)} %copy-done, bf16[32,128,128]{2,1,0:T(8,128)(2,1)} %all-to-all-done.2.c_ref, bf16[32,1024,128]{2,1,0:T(8,128)(2,1)} %get-tuple-element.12.arrived_ref), custom_call_target="tpu_custom_call" | custom-call | flops 17999998976 | bytes 1048576 | tf_op jit(solution)/shard_map/scores/pallas_call | solution.py:276
  110.7 0.6 all-to-all-done.1.b_ref
  111.3 17.4 %all_to_all.25 = f32[32,32,128]{2,1,0:T(8,128)S(1)} all-to-all(f32[32,32,128]{2,1,0:T(8,128)} %scores.1), channel_id=1, replica_groups=mesh['dp'=8,'z'=8,'x'=4] {'dp','x'}, dimensions={0} | all-to-all | bytes 1048576 | tf_op jit(solution)/shard_map/all_to_all | solution.py:325
  128.7 1.8 %reduce-scatter.2.cloned.1.call-done = f32[1,4,256,128]{3,2,1,0:T(8,128)} async-done(((f32[8,4,256,128]{3,2,1,0:T(8,128)}), f32[1,4,256,128]{3,2,1,0:T(8,128)}) %reduce-scatter.2.cloned.1.call-update) | async-done | bytes 524304 | tf_op jit(solution)/shard_map/reduce_scatter | solution.py:326
  130.5 4.2 %all-to-all-start.4 = ((f32[4,256,128]{2,1,0:T(8,128)}), f32[4,256,128]{2,1,0:T(8,128)S(1)}, u32[]{:S(2)}, u32[]{:S(2)}) async-start(f32[4,256,128]{2,1,0:T(8,128)} %bitcast.15), calls=%async_computation.5 | async-start | bytes 1048576 | tf_op jit(solution)/shard_map/all_to_all | solution.py:327
  134.7 3.5 %rows.1 = bf16[128,4096]{1,0:T(8,128)(2,1)} custom-call(bf16[32,128,128]{2,1,0:T(8,128)(2,1)} %all-to-all-done.1.b_ref), custom_call_target="tpu_custom_call" | custom-call | flops 2000000000 | bytes 1048576 | tf_op jit(solution)/shard_map/rows/pallas_call | solution.py:300
  138.2 0.6 reduce_sum.9
  138.9 5.4 %all-to-all-done.4 = f32[4,256,128]{2,1,0:T(8,128)S(1)} async-done(((f32[4,256,128]{2,1,0:T(8,128)}), f32[4,256,128]{2,1,0:T(8,128)S(1)}, u32[]{:S(2)}, u32[]{:S(2)}) %all-to-all-start.4) | async-done | bytes 524320 | tf_op jit(solution)/shard_map/all_to_all | solution.py:327
  144.3 0.8 pad_maximum_fusion
  (1 shorter events, 0.0 us)
Async XLA Ops:
  9.2 22.4 %all-to-all-start = ((bf16[32,112,128]{2,1,0:T(8,128)(2,1)}), bf16[32,112,128]{2,1,0:T(8,128)(2,1)S(1)}, u32[]{:S(2)}, u32[]{:S(2)}) async-start(bf16[32,112,128]{2,1,0:T(8,128)(2,1)} %slots.1), calls=%async_computation | async-start | bytes 1835008 | tf_op jit(solution)/shard_map/all_to_all | solution.py:316
  16.8 57.5 %all-gather.3.cloned.1.call-start = ((), (), s32[]{:S(2)}) async-start(), calls=%async_computation.7 | async-start | bytes 2359296 | tf_op jit(solution)/shard_map/all_gather | solution.py:318
  31.6 6.3 %copy-start = (bf16[32,112,128]{2,1,0:T(8,128)(2,1)}, bf16[32,112,128]{2,1,0:T(8,128)(2,1)S(1)}, u32[]{:S(2)}) copy-start(bf16[32,112,128]{2,1,0:T(8,128)(2,1)S(1)} %all-to-all-done.m_ref.t_ref) | copy-start | bytes 2752516
  32.4 28.3 %all-to-all-start.2 = ((bf16[32,128,128]{2,1,0:T(8,128)(2,1)}), bf16[32,128,128]{2,1,0:T(8,128)(2,1)}, u32[]{:S(2)}, u32[]{:S(2)}) async-start(bf16[32,128,128]{2,1,0:T(8,128)(2,1)} %blocks.1), calls=%async_computation.2 | async-start | bytes 2097152 | tf_op jit(solution)/shard_map/all_to_all | solution.py:319
  37.8 92.7 %reduce-scatter.2.cloned.1.call-start = ((), (), s32[]{:S(2)}) async-start(), calls=%async_computation.6 | async-start | bytes 4718592 | tf_op jit(solution)/shard_map/reduce_scatter | solution.py:326
  87.6 23.7 %all-to-all-start.1 = ((bf16[32,128,128]{2,1,0:T(8,128)(2,1)}), bf16[32,128,128]{2,1,0:T(8,128)(2,1)}, u32[]{:S(2)}, u32[]{:S(2)}) async-start(bf16[32,128,128]{2,1,0:T(8,128)(2,1)} %get-tuple-element.10), calls=%async_computation.1 | async-start | bytes 2097152 | tf_op jit(solution)/shard_map/all_to_all | solution.py:323
  130.5 13.8 %all-to-all-start.4 = ((f32[4,256,128]{2,1,0:T(8,128)}), f32[4,256,128]{2,1,0:T(8,128)S(1)}, u32[]{:S(2)}, u32[]{:S(2)}) async-start(f32[4,256,128]{2,1,0:T(8,128)} %bitcast.15), calls=%async_computation.5 | async-start | bytes 1048576 | tf_op jit(solution)/shard_map/all_to_all | solution.py:327
Sparse Core Ops, SparseCore 0:
  32.5 41.6 all-gather.2
  76.8 53.6 reduce-scatter.1

commit v6 on v5

--- a/solution.py
+++ b/solution.py
@@ -18,10 +18,10 @@
 GRP = NX * CAP
 POS = NZ * GRP
 M_C = TOPK
-M_T = 2 * TOPK
-M_V = M_T + 16
+M_V = 2 * TOPK
 PIECE = OWN // ND
 M_ALL = M_V + PIECE
+C_ALL = TOK + 16
 MIB = 1024 * 1024
 
 
@@ -30,11 +30,45 @@
     return hi, (v - hi.astype(F32)).astype(BF)
 
 
-def slots_kernel(at_ref, own_ref, w_ref, pos_ref, list_ref, v_ref, out_ref, wide):
+def slots_kernel(at_ref, own_ref, w_ref, pos_ref, v_ref, out_ref):
     z = at_ref[0]
     pos = pos_ref[...]
     plane = ((pos >> 7) - z) & (NZ - 1)
     code = (((pos & (GRP - 1)) + GRP) << plane).astype(F32).astype(BF)
+    w = w_ref[...]
+    for i in range(NS):
+        out_ref[i, 0:M_C, :] = w
+        out_ref[i, M_C:M_V, :] = code
+        out_ref[i, M_V:M_ALL, :] = v_ref[:, i * CB:(i + 1) * CB]
+
+
+def cost(us):
+    return pl.CostEstimate(flops=int(us * 1e9), bytes_accessed=2**20, transcendentals=0)
+
+
+def slots(at, own, w, pos, values):
+    spec = pltpu.PrefetchScalarGridSpec(
+        num_scalar_prefetch=2,
+        grid=(1,),
+        in_specs=[
+            pl.BlockSpec((TOPK, TOK), lambda i, at, own: (0, 0)),
+            pl.BlockSpec((TOPK, TOK), lambda i, at, own: (0, 0)),
+            pl.BlockSpec((PIECE, NS * CB), lambda i, at, own: (own[0], 0)),
+        ],
+        out_specs=pl.BlockSpec((NS, M_ALL, TOK), lambda i, at, own: (0, 0, 0)),
+    )
+    return pl.pallas_call(
+        slots_kernel,
+        grid_spec=spec,
+        out_shape=jax.ShapeDtypeStruct((NS, M_ALL, TOK), BF),
+        compiler_params=pltpu.CompilerParams(vmem_limit_bytes=56 * MIB),
+        cost_estimate=cost(2),
+        name="slots",
+    )(at, own, w, pos, values)
+
+
+def blocks_kernel(at_ref, cot_ref, list_ref, out_ref, wide):
+    z = at_ref[0]
     lists = list_ref[0]
     owner = lax.broadcasted_iota(jnp.int32, (NX * NZ, GRP), 0) & (NX - 1)
     lane = lax.broadcasted_iota(jnp.int32, (NX * NZ, GRP), 1) // CAP
@@ -44,57 +78,30 @@
         four = [wide[pl.ds(((z + h) & (NZ - 1)) * NX + i, 1), :] for i in range(NX)]
         rows.append(four[0] + four[1] + four[2] + four[3])
     lists = jnp.concatenate(rows + rows, axis=0).astype(F32).astype(BF)
-    w = w_ref[...]
-    for i in range(NS):
-        out_ref[i, 0:M_C, :] = w
-        out_ref[i, M_C:M_T, :] = code
-        out_ref[i, M_T:M_V, :] = lists
-        out_ref[i, M_V:M_ALL, :] = v_ref[:, i * CB:(i + 1) * CB]
-
-
-def cost(us):
-    return pl.CostEstimate(flops=int(us * 1e9), bytes_accessed=2**20, transcendentals=0)
-
-
-def slots(at, own, w, pos, lists, values):
+    for i in range(out_ref.shape[0]):
+        out_ref[i, 0:TOK, :] = cot_ref[:, i * CB:(i + 1) * CB]
+        out_ref[i, TOK:C_ALL, :] = lists
+
+
+def blocks(at, cot, lists):
+    per = 8
     spec = pltpu.PrefetchScalarGridSpec(
-        num_scalar_prefetch=2,
-        grid=(1,),
-        in_specs=[
-            pl.BlockSpec((TOPK, TOK), lambda i, at, own: (0, 0)),
-            pl.BlockSpec((TOPK, TOK), lambda i, at, own: (0, 0)),
-            pl.BlockSpec((1, NX * NZ, CAP), lambda i, at, own: (0, 0, 0)),
-            pl.BlockSpec((PIECE, NS * CB), lambda i, at, own: (own[0], 0)),
-        ],
-        out_specs=pl.BlockSpec((NS, M_ALL, TOK), lambda i, at, own: (0, 0, 0)),
+        num_scalar_prefetch=1,
+        grid=(NS // per,),
+        in_specs=[
+            pl.BlockSpec((TOK, per * CB), lambda g, at: (0, g)),
+            pl.BlockSpec((1, NX * NZ, CAP), lambda g, at: (0, 0, 0)),
+        ],
+        out_specs=pl.BlockSpec((per, C_ALL, CB), lambda g, at: (g, 0, 0)),
         scratch_shapes=[pltpu.VMEM((NX * NZ, GRP), jnp.int32)],
     )
     return pl.pallas_call(
-        slots_kernel,
+        blocks_kernel,
         grid_spec=spec,
-        out_shape=jax.ShapeDtypeStruct((NS, M_ALL, TOK), BF),
-        compiler_params=pltpu.CompilerParams(vmem_limit_bytes=56 * MIB),
-        cost_estimate=cost(2),
-        name="slots",
-    )(at, own, w, pos, lists, values)
-
-
-def blocks_kernel(cot_ref, out_ref):
-    for i in range(out_ref.shape[0]):
-        out_ref[i] = cot_ref[:, i * CB:(i + 1) * CB]
-
-
-def blocks(cot):
-    per = 8
-    return pl.pallas_call(
-        blocks_kernel,
-        grid=(NS // per,),
-        in_specs=[pl.BlockSpec((TOK, per * CB), lambda g: (0, g))],
-        out_specs=pl.BlockSpec((per, TOK, CB), lambda g: (g, 0, 0)),
-        out_shape=jax.ShapeDtypeStruct((NS, TOK, CB), BF),
-        cost_estimate=cost(2),
+        out_shape=jax.ShapeDtypeStruct((NS, C_ALL, CB), BF),
+        cost_estimate=cost(3),
         name="blocks",
-    )(cot)
+    )(at, cot, lists)
 
 
 def dense_kernel(m_ref, wt_ref):
@@ -106,7 +113,7 @@
     def one(e, carry):
         accs = [[jnp.zeros((tile, TOK), BF) for _ in tiles] for _ in range(2)]
         we = m_ref[e, 0:M_C, :]
-        ce = m_ref[e, M_C:M_T, :]
+        ce = m_ref[e, M_C:M_V, :]
         for k in range(TOPK):
             w = jnp.broadcast_to(we[k:k + 1, :], (tile, TOK))
             at = jnp.broadcast_to(ce[k:k + 1, :], (tile, TOK))
@@ -126,7 +133,7 @@
     return pl.pallas_call(
         dense_kernel,
         grid=(NZ // 2,),
-        in_specs=[pl.BlockSpec((NS, M_T, TOK), lambda h: (0, 0, 0))],
+        in_specs=[pl.BlockSpec((NS, M_V, TOK), lambda h: (0, 0, 0))],
         out_specs=pl.BlockSpec((NS, 2 * GRP, TOK), lambda h: (0, h, 0)),
         out_shape=jax.ShapeDtypeStruct((NS, POS, TOK), BF),
         compiler_params=pltpu.CompilerParams(vmem_limit_bytes=63 * MIB),
@@ -167,12 +174,12 @@
             out_ref[i, x] = total[:, :CB] + total[:, CB:]
 
 
-def grads(at, m, c, wt):
+def grads(at, c, wt):
     spec = pltpu.PrefetchScalarGridSpec(
         num_scalar_prefetch=1,
         grid=(NZ // 2,),
         in_specs=[
-            pl.BlockSpec((NS, 16, TOK), lambda q, at: (0, M_T // 16, 0)),
+            pl.BlockSpec((NS, 16, TOK), lambda q, at: (0, TOK // 16, 0)),
             pl.BlockSpec((NS, TOK, CB), lambda q, at: (0, 0, 0)),
             pl.BlockSpec((NS, GRP, TOK), lambda q, at: (0, (2 * q - at[0]) & (NZ - 1), 0)),
             pl.BlockSpec((NS, GRP, TOK), lambda q, at: (0, (2 * q + 1 - at[0]) & (NZ - 1), 0)),
@@ -190,7 +197,7 @@
         compiler_params=pltpu.CompilerParams(vmem_limit_bytes=56 * MIB),
         cost_estimate=cost(12),
         name="grads",
-    )(at, m, c, wt, wt)
+    )(at, c, c, wt, wt)
 
 
 EG = 8
@@ -222,14 +229,14 @@
         out_ref[e] = bag.astype(BF)
 
 
-def bags(at, m, wt, v):
+def bags(at, c, wt, v):
     part = lambda g: (g, 0, 0)
     return pl.pallas_call(
         bags_kernel,
         grid=(NS // EG,),
         in_specs=[
             pl.BlockSpec(memory_space=pltpu.SMEM),
-            pl.BlockSpec((EG, 16, TOK), lambda g: (g, M_T // 16, 0)),
+            pl.BlockSpec((EG, 16, TOK), lambda g: (g, TOK // 16, 0)),
             pl.BlockSpec((EG, POS, TOK), part),
             pl.BlockSpec((NZ, NS, PIECE, CB), lambda g: (0, 0, 0, 0)),
         ],
@@ -245,7 +252,7 @@
         compiler_params=pltpu.CompilerParams(vmem_limit_bytes=56 * MIB),
         cost_estimate=cost(18),
         name="bags",
-    )(at, m, wt, v)
+    )(at, c, wt, v)
 
 
 def scores_kernel(m_ref, c_ref, arrived_ref, out_ref):
@@ -312,14 +319,14 @@
     at = lax.axis_index("z").astype(jnp.int32).reshape(1)
     own = lax.axis_index("dp").astype(jnp.int32).reshape(1)
     plane = ("dp", "x")
-    m = slots(at, own, slot_weight.T, slot_pos.T, touched, values)
+    m = slots(at, own, slot_weight.T, slot_pos.T, values)
     m = lax.all_to_all(m, plane, 0, 0, tiled=True)
-    m, c = lax.optimization_barrier((m, blocks(cotangent)))
+    m, c = lax.optimization_barrier((m, blocks(at, cotangent, touched)))
     v = lax.all_gather(m[:, M_V:, :], "z")
     c = lax.all_to_all(c, plane, 0, 0, tiled=True)
     wt = dense(m)
-    table = grads(at, m, c, wt)
-    arrived, b = bags(at, m, wt, v)
+    table = grads(at, c, wt)
+    arrived, b = bags(at, c, wt, v)
     b = lax.all_to_all(b, plane, 0, 0, tiled=True)
     b, g = lax.optimization_barrier((b, scores(m, c, arrived)))
     g = lax.all_to_all(g, plane, 0, 0, tiled=True)

time: 153 us -> 151 us (0.987)
  transfers between devices with their start and end apart: 6 -> 6, of which waited for: 5 -> 5; matrix products, arithmetic and copies ran while one was open for 0% -> 0% of each run, Pallas kernels for 46% -> 47%
where the time goes in v6:
time: 151 us
  Pallas kernels  72.4 us (48%)
  starting transfers between devices  24.8 us (16%)
  waiting for transfers between devices  19.7 us (13%)
  blocking collectives  17.4 us (12%)
  between operations  14.1 us (9%)
    pallas_call x1, Pallas kernels, dense(): pl.pallas_call(dense_kernel, grid=(NZ // 2,), in_specs=[pl.BlockSpec((NS,...  22.8 us
    all_to_all x1, blocking collectives, on_device(): g = lax.all_to_all(g, plane, 0, 0, tiled=True)  17.4 us
    pallas_call x1, Pallas kernels, scores(): pl.pallas_call(scores_kernel, grid=(NS // EG,), in_specs=[pl.BlockSpec((E...  15.7 us
    pallas_call x1, Pallas kernels, bags(): pl.pallas_call(bags_kernel, grid=(NS // EG,), in_specs=[pl.BlockSpec(memo...  13.4 us
    pallas_call x1, Pallas kernels, grads(): pl.pallas_call(grads_kernel, grid_spec=spec, out_shape=jax.ShapeDtypeStru...  11.5 us
    all_to_all x1, waiting for transfers between devices, on_device(): m = lax.all_to_all(m, plane, 0, 0, tiled=True)  9.88 us
    all_to_all x1, starting transfers between devices, on_device(): m = lax.all_to_all(m, plane, 0, 0, tiled=True)  7.54 us
    all_to_all x1, starting transfers between devices, on_device(): b = lax.all_to_all(b, plane, 0, 0, tiled=True)  7.45 us
  transfers between devices with their start and end apart: 6, of which 5 were waited for; matrix products, arithmetic and copies ran while one was open for 0% of the time, Pallas kernels for 47%

profile of v6, /device:TPU:8, one launch (start us, length us, event | category | flops | bytes accessed | tf_op | source)
XLA Modules:
  0.0 150.6 jit_solution(10970420843103389706)
XLA Ops:
  7.2 1.9 %slots.1 = bf16[32,96,128]{2,1,0:T(8,128)(2,1)} custom-call(s32[1]{0:T(128)} %bitcast.at_ref, s32[1]{0:T(128)} %bitcast.1.own_ref, bf16[32,128]{1,0:T(8,128)(2,1)} %bitcast.19, s32[32,128]{1,0:T(8,128)} %bitcast.18, bf16[256,4096]{1,0:T(8,128)(2,1)} %v_ref.1), custom_call_target="tpu_custom_call" | custom-call | flops 2000000000 | bytes 1048576 | tf_op jit(solution)/shard_map/slots/pallas_call | solution.py:60
  9.1 7.5 %all-to-all-start = ((bf16[32,96,128]{2,1,0:T(8,128)(2,1)}), bf16[32,96,128]{2,1,0:T(8,128)(2,1)S(1)}, u32[]{:S(2)}, u32[]{:S(2)}) async-start(bf16[32,96,128]{2,1,0:T(8,128)(2,1)} %slots.1), calls=%async_computation | async-start | bytes 1572864 | tf_op jit(solution)/shard_map/all_to_all | solution.py:323
  16.7 0.0 all-gather.3.cloned.1.call-start
  16.7 3.6 %blocks.1 = bf16[32,144,128]{2,1,0:T(8,128)(2,1)} custom-call(s32[1]{0:T(128)} %bitcast.at_ref, bf16[128,4096]{1,0:T(8,128)(2,1)} %cot_ref.1, s32[1,32,32]{2,1,0:T(8,128)} %list_ref.1), custom_call_target="tpu_custom_call" | custom-call | flops 3000000000 | bytes 1048576 | tf_op jit(solution)/shard_map/blocks/pallas_call | solution.py:98
  20.3 9.9 %all-to-all-done.m_ref = bf16[32,96,128]{2,1,0:T(8,128)(2,1)S(1)} async-done(((bf16[32,96,128]{2,1,0:T(8,128)(2,1)}), bf16[32,96,128]{2,1,0:T(8,128)(2,1)S(1)}, u32[]{:S(2)}, u32[]{:S(2)}) %all-to-all-start) | async-done | bytes 786464 | tf_op jit(solution)/shard_map/all_to_all | solution.py:323
  30.2 0.0 copy-start
  30.2 0.8 slice.15
  30.9 0.0 all-gather.3.cloned.1.call-update
  31.0 5.5 %all-to-all-start.1 = ((bf16[32,144,128]{2,1,0:T(8,128)(2,1)}), bf16[32,144,128]{2,1,0:T(8,128)(2,1)}, u32[]{:S(2)}, u32[]{:S(2)}) async-start(bf16[32,144,128]{2,1,0:T(8,128)(2,1)} %blocks.1), calls=%async_computation.1 | async-start | bytes 2359296 | tf_op jit(solution)/shard_map/all_to_all | solution.py:326
  36.4 0.0 reduce-scatter.2.cloned.1.call-start
  36.5 0.0 copy-done
  36.5 22.8 %dense.1.wt_ref.wt0_ref.wt1_ref = bf16[32,1024,128]{2,1,0:T(8,128)(2,1)} custom-call(bf16[32,96,128]{2,1,0:T(8,128)(2,1)} %copy-done), custom_call_target="tpu_custom_call" | custom-call | flops 24999999488 | bytes 1048576 | tf_op jit(solution)/shard_map/dense/pallas_call | solution.py:133
  59.3 0.0 all-to-all-done.1.t_ref.c_ref
  59.3 11.5 %grads.1 = f32[8,4,256,128]{3,2,1,0:T(8,128)} custom-call(s32[1]{0:T(128)} %bitcast.at_ref, bf16[32,144,128]{2,1,0:T(8,128)(2,1)} %all-to-all-done.1.t_ref.c_ref, bf16[32,144,128]{2,1,0:T(8,128)(2,1)} %all-to-all-done.1.t_ref.c_ref, bf16[32,1024,128]{2,1,0:T(8,128)(2,1)} %dense.1.wt_ref.wt0_ref.wt1_ref, bf16[32,1024,128]{2,1,0:T(8,128)(2,1)} %dense.1.wt_ref.wt0_ref.wt1_ref), custom_call_target="tpu_custom_call" | custom-call | flops 12000000000 | bytes 1048576 | tf_op jit(solution)/shard_map/grads/pallas_call | solution.py:193
  70.8 0.0 reduce-scatter.2.cloned.1.call-update
  70.9 1.9 %all-gather.3.cloned.1.call-done = bf16[256,32,128]{2,1,0:T(8,128)(2,1)} async-done(((bf16[32,32,128]{2,1,0:T(8,128)(2,1)}), bf16[256,32,128]{2,1,0:T(8,128)(2,1)}) %all-gather.3.cloned.1.call-update) | async-done | bytes 2097168 | tf_op jit(solution)/shard_map/all_gather | solution.py:325
  72.7 13.4 %bags.1 = (bf16[32,1024,128]{2,1,0:T(8,128)(2,1)}, bf16[32,128,128]{2,1,0:T(8,128)(2,1)}) custom-call(s32[1]{0:T(128)} %bitcast.at_ref, bf16[32,144,128]{2,1,0:T(8,128)(2,1)} %all-to-all-done.1.t_ref.c_ref, bf16[32,1024,128]{2,1,0:T(8,128)(2,1)} %dense.1.wt_ref.wt0_ref.wt1_ref, bf16[8,32,32,128]{3,2,1,0:T(8,128)(2,1)} %bitcast.17), custom_call_target="tpu_custom_call" | custom-call | flops 17999998976 | bytes 1048576 | tf_op jit(solution)/shard_map/bags/pallas_call | solution.py:234
  86.1 7.4 %all-to-all-start.2 = ((bf16[32,128,128]{2,1,0:T(8,128)(2,1)}), bf16[32,128,128]{2,1,0:T(8,128)(2,1)}, u32[]{:S(2)}, u32[]{:S(2)}) async-start(bf16[32,128,128]{2,1,0:T(8,128)(2,1)} %get-tuple-element.11), calls=%async_computation.2 | async-start | bytes 2097152 | tf_op jit(solution)/shard_map/all_to_all | solution.py:330
  93.6 15.7 %scores.1 = f32[32,32,128]{2,1,0:T(8,128)} custom-call(bf16[32,96,128]{2,1,0:T(8,128)(2,1)} %copy-done, bf16[32,144,128]{2,1,0:T(8,128)(2,1)} %all-to-all-done.1.t_ref.c_ref, bf16[32,1024,128]{2,1,0:T(8,128)(2,1)} %get-tuple-element.12.arrived_ref), custom_call_target="tpu_custom_call" | custom-call | flops 17999998976 | bytes 1048576 | tf_op jit(solution)/shard_map/scores/pallas_call | solution.py:283
  109.2 0.6 all-to-all-done.2.b_ref
  109.8 17.4 %all_to_all.25 = f32[32,32,128]{2,1,0:T(8,128)S(1)} all-to-all(f32[32,32,128]{2,1,0:T(8,128)} %scores.1), channel_id=1, replica_groups=mesh['dp'=8,'z'=8,'x'=4] {'dp','x'}, dimensions={0} | all-to-all | bytes 1048576 | tf_op jit(solution)/shard_map/all_to_all | solution.py:332
  127.2 1.9 %reduce-scatter.2.cloned.1.call-done = f32[1,4,256,128]{3,2,1,0:T(8,128)} async-done(((f32[8,4,256,128]{3,2,1,0:T(8,128)}), f32[1,4,256,128]{3,2,1,0:T(8,128)}) %reduce-scatter.2.cloned.1.call-update) | async-done | bytes 524304 | tf_op jit(solution)/shard_map/reduce_scatter | solution.py:333
  129.1 4.2 %all-to-all-start.4 = ((f32[4,256,128]{2,1,0:T(8,128)}), f32[4,256,128]{2,1,0:T(8,128)S(1)}, u32[]{:S(2)}, u32[]{:S(2)}) async-start(f32[4,256,128]{2,1,0:T(8,128)} %bitcast.15), calls=%async_computation.5 | async-start | bytes 1048576 | tf_op jit(solution)/shard_map/all_to_all | solution.py:334
  133.3 3.5 %rows.1 = bf16[128,4096]{1,0:T(8,128)(2,1)} custom-call(bf16[32,128,128]{2,1,0:T(8,128)(2,1)} %all-to-all-done.2.b_ref), custom_call_target="tpu_custom_call" | custom-call | flops 2000000000 | bytes 1048576 | tf_op jit(solution)/shard_map/rows/pallas_call | solution.py:307
  136.8 0.6 reduce_sum.9
  137.5 5.4 %all-to-all-done.4 = f32[4,256,128]{2,1,0:T(8,128)S(1)} async-done(((f32[4,256,128]{2,1,0:T(8,128)}), f32[4,256,128]{2,1,0:T(8,128)S(1)}, u32[]{:S(2)}, u32[]{:S(2)}) %all-to-all-start.4) | async-done | bytes 524320 | tf_op jit(solution)/shard_map/all_to_all | solution.py:334
  142.9 0.8 pad_maximum_fusion
  (1 shorter events, 0.0 us)
Async XLA Ops:
  9.1 21.1 %all-to-all-start = ((bf16[32,96,128]{2,1,0:T(8,128)(2,1)}), bf16[32,96,128]{2,1,0:T(8,128)(2,1)S(1)}, u32[]{:S(2)}, u32[]{:S(2)}) async-start(bf16[32,96,128]{2,1,0:T(8,128)(2,1)} %slots.1), calls=%async_computation | async-start | bytes 1572864 | tf_op jit(solution)/shard_map/all_to_all | solution.py:323
  16.7 56.1 %all-gather.3.cloned.1.call-start = ((), (), s32[]{:S(2)}) async-start(), calls=%async_computation.7 | async-start | bytes 2359296 | tf_op jit(solution)/shard_map/all_gather | solution.py:325
  30.2 6.3 %copy-start = (bf16[32,96,128]{2,1,0:T(8,128)(2,1)}, bf16[32,96,128]{2,1,0:T(8,128)(2,1)S(1)}, u32[]{:S(2)}) copy-start(bf16[32,96,128]{2,1,0:T(8,128)(2,1)S(1)} %all-to-all-done.m_ref) | copy-start | bytes 2359300
  31.0 28.4 %all-to-all-start.1 = ((bf16[32,144,128]{2,1,0:T(8,128)(2,1)}), bf16[32,144,128]{2,1,0:T(8,128)(2,1)}, u32[]{:S(2)}, u32[]{:S(2)}) async-start(bf16[32,144,128]{2,1,0:T(8,128)(2,1)} %blocks.1), calls=%async_computation.1 | async-start | bytes 2359296 | tf_op jit(solution)/shard_map/all_to_all | solution.py:326
  36.4 92.7 %reduce-scatter.2.cloned.1.call-start = ((), (), s32[]{:S(2)}) async-start(), calls=%async_computation.6 | async-start | bytes 4718592 | tf_op jit(solution)/shard_map/reduce_scatter | solution.py:333
  86.1 23.7 %all-to-all-start.2 = ((bf16[32,128,128]{2,1,0:T(8,128)(2,1)}), bf16[32,128,128]{2,1,0:T(8,128)(2,1)}, u32[]{:S(2)}, u32[]{:S(2)}) async-start(bf16[32,128,128]{2,1,0:T(8,128)(2,1)} %get-tuple-element.11), calls=%async_computation.2 | async-start | bytes 2097152 | tf_op jit(solution)/shard_map/all_to_all | solution.py:330
  129.1 13.8 %all-to-all-start.4 = ((f32[4,256,128]{2,1,0:T(8,128)}), f32[4,256,128]{2,1,0:T(8,128)S(1)}, u32[]{:S(2)}, u32[]{:S(2)}) async-start(f32[4,256,128]{2,1,0:T(8,128)} %bitcast.15), calls=%async_computation.5 | async-start | bytes 1048576 | tf_op jit(solution)/shard_map/all_to_all | solution.py:334
Sparse Core Ops, SparseCore 0:
  31.1 41.6 all-gather.2
  75.3 53.7 reduce-scatter.1

commit v7 on v6

--- a/solution.py
+++ b/solution.py
@@ -18,9 +18,7 @@
 GRP = NX * CAP
 POS = NZ * GRP
 M_C = TOPK
-M_V = 2 * TOPK
-PIECE = OWN // ND
-M_ALL = M_V + PIECE
+M_ALL = 2 * TOPK
 C_ALL = TOK + 16
 MIB = 1024 * 1024
 
@@ -30,7 +28,7 @@
     return hi, (v - hi.astype(F32)).astype(BF)
 
 
-def slots_kernel(at_ref, own_ref, w_ref, pos_ref, v_ref, out_ref):
+def slots_kernel(at_ref, w_ref, pos_ref, out_ref):
     z = at_ref[0]
     pos = pos_ref[...]
     plane = ((pos >> 7) - z) & (NZ - 1)
@@ -38,24 +36,22 @@
     w = w_ref[...]
     for i in range(NS):
         out_ref[i, 0:M_C, :] = w
-        out_ref[i, M_C:M_V, :] = code
-        out_ref[i, M_V:M_ALL, :] = v_ref[:, i * CB:(i + 1) * CB]
+        out_ref[i, M_C:M_ALL, :] = code
 
 
 def cost(us):
     return pl.CostEstimate(flops=int(us * 1e9), bytes_accessed=2**20, transcendentals=0)
 
 
-def slots(at, own, w, pos, values):
+def slots(at, w, pos):
     spec = pltpu.PrefetchScalarGridSpec(
-        num_scalar_prefetch=2,
+        num_scalar_prefetch=1,
         grid=(1,),
         in_specs=[
-            pl.BlockSpec((TOPK, TOK), lambda i, at, own: (0, 0)),
-            pl.BlockSpec((TOPK, TOK), lambda i, at, own: (0, 0)),
-            pl.BlockSpec((PIECE, NS * CB), lambda i, at, own: (own[0], 0)),
-        ],
-        out_specs=pl.BlockSpec((NS, M_ALL, TOK), lambda i, at, own: (0, 0, 0)),
+            pl.BlockSpec((TOPK, TOK), lambda i, at: (0, 0)),
+            pl.BlockSpec((TOPK, TOK), lambda i, at: (0, 0)),
+        ],
+        out_specs=pl.BlockSpec((NS, M_ALL, TOK), lambda i, at: (0, 0, 0)),
     )
     return pl.pallas_call(
         slots_kernel,
@@ -64,7 +60,7 @@
         compiler_params=pltpu.CompilerParams(vmem_limit_bytes=56 * MIB),
         cost_estimate=cost(2),
         name="slots",
-    )(at, own, w, pos, values)
+    )(at, w, pos)
 
 
 def blocks_kernel(at_ref, cot_ref, list_ref, out_ref, wide):
@@ -113,7 +109,7 @@
     def one(e, carry):
         accs = [[jnp.zeros((tile, TOK), BF) for _ in tiles] for _ in range(2)]
         we = m_ref[e, 0:M_C, :]
-        ce = m_ref[e, M_C:M_V, :]
+        ce = m_ref[e, M_C:M_ALL, :]
         for k in range(TOPK):
             w = jnp.broadcast_to(we[k:k + 1, :], (tile, TOK))
             at = jnp.broadcast_to(ce[k:k + 1, :], (tile, TOK))
@@ -133,7 +129,7 @@
     return pl.pallas_call(
         dense_kernel,
         grid=(NZ // 2,),
-        in_specs=[pl.BlockSpec((NS, M_V, TOK), lambda h: (0, 0, 0))],
+        in_specs=[pl.BlockSpec((NS, M_ALL, TOK), lambda h: (0, 0, 0))],
         out_specs=pl.BlockSpec((NS, 2 * GRP, TOK), lambda h: (0, h, 0)),
         out_shape=jax.ShapeDtypeStruct((NS, POS, TOK), BF),
         compiler_params=pltpu.CompilerParams(vmem_limit_bytes=63 * MIB),
@@ -203,7 +199,7 @@
 EG = 8
 
 
-def bags_kernel(at_ref, t_ref, wt_ref, v_ref, arrived_ref, out_ref, hots, lists):
+def bags_kernel(at_ref, x_ref, t_ref, wt_ref, v_ref, arrived_ref, out_ref, hots, lists):
     z = at_ref[0]
     for e in range(EG):
         lists[e * 16:(e + 1) * 16, :] = t_ref[e].astype(F32)
@@ -215,9 +211,7 @@
             for x in range(NX):
                 hots[x, e * CAP:(e + 1) * CAP, :] = hot[x * CAP:(x + 1) * CAP]
         for x in range(NX):
-            rows = jnp.concatenate(
-                [v_ref[(z + h) & (NZ - 1), d * NX + x] for d in range(ND)], axis=0
-            )
+            rows = v_ref[(z + h) & (NZ - 1), (x - x_ref[0]) & (NX - 1)]
             got = jnp.dot(hots[x], rows, preferred_element_type=F32).astype(BF)
             at = h * GRP + x * CAP
             for e in range(EG):
@@ -229,16 +223,17 @@
         out_ref[e] = bag.astype(BF)
 
 
-def bags(at, c, wt, v):
+def bags(at, x, c, wt, v):
     part = lambda g: (g, 0, 0)
     return pl.pallas_call(
         bags_kernel,
         grid=(NS // EG,),
         in_specs=[
+            pl.BlockSpec(memory_space=pltpu.SMEM),
             pl.BlockSpec(memory_space=pltpu.SMEM),
             pl.BlockSpec((EG, 16, TOK), lambda g: (g, TOK // 16, 0)),
             pl.BlockSpec((EG, POS, TOK), part),
-            pl.BlockSpec((NZ, NS, PIECE, CB), lambda g: (0, 0, 0, 0)),
+            pl.BlockSpec((NZ, NX, OWN, CB), lambda g: (0, 0, 0, 0)),
         ],
         out_specs=[pl.BlockSpec((EG, POS, CB), part), pl.BlockSpec((EG, TOK, CB), part)],
         out_shape=[
@@ -252,7 +247,7 @@
         compiler_params=pltpu.CompilerParams(vmem_limit_bytes=56 * MIB),
         cost_estimate=cost(18),
         name="bags",
-    )(at, c, wt, v)
+    )(at, x, c, wt, v)
 
 
 def scores_kernel(m_ref, c_ref, arrived_ref, out_ref):
@@ -316,17 +311,28 @@
 
 
 def on_device(slot_weight, slot_pos, touched, values, cotangent):
+    x = lax.axis_index("x").astype(jnp.int32)
+    d = lax.axis_index("dp").astype(jnp.int32)
     at = lax.axis_index("z").astype(jnp.int32).reshape(1)
-    own = lax.axis_index("dp").astype(jnp.int32).reshape(1)
     plane = ("dp", "x")
-    m = slots(at, own, slot_weight.T, slot_pos.T, values)
+    parts = []
+    for i in range(NX):
+        to = (x - i) & (NX - 1)
+        parts.append(lax.dynamic_slice(values, (0, (d * NX + to) * CB), (OWN, CB)))
+    parts, slot_weight = lax.optimization_barrier((parts, slot_weight))
+    mine = parts[:1] + [
+        lax.ppermute(parts[i], "x", [(j, (j - i) % NX) for j in range(NX)]) for i in range(1, NX)
+    ]
+    m = slots(at, slot_weight.T, slot_pos.T)
+    m, cotangent, _ = lax.optimization_barrier((m, cotangent, mine[1]))
     m = lax.all_to_all(m, plane, 0, 0, tiled=True)
-    m, c = lax.optimization_barrier((m, blocks(at, cotangent, touched)))
-    v = lax.all_gather(m[:, M_V:, :], "z")
+    mine = jnp.stack(mine)
+    m, c, _ = lax.optimization_barrier((m, blocks(at, cotangent, touched), mine))
+    v = lax.all_gather(mine, "z")
     c = lax.all_to_all(c, plane, 0, 0, tiled=True)
     wt = dense(m)
     table = grads(at, c, wt)
-    arrived, b = bags(at, c, wt, v)
+    arrived, b = bags(at, x.reshape(1), c, wt, v)
     b = lax.all_to_all(b, plane, 0, 0, tiled=True)
     b, g = lax.optimization_barrier((b, scores(m, c, arrived)))
     g = lax.all_to_all(g, plane, 0, 0, tiled=True)

time: 151 us -> 158 us (1.046)
  starting transfers between devices: 24.8 us -> 31.9 us
    all_to_all x1, waiting for transfers between devices: 9.88 us -> 0.01 us  [on_device(): m = lax.all_to_all(m, plane, 0, 0, tiled=True)]
    ppermute x0 -> x3, waiting for transfers between devices: none -> 8.51 us  [on_device(): lax.ppermute(parts[i], 'x', [(j, (j - i) % NX) for j in range(NX)])]
    ppermute x0 -> x3, starting transfers between devices: none -> 7.05 us  [on_device(): lax.ppermute(parts[i], 'x', [(j, (j - i) % NX) for j in range(NX)])]
    all_gather x1, waiting for transfers between devices: 1.89 us -> 0.02 us  [on_device(): v = lax.all_gather(mine, 'z')]
    reduce_scatter x1, waiting for transfers between devices: 1.88 us -> 3.68 us  [on_device(): table = lax.psum_scatter(table, 'z', scatter_dimension=0, tiled=True)]
  transfers between devices with their start and end apart: 6 -> 9, of which waited for: 5 -> 6; matrix products, arithmetic and copies ran while one was open for 0% -> 1% of each run, Pallas kernels for 47% -> 46%
where the time goes in v7:
time: 158 us; the launch traced here: 157 us
  Pallas kernels  72 us (46%)
  starting transfers between devices  31.9 us (20%)
  waiting for transfers between devices  18.3 us (12%)
  blocking collectives  17.4 us (11%)
  between operations  14.1 us (9%)
  other arithmetic  2.22 us (1%)
    pallas_call x1, Pallas kernels, dense(): pl.pallas_call(dense_kernel, grid=(NZ // 2,), in_specs=[pl.BlockSpec((NS,...  22.9 us
    all_to_all x1, blocking collectives, on_device(): g = lax.all_to_all(g, plane, 0, 0, tiled=True)  17.4 us
    pallas_call x1, Pallas kernels, scores(): pl.pallas_call(scores_kernel, grid=(NS // EG,), in_specs=[pl.BlockSpec((E...  15.6 us
    pallas_call x1, Pallas kernels, bags(): pl.pallas_call(bags_kernel, grid=(NS // EG,), in_specs=[pl.BlockSpec(memo...  13.4 us
    pallas_call x1, Pallas kernels, grads(): pl.pallas_call(grads_kernel, grid_spec=spec, out_shape=jax.ShapeDtypeStru...  11.5 us
    ppermute x3, waiting for transfers between devices, on_device(): lax.ppermute(parts[i], 'x', [(j, (j - i) % NX) for j in range(NX)])  8.51 us
    all_to_all x1, starting transfers between devices, on_device(): m = lax.all_to_all(m, plane, 0, 0, tiled=True)  8.08 us
    all_to_all x1, starting transfers between devices, on_device(): b = lax.all_to_all(b, plane, 0, 0, tiled=True)  7.43 us
  transfers between devices with their start and end apart: 9, of which 6 were waited for; matrix products, arithmetic and copies ran while one was open for 1% of the time, Pallas kernels for 46%

profile of v7, /device:TPU:8, one launch (start us, length us, event | category | flops | bytes accessed | tf_op | source)
XLA Modules:
  0.0 156.9 jit_solution(13217934000989963686)
XLA Ops:
  7.2 1.0 constant_dynamic-slice_fusion
  8.2 2.8 %collective-permute-start = (bf16[256,128]{1,0:T(8,128)(2,1)S(1)}, bf16[256,128]{1,0:T(8,128)(2,1)S(1)}, u32[]{:S(2)}, u32[]{:S(2)}) collective-permute-start(bf16[256,128]{1,0:T(8,128)(2,1)S(1)} %get-tuple-element.17), channel_id=1, source_target_pairs={{0,3},{1,0},{2,1},{3,2},{4,7},{5,4},{6,5},{7,6},{8,11},{9,8},{10,9... | collective-permute-start | bytes 196616 | tf_op jit(solution)/shard_map/ppermute | solution.py:324
  11.0 1.6 %slots.1 = bf16[32,64,128]{2,1,0:T(8,128)(2,1)} custom-call(s32[1]{0:T(128)} %bitcast.at_ref, bf16[32,128]{1,0:T(8,128)(2,1)} %bitcast.27, s32[32,128]{1,0:T(8,128)} %bitcast.26), custom_call_target="tpu_custom_call" | custom-call | flops 2000000000 | bytes 1048576 | tf_op jit(solution)/shard_map/slots/pallas_call | solution.py:56
  12.6 0.3 collective-permute-done
  12.9 8.1 %all-to-all-start = ((bf16[32,64,128]{2,1,0:T(8,128)(2,1)}), bf16[32,64,128]{2,1,0:T(8,128)(2,1)S(1)}, u32[]{:S(2)}, u32[]{:S(2)}) async-start(bf16[32,64,128]{2,1,0:T(8,128)(2,1)} %slots.1), calls=%async_computation | async-start | bytes 1048576 | tf_op jit(solution)/shard_map/all_to_all | solution.py:328
  21.0 0.0 all-gather.3.cloned.1.call-start
  21.0 1.5 collective-permute-start.2
  22.6 2.7 %collective-permute-start.1 = (bf16[256,128]{1,0:T(8,128)(2,1)S(1)}, bf16[256,128]{1,0:T(8,128)(2,1)S(1)}, u32[]{:S(2)}, u32[]{:S(2)}) collective-permute-start(bf16[256,128]{1,0:T(8,128)(2,1)S(1)} %get-tuple-element.21), channel_id=1, source_target_pairs={{0,2},{1,3},{2,0},{3,1},{4,6},{5,7},{6,4},{7,5},{8,10},{9,11},{10,... | collective-permute-start | bytes 196616 | tf_op jit(solution)/shard_map/ppermute | solution.py:324
  25.2 6.7 %collective-permute-done.2 = bf16[256,128]{1,0:T(8,128)(2,1)S(1)} collective-permute-done((bf16[256,128]{1,0:T(8,128)(2,1)S(1)}, bf16[256,128]{1,0:T(8,128)(2,1)S(1)}, u32[]{:S(2)}, u32[]{:S(2)}) %collective-permute-start.2) | collective-permute-done | bytes 65568 | tf_op jit(solution)/shard_map/ppermute | solution.py:324
  31.9 1.5 collective-permute-done.1
  33.5 0.7 pad_maximum_fusion.1
  34.2 0.0 all-gather.3.cloned.1.call-update
  34.2 3.6 %blocks.1 = bf16[32,144,128]{2,1,0:T(8,128)(2,1)} custom-call(s32[1]{0:T(128)} %bitcast.at_ref, bf16[128,4096]{1,0:T(8,128)(2,1)} %cot_ref, s32[1,32,32]{2,1,0:T(8,128)} %list_ref.1), custom_call_target="tpu_custom_call" | custom-call | flops 3000000000 | bytes 1048576 | tf_op jit(solution)/shard_map/blocks/pallas_call | solution.py:94
  37.8 0.0 all-to-all-done.m_ref
  37.8 0.0 copy-start
  37.8 5.0 %all-to-all-start.1 = ((bf16[32,144,128]{2,1,0:T(8,128)(2,1)}), bf16[32,144,128]{2,1,0:T(8,128)(2,1)}, u32[]{:S(2)}, u32[]{:S(2)}) async-start(bf16[32,144,128]{2,1,0:T(8,128)(2,1)} %blocks.1), calls=%async_computation.1 | async-start | bytes 2359296 | tf_op jit(solution)/shard_map/all_to_all | solution.py:332
  42.8 0.0 reduce-scatter.2.cloned.1.call-start
  42.9 0.0 copy-done
  42.9 22.9 %dense.1.wt_ref.wt0_ref.wt1_ref = bf16[32,1024,128]{2,1,0:T(8,128)(2,1)} custom-call(bf16[32,64,128]{2,1,0:T(8,128)(2,1)} %copy-done), custom_call_target="tpu_custom_call" | custom-call | flops 24999999488 | bytes 1048576 | tf_op jit(solution)/shard_map/dense/pallas_call | solution.py:129
  65.7 0.0 all-to-all-done.1.t_ref.c_ref
  65.7 11.5 %grads.1 = f32[8,4,256,128]{3,2,1,0:T(8,128)} custom-call(s32[1]{0:T(128)} %bitcast.at_ref, bf16[32,144,128]{2,1,0:T(8,128)(2,1)} %all-to-all-done.1.t_ref.c_ref, bf16[32,144,128]{2,1,0:T(8,128)(2,1)} %all-to-all-done.1.t_ref.c_ref, bf16[32,1024,128]{2,1,0:T(8,128)(2,1)} %dense.1.wt_ref.wt0_ref.wt1_ref, bf16[32,1024,128]{2,1,0:T(8,128)(2,1)} %dense.1.wt_ref.wt0_ref.wt1_ref), custom_call_target="tpu_custom_call" | custom-call | flops 12000000000 | bytes 1048576 | tf_op jit(solution)/shard_map/grads/pallas_call | solution.py:189
  77.2 0.0 reduce-scatter.2.cloned.1.call-update
  77.3 0.0 all-gather.3.cloned.1.call-done
  77.3 13.4 %bags.1 = (bf16[32,1024,128]{2,1,0:T(8,128)(2,1)}, bf16[32,128,128]{2,1,0:T(8,128)(2,1)}) custom-call(s32[1]{0:T(128)} %bitcast.at_ref, s32[1]{0:T(128)} %bitcast.1.x_ref, bf16[32,144,128]{2,1,0:T(8,128)(2,1)} %all-to-all-done.1.t_ref.c_ref, bf16[32,1024,128]{2,1,0:T(8,128)(2,1)} %dense.1.wt_ref.wt0_ref.wt1_ref, bf16[8,4,256,128]{3,2,1,0:T(8,128)(2,1)} %bitcast.25), custom_call_target="tpu_custom_call" | custom-call | flops 17999998976 | bytes 1048576 | tf_op jit(solution)/shard_map/bags/pallas_call | solution.py:228
  90.7 7.4 %all-to-all-start.2 = ((bf16[32,128,128]{2,1,0:T(8,128)(2,1)}), bf16[32,128,128]{2,1,0:T(8,128)(2,1)}, u32[]{:S(2)}, u32[]{:S(2)}) async-start(bf16[32,128,128]{2,1,0:T(8,128)(2,1)} %get-tuple-element.25), calls=%async_computation.2 | async-start | bytes 2097152 | tf_op jit(solution)/shard_map/all_to_all | solution.py:336
  98.1 15.6 %scores.1 = f32[32,32,128]{2,1,0:T(8,128)} custom-call(bf16[32,64,128]{2,1,0:T(8,128)(2,1)} %copy-done, bf16[32,144,128]{2,1,0:T(8,128)(2,1)} %all-to-all-done.1.t_ref.c_ref, bf16[32,1024,128]{2,1,0:T(8,128)(2,1)} %get-tuple-element.26.arrived_ref), custom_call_target="tpu_custom_call" | custom-call | flops 17999998976 | bytes 1048576 | tf_op jit(solution)/shard_map/scores/pallas_call | solution.py:278
  113.7 0.6 all-to-all-done.2.b_ref
  114.3 17.4 %all_to_all.25 = f32[32,32,128]{2,1,0:T(8,128)S(1)} all-to-all(f32[32,32,128]{2,1,0:T(8,128)} %scores.1), channel_id=1, replica_groups=mesh['dp'=8,'z'=8,'x'=4] {'dp','x'}, dimensions={0} | all-to-all | bytes 1048576 | tf_op jit(solution)/shard_map/all_to_all | solution.py:338
  131.7 3.7 %reduce-scatter.2.cloned.1.call-done = f32[1,4,256,128]{3,2,1,0:T(8,128)} async-done(((f32[8,4,256,128]{3,2,1,0:T(8,128)}), f32[1,4,256,128]{3,2,1,0:T(8,128)}) %reduce-scatter.2.cloned.1.call-update) | async-done | bytes 524304 | tf_op jit(solution)/shard_map/reduce_scatter | solution.py:339
  135.4 4.2 %all-to-all-start.4 = ((f32[4,256,128]{2,1,0:T(8,128)}), f32[4,256,128]{2,1,0:T(8,128)S(1)}, u32[]{:S(2)}, u32[]{:S(2)}) async-start(f32[4,256,128]{2,1,0:T(8,128)} %bitcast.19), calls=%async_computation.5 | async-start | bytes 1048576 | tf_op jit(solution)/shard_map/all_to_all | solution.py:340
  139.7 3.5 %rows.1 = bf16[128,4096]{1,0:T(8,128)(2,1)} custom-call(bf16[32,128,128]{2,1,0:T(8,128)(2,1)} %all-to-all-done.2.b_ref), custom_call_target="tpu_custom_call" | custom-call | flops 2000000000 | bytes 1048576 | tf_op jit(solution)/shard_map/rows/pallas_call | solution.py:302
  143.1 0.6 reduce_sum.9
  143.8 5.4 %all-to-all-done.4 = f32[4,256,128]{2,1,0:T(8,128)S(1)} async-done(((f32[4,256,128]{2,1,0:T(8,128)}), f32[4,256,128]{2,1,0:T(8,128)S(1)}, u32[]{:S(2)}, u32[]{:S(2)}) %all-to-all-start.4) | async-done | bytes 524320 | tf_op jit(solution)/shard_map/all_to_all | solution.py:340
  149.3 0.8 pad_maximum_fusion
  (1 shorter events, 0.0 us)
Async XLA Ops:
  8.2 4.7 %collective-permute-start = (bf16[256,128]{1,0:T(8,128)(2,1)S(1)}, bf16[256,128]{1,0:T(8,128)(2,1)S(1)}, u32[]{:S(2)}, u32[]{:S(2)}) collective-permute-start(bf16[256,128]{1,0:T(8,128)(2,1)S(1)} %get-tuple-element.17), channel_id=1, source_target_pairs={{0,3},{1,0},{2,1},{3,2},{4,7},{5,4},{6,5},{7,6},{8,11},{9,8},{10,9... | collective-permute-start | bytes 196616 | tf_op jit(solution)/shard_map/ppermute | solution.py:324
  12.9 24.9 %all-to-all-start = ((bf16[32,64,128]{2,1,0:T(8,128)(2,1)}), bf16[32,64,128]{2,1,0:T(8,128)(2,1)S(1)}, u32[]{:S(2)}, u32[]{:S(2)}) async-start(bf16[32,64,128]{2,1,0:T(8,128)(2,1)} %slots.1), calls=%async_computation | async-start | bytes 1048576 | tf_op jit(solution)/shard_map/all_to_all | solution.py:328
  21.0 56.3 %all-gather.3.cloned.1.call-start = ((), (), s32[]{:S(2)}) async-start(), calls=%async_computation.7 | async-start | bytes 2359296 | tf_op jit(solution)/shard_map/all_gather | solution.py:331
  21.0 10.9 %collective-permute-start.2 = (bf16[256,128]{1,0:T(8,128)(2,1)S(1)}, bf16[256,128]{1,0:T(8,128)(2,1)S(1)}, u32[]{:S(2)}, u32[]{:S(2)}) collective-permute-start(bf16[256,128]{1,0:T(8,128)(2,1)S(1)} %get-tuple-element.22), channel_id=1, source_target_pairs={{0,1},{1,2},{2,3},{3,0},{4,5},{5,6},{6,7},{7,4},{8,9},{9,10},{10,1... | collective-permute-start | bytes 196616 | tf_op jit(solution)/shard_map/ppermute | solution.py:324
  22.6 10.9 %collective-permute-start.1 = (bf16[256,128]{1,0:T(8,128)(2,1)S(1)}, bf16[256,128]{1,0:T(8,128)(2,1)S(1)}, u32[]{:S(2)}, u32[]{:S(2)}) collective-permute-start(bf16[256,128]{1,0:T(8,128)(2,1)S(1)} %get-tuple-element.21), channel_id=1, source_target_pairs={{0,2},{1,3},{2,0},{3,1},{4,6},{5,7},{6,4},{7,5},{8,10},{9,11},{10,... | collective-permute-start | bytes 196616 | tf_op jit(solution)/shard_map/ppermute | solution.py:324
  37.8 5.1 %copy-start = (bf16[32,64,128]{2,1,0:T(8,128)(2,1)}, bf16[32,64,128]{2,1,0:T(8,128)(2,1)S(1)}, u32[]{:S(2)}) copy-start(bf16[32,64,128]{2,1,0:T(8,128)(2,1)S(1)} %all-to-all-done.m_ref) | copy-start | bytes 1572868
  37.8 27.9 %all-to-all-start.1 = ((bf16[32,144,128]{2,1,0:T(8,128)(2,1)}), bf16[32,144,128]{2,1,0:T(8,128)(2,1)}, u32[]{:S(2)}, u32[]{:S(2)}) async-start(bf16[32,144,128]{2,1,0:T(8,128)(2,1)} %blocks.1), calls=%async_computation.1 | async-start | bytes 2359296 | tf_op jit(solution)/shard_map/all_to_all | solution.py:332
  42.8 92.6 %reduce-scatter.2.cloned.1.call-start = ((), (), s32[]{:S(2)}) async-start(), calls=%async_computation.6 | async-start | bytes 4718592 | tf_op jit(solution)/shard_map/reduce_scatter | solution.py:339
  90.7 23.7 %all-to-all-start.2 = ((bf16[32,128,128]{2,1,0:T(8,128)(2,1)}), bf16[32,128,128]{2,1,0:T(8,128)(2,1)}, u32[]{:S(2)}, u32[]{:S(2)}) async-start(bf16[32,128,128]{2,1,0:T(8,128)(2,1)} %get-tuple-element.25), calls=%async_computation.2 | async-start | bytes 2097152 | tf_op jit(solution)/shard_map/all_to_all | solution.py:336
  135.4 13.8 %all-to-all-start.4 = ((f32[4,256,128]{2,1,0:T(8,128)}), f32[4,256,128]{2,1,0:T(8,128)S(1)}, u32[]{:S(2)}, u32[]{:S(2)}) async-start(f32[4,256,128]{2,1,0:T(8,128)} %bitcast.19), calls=%async_computation.5 | async-start | bytes 1048576 | tf_op jit(solution)/shard_map/all_to_all | solution.py:340
Sparse Core Ops, SparseCore 0:
  34.4 41.6 all-gather.2
  78.6 56.7 reduce-scatter.1

commit v8 on v6

--- a/solution.py
+++ b/solution.py
@@ -30,6 +30,10 @@
     return hi, (v - hi.astype(F32)).astype(BF)
 
 
+def columns_of(i):
+    return ((i % ND) * NX + i // ND) * CB
+
+
 def slots_kernel(at_ref, own_ref, w_ref, pos_ref, v_ref, out_ref):
     z = at_ref[0]
     pos = pos_ref[...]
@@ -39,7 +43,7 @@
     for i in range(NS):
         out_ref[i, 0:M_C, :] = w
         out_ref[i, M_C:M_V, :] = code
-        out_ref[i, M_V:M_ALL, :] = v_ref[:, i * CB:(i + 1) * CB]
+        out_ref[i, M_V:M_ALL, :] = v_ref[:, columns_of(i):columns_of(i) + CB]
 
 
 def cost(us):
@@ -79,7 +83,8 @@
         rows.append(four[0] + four[1] + four[2] + four[3])
     lists = jnp.concatenate(rows + rows, axis=0).astype(F32).astype(BF)
     for i in range(out_ref.shape[0]):
-        out_ref[i, 0:TOK, :] = cot_ref[:, i * CB:(i + 1) * CB]
+        at = pl.multiple_of((i * NX + pl.program_id(0)) * CB, CB)
+        out_ref[i, 0:TOK, :] = cot_ref[:, pl.ds(at, CB)]
         out_ref[i, TOK:C_ALL, :] = lists
 
 
@@ -89,7 +94,7 @@
         num_scalar_prefetch=1,
         grid=(NS // per,),
         in_specs=[
-            pl.BlockSpec((TOK, per * CB), lambda g, at: (0, g)),
+            pl.BlockSpec((TOK, NS * CB), lambda g, at: (0, 0)),
             pl.BlockSpec((1, NX * NZ, CAP), lambda g, at: (0, 0, 0)),
         ],
         out_specs=pl.BlockSpec((per, C_ALL, CB), lambda g, at: (g, 0, 0)),
@@ -216,7 +221,7 @@
                 hots[x, e * CAP:(e + 1) * CAP, :] = hot[x * CAP:(x + 1) * CAP]
         for x in range(NX):
             rows = jnp.concatenate(
-                [v_ref[(z + h) & (NZ - 1), d * NX + x] for d in range(ND)], axis=0
+                [v_ref[(z + h) & (NZ - 1), x * ND + d] for d in range(ND)], axis=0
             )
             got = jnp.dot(hots[x], rows, preferred_element_type=F32).astype(BF)
             at = h * GRP + x * CAP
@@ -298,18 +303,16 @@
 
 def gather_kernel(b_ref, out_ref):
     for i in range(b_ref.shape[0]):
-        out_ref[:, i * CB:(i + 1) * CB] = b_ref[i]
+        out_ref[:, columns_of(i):columns_of(i) + CB] = b_ref[i]
 
 
 def gather_blocks(b):
-    per = 8
-    rows = b.shape[1]
+    vm = pl.BlockSpec(memory_space=pltpu.VMEM)
     return pl.pallas_call(
         gather_kernel,
-        grid=(b.shape[0] // per,),
-        in_specs=[pl.BlockSpec((per, rows, CB), lambda g: (g, 0, 0))],
-        out_specs=pl.BlockSpec((rows, per * CB), lambda g: (0, g)),
-        out_shape=jax.ShapeDtypeStruct((rows, b.shape[0] * CB), b.dtype),
+        in_specs=[vm],
+        out_specs=vm,
+        out_shape=jax.ShapeDtypeStruct((TOK, NS * CB), b.dtype),
         cost_estimate=cost(2),
         name="rows",
     )(b)
@@ -318,7 +321,7 @@
 def on_device(slot_weight, slot_pos, touched, values, cotangent):
     at = lax.axis_index("z").astype(jnp.int32).reshape(1)
     own = lax.axis_index("dp").astype(jnp.int32).reshape(1)
-    plane = ("dp", "x")
+    plane = ("x", "dp")
     m = slots(at, own, slot_weight.T, slot_pos.T, values)
     m = lax.all_to_all(m, plane, 0, 0, tiled=True)
     m, c = lax.optimization_barrier((m, blocks(at, cotangent, touched)))

time: 151 us -> 151 us (level)
  Pallas kernels: 72.4 us -> 70.8 us
  transfers between devices with their start and end apart: 6 -> 6, of which waited for: 5 -> 4; matrix products, arithmetic and copies ran while one was open for 0% -> 0% of each run, Pallas kernels for 47% -> 46%
where the time goes in v8:
time: 151 us; the launch traced here: 150 us
  Pallas kernels  70.8 us (47%)
  starting transfers between devices  24.6 us (16%)
  waiting for transfers between devices  20.8 us (14%)
  blocking collectives  17.5 us (12%)
  between operations  14.1 us (9%)
    pallas_call x1, Pallas kernels, dense(): pl.pallas_call(dense_kernel, grid=(NZ // 2,), in_specs=[pl.BlockSpec((NS,...  22.8 us
    all_to_all x1, blocking collectives, on_device(): g = lax.all_to_all(g, plane, 0, 0, tiled=True)  17.5 us
    pallas_call x1, Pallas kernels, scores(): pl.pallas_call(scores_kernel, grid=(NS // EG,), in_specs=[pl.BlockSpec((E...  15.6 us
    pallas_call x1, Pallas kernels, bags(): pl.pallas_call(bags_kernel, grid=(NS // EG,), in_specs=[pl.BlockSpec(memo...  13.4 us
    pallas_call x1, Pallas kernels, grads(): pl.pallas_call(grads_kernel, grid_spec=spec, out_shape=jax.ShapeDtypeStru...  11.5 us
    all_to_all x1, waiting for transfers between devices, on_device(): m = lax.all_to_all(m, plane, 0, 0, tiled=True)  9.83 us
    all_to_all x1, starting transfers between devices, on_device(): m = lax.all_to_all(m, plane, 0, 0, tiled=True)  7.53 us
    all_to_all x1, starting transfers between devices, on_device(): b = lax.all_to_all(b, plane, 0, 0, tiled=True)  7.25 us
  transfers between devices with their start and end apart: 6, of which 4 were waited for; matrix products, arithmetic and copies ran while one was open for 0% of the time, Pallas kernels for 46%

profile of v8, /device:TPU:8, one launch (start us, length us, event | category | flops | bytes accessed | tf_op | source)
XLA Modules:
  0.0 150.0 jit_solution(856008498033862450)
XLA Ops:
  7.2 1.9 %slots.1 = bf16[32,96,128]{2,1,0:T(8,128)(2,1)} custom-call(s32[1]{0:T(128)} %bitcast.at_ref, s32[1]{0:T(128)} %bitcast.1.own_ref, bf16[32,128]{1,0:T(8,128)(2,1)} %bitcast.19, s32[32,128]{1,0:T(8,128)} %bitcast.18, bf16[256,4096]{1,0:T(8,128)(2,1)} %v_ref.1), custom_call_target="tpu_custom_call" | custom-call | flops 2000000000 | bytes 1048576 | tf_op jit(solution)/shard_map/slots/pallas_call | solution.py:64
  9.1 7.5 %all-to-all-start = ((bf16[32,96,128]{2,1,0:T(8,128)(2,1)}), bf16[32,96,128]{2,1,0:T(8,128)(2,1)S(1)}, u32[]{:S(2)}, u32[]{:S(2)}) async-start(bf16[32,96,128]{2,1,0:T(8,128)(2,1)} %slots.1), calls=%async_computation | async-start | bytes 1572864 | tf_op jit(solution)/shard_map/all_to_all | solution.py:326
  16.7 0.0 all-gather.3.cloned.1.call-start
  16.7 3.0 %blocks.1 = bf16[32,144,128]{2,1,0:T(8,128)(2,1)} custom-call(s32[1]{0:T(128)} %bitcast.at_ref, bf16[128,4096]{1,0:T(8,128)(2,1)} %cot_ref.1, s32[1,32,32]{2,1,0:T(8,128)} %list_ref.1), custom_call_target="tpu_custom_call" | custom-call | flops 3000000000 | bytes 1048576 | tf_op jit(solution)/shard_map/blocks/pallas_call | solution.py:103
  19.7 9.8 %all-to-all-done.m_ref = bf16[32,96,128]{2,1,0:T(8,128)(2,1)S(1)} async-done(((bf16[32,96,128]{2,1,0:T(8,128)(2,1)}), bf16[32,96,128]{2,1,0:T(8,128)(2,1)S(1)}, u32[]{:S(2)}, u32[]{:S(2)}) %all-to-all-start) | async-done | bytes 786464 | tf_op jit(solution)/shard_map/all_to_all | solution.py:326
  29.6 0.0 copy-start
  29.6 0.8 slice.15
  30.3 0.0 all-gather.3.cloned.1.call-update
  30.4 5.4 %all-to-all-start.1 = ((bf16[32,144,128]{2,1,0:T(8,128)(2,1)}), bf16[32,144,128]{2,1,0:T(8,128)(2,1)}, u32[]{:S(2)}, u32[]{:S(2)}) async-start(bf16[32,144,128]{2,1,0:T(8,128)(2,1)} %blocks.1), calls=%async_computation.1 | async-start | bytes 2359296 | tf_op jit(solution)/shard_map/all_to_all | solution.py:329
  35.8 0.0 reduce-scatter.2.cloned.1.call-start
  35.9 0.0 copy-done
  35.9 22.8 %dense.1.wt_ref.wt0_ref.wt1_ref = bf16[32,1024,128]{2,1,0:T(8,128)(2,1)} custom-call(bf16[32,96,128]{2,1,0:T(8,128)(2,1)} %copy-done), custom_call_target="tpu_custom_call" | custom-call | flops 24999999488 | bytes 1048576 | tf_op jit(solution)/shard_map/dense/pallas_call | solution.py:138
  58.7 0.0 all-to-all-done.1.t_ref.c_ref
  58.7 11.5 %grads.1 = f32[8,4,256,128]{3,2,1,0:T(8,128)} custom-call(s32[1]{0:T(128)} %bitcast.at_ref, bf16[32,144,128]{2,1,0:T(8,128)(2,1)} %all-to-all-done.1.t_ref.c_ref, bf16[32,144,128]{2,1,0:T(8,128)(2,1)} %all-to-all-done.1.t_ref.c_ref, bf16[32,1024,128]{2,1,0:T(8,128)(2,1)} %dense.1.wt_ref.wt0_ref.wt1_ref, bf16[32,1024,128]{2,1,0:T(8,128)(2,1)} %dense.1.wt_ref.wt0_ref.wt1_ref), custom_call_target="tpu_custom_call" | custom-call | flops 12000000000 | bytes 1048576 | tf_op jit(solution)/shard_map/grads/pallas_call | solution.py:198
  70.2 0.0 reduce-scatter.2.cloned.1.call-update
  70.3 2.1 %all-gather.3.cloned.1.call-done = bf16[256,32,128]{2,1,0:T(8,128)(2,1)} async-done(((bf16[32,32,128]{2,1,0:T(8,128)(2,1)}), bf16[256,32,128]{2,1,0:T(8,128)(2,1)}) %all-gather.3.cloned.1.call-update) | async-done | bytes 2097168 | tf_op jit(solution)/shard_map/all_gather | solution.py:328
  72.3 13.4 %bags.1 = (bf16[32,1024,128]{2,1,0:T(8,128)(2,1)}, bf16[32,128,128]{2,1,0:T(8,128)(2,1)}) custom-call(s32[1]{0:T(128)} %bitcast.at_ref, bf16[32,144,128]{2,1,0:T(8,128)(2,1)} %all-to-all-done.1.t_ref.c_ref, bf16[32,1024,128]{2,1,0:T(8,128)(2,1)} %dense.1.wt_ref.wt0_ref.wt1_ref, bf16[8,32,32,128]{3,2,1,0:T(8,128)(2,1)} %bitcast.17), custom_call_target="tpu_custom_call" | custom-call | flops 17999998976 | bytes 1048576 | tf_op jit(solution)/shard_map/bags/pallas_call | solution.py:239
  85.7 7.2 %all-to-all-start.2 = ((bf16[32,128,128]{2,1,0:T(8,128)(2,1)}), bf16[32,128,128]{2,1,0:T(8,128)(2,1)}, u32[]{:S(2)}, u32[]{:S(2)}) async-start(bf16[32,128,128]{2,1,0:T(8,128)(2,1)} %get-tuple-element.11), calls=%async_computation.2 | async-start | bytes 2097152 | tf_op jit(solution)/shard_map/all_to_all | solution.py:333
  93.0 15.6 %scores.1 = f32[32,32,128]{2,1,0:T(8,128)} custom-call(bf16[32,96,128]{2,1,0:T(8,128)(2,1)} %copy-done, bf16[32,144,128]{2,1,0:T(8,128)(2,1)} %all-to-all-done.1.t_ref.c_ref, bf16[32,1024,128]{2,1,0:T(8,128)(2,1)} %get-tuple-element.12.arrived_ref), custom_call_target="tpu_custom_call" | custom-call | flops 17999998976 | bytes 1048576 | tf_op jit(solution)/shard_map/scores/pallas_call | solution.py:288
  108.6 0.0 all-to-all-done.2.b_ref
  108.6 17.5 %all_to_all.25 = f32[32,32,128]{2,1,0:T(8,128)S(1)} all-to-all(f32[32,32,128]{2,1,0:T(8,128)} %scores.1), channel_id=1, replica_groups=mesh['dp'=8,'z'=8,'x'=4] {'x','dp'}, dimensions={0} | all-to-all | bytes 1048576 | tf_op jit(solution)/shard_map/all_to_all | solution.py:335
  126.1 2.4 %reduce-scatter.2.cloned.1.call-done = f32[1,4,256,128]{3,2,1,0:T(8,128)} async-done(((f32[8,4,256,128]{3,2,1,0:T(8,128)}), f32[1,4,256,128]{3,2,1,0:T(8,128)}) %reduce-scatter.2.cloned.1.call-update) | async-done | bytes 524304 | tf_op jit(solution)/shard_map/reduce_scatter | solution.py:336
  128.5 4.3 %all-to-all-start.4 = ((f32[4,256,128]{2,1,0:T(8,128)}), f32[4,256,128]{2,1,0:T(8,128)S(1)}, u32[]{:S(2)}, u32[]{:S(2)}) async-start(f32[4,256,128]{2,1,0:T(8,128)} %bitcast.15), calls=%async_computation.5 | async-start | bytes 1048576 | tf_op jit(solution)/shard_map/all_to_all | solution.py:337
  132.8 2.5 %rows.1 = bf16[128,4096]{1,0:T(8,128)(2,1)} custom-call(bf16[32,128,128]{2,1,0:T(8,128)(2,1)} %all-to-all-done.2.b_ref), custom_call_target="tpu_custom_call" | custom-call | flops 2000000000 | bytes 1048576 | tf_op jit(solution)/shard_map/rows/pallas_call | solution.py:311
  135.2 0.6 reduce_sum.9
  135.9 6.4 %all-to-all-done.4 = f32[4,256,128]{2,1,0:T(8,128)S(1)} async-done(((f32[4,256,128]{2,1,0:T(8,128)}), f32[4,256,128]{2,1,0:T(8,128)S(1)}, u32[]{:S(2)}, u32[]{:S(2)}) %all-to-all-start.4) | async-done | bytes 524320 | tf_op jit(solution)/shard_map/all_to_all | solution.py:337
  142.3 0.8 pad_maximum_fusion
  (1 shorter events, 0.0 us)
Async XLA Ops:
  9.1 20.5 %all-to-all-start = ((bf16[32,96,128]{2,1,0:T(8,128)(2,1)}), bf16[32,96,128]{2,1,0:T(8,128)(2,1)S(1)}, u32[]{:S(2)}, u32[]{:S(2)}) async-start(bf16[32,96,128]{2,1,0:T(8,128)(2,1)} %slots.1), calls=%async_computation | async-start | bytes 1572864 | tf_op jit(solution)/shard_map/all_to_all | solution.py:326
  16.7 55.7 %all-gather.3.cloned.1.call-start = ((), (), s32[]{:S(2)}) async-start(), calls=%async_computation.7 | async-start | bytes 2359296 | tf_op jit(solution)/shard_map/all_gather | solution.py:328
  29.6 6.3 %copy-start = (bf16[32,96,128]{2,1,0:T(8,128)(2,1)}, bf16[32,96,128]{2,1,0:T(8,128)(2,1)S(1)}, u32[]{:S(2)}) copy-start(bf16[32,96,128]{2,1,0:T(8,128)(2,1)S(1)} %all-to-all-done.m_ref) | copy-start | bytes 2359300
  30.4 28.4 %all-to-all-start.1 = ((bf16[32,144,128]{2,1,0:T(8,128)(2,1)}), bf16[32,144,128]{2,1,0:T(8,128)(2,1)}, u32[]{:S(2)}, u32[]{:S(2)}) async-start(bf16[32,144,128]{2,1,0:T(8,128)(2,1)} %blocks.1), calls=%async_computation.1 | async-start | bytes 2359296 | tf_op jit(solution)/shard_map/all_to_all | solution.py:329
  35.8 92.7 %reduce-scatter.2.cloned.1.call-start = ((), (), s32[]{:S(2)}) async-start(), calls=%async_computation.6 | async-start | bytes 4718592 | tf_op jit(solution)/shard_map/reduce_scatter | solution.py:336
  85.7 22.9 %all-to-all-start.2 = ((bf16[32,128,128]{2,1,0:T(8,128)(2,1)}), bf16[32,128,128]{2,1,0:T(8,128)(2,1)}, u32[]{:S(2)}, u32[]{:S(2)}) async-start(bf16[32,128,128]{2,1,0:T(8,128)(2,1)} %get-tuple-element.11), calls=%async_computation.2 | async-start | bytes 2097152 | tf_op jit(solution)/shard_map/all_to_all | solution.py:333
  128.5 13.8 %all-to-all-start.4 = ((f32[4,256,128]{2,1,0:T(8,128)}), f32[4,256,128]{2,1,0:T(8,128)S(1)}, u32[]{:S(2)}, u32[]{:S(2)}) async-start(f32[4,256,128]{2,1,0:T(8,128)} %bitcast.15), calls=%async_computation.5 | async-start | bytes 1048576 | tf_op jit(solution)/shard_map/all_to_all | solution.py:337
Sparse Core Ops, SparseCore 0:
  30.5 41.8 all-gather.2
  74.9 53.5 reduce-scatter.1
